TPU v7x, 32 devices: a whole 2x2x4 slice. The times are simulated.
32 devices in a mesh: row: 8 (over z, y), col: 4 (over x, core).
Axes of the slice: x: 2, y: 2, z: 4, core: 2. Of those that a mesh axis runs over, the one named last changes fastest.
Arguments:
- emb_source: bfloat16 [65536, 64], P('row'), may hold values from -0.625 to 0.625
- emb_target: bfloat16 [65536, 64], P(('col', 'row')), may hold values from -0.625 to 0.625
- source_mass: float32 [65536], P('row'), may hold values from 0.5 to 4
- target_mass: float32 [65536], P('col'), may hold values from 0.5 to 4
- start_potential: float32 [65536], P('col'), may hold values from -6 to 6
- support: int32 [512, 4, 4], P('row', 'col'), may hold values from 0 to 127, as said below
- count: int32 [512, 4], P('row', 'col'), may hold values from 1 to 4, as said below
Outputs:
- source_potential: float32 [65536], P('row')
- target_potential: float32 [65536], P('col')
Inputs may be any that keep to these rules, and one draw needn't show every extreme that they name: support[r, c, k] names target block c * 128 + support[r, c, k]; the first count[r, c] entries of each list are distinct, and every target block is named by a live entry of some list. count[r, c] is the number of live entries of list (r, c).
All inputs are finite; a program needn't handle non-finite values.
Results may differ from a plain program's by a relative error of at most 0.0003.
Values may be sent and summed in bfloat16 or wider, within the bound.
No kernel may reach another device: no remote copies, remote signals or barrier semaphores. Data moves between devices by JAX's collectives and lax.ppermute only.
A program may use at most 64 MiB of HBM per device.

v0:
```python
import jax
import jax.numpy as jnp
from jax import lax
from jax.sharding import PartitionSpec as P

D = 64
BLOCK = 128


entropy = 0.05
sentinel = -1e30
per_turn = 4


def combined_all(value, axis, join):
    pieces = jax.tree.map(lambda part: lax.all_gather(part, axis), value)
    head = jax.tree.map(lambda part: part[0], pieces)
    tail = jax.tree.map(lambda part: part[1:], pieces)
    total, _ = lax.scan(lambda total, slab: (join(total, slab), None), head, tail)
    return total


def join_parts(first, second):
    joint_peak = jnp.maximum(first[0], second[0])
    return (
        joint_peak,
        first[1] * jnp.exp(first[0] - joint_peak) + second[1] * jnp.exp(second[0] - joint_peak),
    )


def shards(emb_source, emb_target, source_mass, target_mass, start_potential, support, count):
    gathered = lax.all_gather(emb_target, "row", axis=0, tiled=True)
    target_count = gathered.shape[0] // BLOCK
    target_blocks = gathered.reshape(target_count, BLOCK, D)
    target_sq = jnp.einsum(
        "tjd,tjd->tj", target_blocks, target_blocks, preferred_element_type=jnp.float32
    )
    source_rows = support.shape[0]
    slot_count = support.shape[2]
    turns = source_rows // per_turn
    slot_ids = support.reshape(turns, per_turn, slot_count)
    alive = (jnp.arange(slot_count, dtype=jnp.int32)[None, :] < count).reshape(
        turns, per_turn, slot_count
    )
    source_blocks = emb_source.reshape(turns, per_turn, BLOCK, D)
    source_sq = jnp.einsum(
        "tsid,tsid->tsi", source_blocks, source_blocks, preferred_element_type=jnp.float32
    )

    def costs_of(src_part, sq_part, ids_part):
        tiles = target_blocks[ids_part]
        cross_term = jnp.einsum(
            "sid,skjd->skij", src_part, tiles, preferred_element_type=jnp.float32
        )
        return 0.5 * (sq_part[:, None, :, None] + target_sq[ids_part][:, :, None, :]) - cross_term

    def source_update(target_pot):
        pot_blocks = target_pot.reshape(target_count, BLOCK)

        def source_one_turn(items):
            src_part, sq_part, ids_part, live_part = items
            scores = (
                pot_blocks[ids_part][:, :, None, :] - costs_of(src_part, sq_part, ids_part)
            ) / entropy
            scores = jnp.where(live_part[:, :, None, None], scores, -jnp.inf)
            row_peak = jnp.max(scores, axis=(1, 3))
            row_total = jnp.sum(jnp.exp(scores - row_peak[:, None, :, None]), axis=(1, 3))
            return (row_peak, row_total)

        row_peak, row_total = lax.map(source_one_turn, (source_blocks, source_sq, slot_ids, alive))
        row_peak = row_peak.reshape(-1)
        row_total = row_total.reshape(-1)
        peak_all, total_all = combined_all((row_peak, row_total), "col", join_parts)
        return entropy * jnp.log(source_mass) - entropy * (peak_all + jnp.log(total_all))

    def target_update(source_pot):
        pot_rows = source_pot.reshape(turns, per_turn, BLOCK)

        def target_one_turn(items):
            src_part, sq_part, ids_part, live_part, pot_part = items
            scores = (pot_part[:, None, :, None] - costs_of(src_part, sq_part, ids_part)) / entropy
            col_peak = jnp.max(scores, axis=2)
            col_total = jnp.sum(jnp.exp(scores - col_peak[:, :, None, :]), axis=2)
            col_peak = jnp.where(live_part[:, :, None], col_peak, sentinel)
            col_total = jnp.where(live_part[:, :, None], col_total, 0.0)
            return (col_peak, col_total)

        col_peak, col_total = lax.map(
            target_one_turn, (source_blocks, source_sq, slot_ids, alive, pot_rows)
        )
        flat_ids = slot_ids.reshape(-1)
        col_peak = col_peak.reshape(-1, BLOCK)
        col_total = col_total.reshape(-1, BLOCK)
        block_peak = (
            jnp.full((target_count, BLOCK), sentinel, jnp.float32).at[flat_ids].max(col_peak)
        )
        scaled = col_total * jnp.exp(col_peak - block_peak[flat_ids])
        member = (flat_ids[:, None] == jnp.arange(target_count, dtype=jnp.int32)[None, :]).astype(
            jnp.float32
        )
        block_total = jnp.einsum("tb,tj->bj", member, scaled, precision=lax.Precision.HIGHEST)
        cell_peak = block_peak.reshape(-1)
        cell_total = block_total.reshape(-1)
        peak_all = lax.pmax(cell_peak.astype(jnp.bfloat16), "row").astype(cell_peak.dtype)
        total_all = lax.psum(
            (cell_total * jnp.exp(cell_peak - peak_all)).astype(jnp.bfloat16), "row"
        ).astype(jnp.float32)
        return entropy * jnp.log(target_mass) - entropy * (peak_all + jnp.log(total_all))

    first_f = source_update(start_potential)
    first_g = target_update(first_f)
    second_f = source_update(first_g)
    second_g = target_update(second_f)
    return (second_f, second_g)


def solution(mesh):
    in_specs = (
        P("row", None),
        P(("col", "row"), None),
        P("row"),
        P("col"),
        P("col"),
        P("row", "col", None),
        P("row", "col"),
    )
    out_specs = (P("row"), P("col"))
    return jax.shard_map(shards, mesh=mesh, in_specs=in_specs, out_specs=out_specs, check_vma=False)
```

profile of v0, /device:TPU:0, one launch (start us, length us, event | category | flops | bytes accessed | tf_op | source)
XLA Modules:
  0.0 548.0 jit_solution(14923050492095380380)
XLA Ops:
  14.1 48.1 %all-gather.6.cloned.1.call-done = bf16[16384,64]{0,1:T(8,128)(2,1)} async-done(((bf16[2048,64]{0,1:T(8,128)(2,1)}), bf16[16384,64]{0,1:T(8,128)(2,1)}) %all-gather.6.cloned.1.call-update) | async-done | bytes 2097168 | tf_op jit(solution)/shard_map/all_gather | solution.py:32
  62.2 4.8 copy.55
  67.0 4.4 fusion.30
  71.4 85.1 %while.72 = (s32[]{:T(128)}, f32[16,4,128]{2,1,0:T(4,128)S(1)}, f32[16,4,128]{2,1,0:T(4,128)S(1)}, pred[16,4,4]{2,1,0:T(4,128)(4,1)S(1)}, s32[16,4,4]{2,1,0:T(4,...) while((s32[]{:T(128)}, f32[16,4,128]{2,1,0:T(4,128)S(1)}, ...), condition=%wide.region_3.4_spmd, body=%wide.region_0.3_spmd.sunk | while | flops 35913776 | bytes 3286177 | solution.py:70
  71.6 2.8 gather_fusion
  76.9 2.8 gather_fusion
  82.2 2.8 gather_fusion
  103.5 2.8 gather_fusion
  108.8 2.8 gather_fusion
  124.7 2.8 gather_fusion
  130.1 2.8 gather_fusion
  151.3 2.8 gather_fusion
  156.5 5.4 all-gather
  162.0 5.4 all-gather.1
  168.1 68.3 %while.74 = (s32[]{:T(128)}, f32[16,4,4,128]{3,2,1,0:T(4,128)S(1)}, f32[16,4,4,128]{3,2,1,0:T(4,128)S(1)}, pred[16,4,4]{2,1,0:T(4,128)(4,1)S(1)}, f32[16,4,128]{...) while((s32[]{:T(128)}, f32[16,4,4,128]{3,2,1,0:T(4,128)S(1)}, ...), condition=%wide.region_9.10_spmd, body=%wide.region_6.9_spmd.sunk | while | flops 35652656 | bytes 3310689 | solution.py:88
  168.2 2.8 gather_fusion.3
  202.4 2.8 gather_fusion.3
  215.2 2.8 gather_fusion.3
  228.0 2.8 gather_fusion.3
  238.6 34.7 %pmax.14 = bf16[16384]{0:T(1024)(128)(2,1)S(1)} all-reduce(bf16[16384]{0:T(1024)(128)(2,1)S(1)} %bitcast_convert_fusion.1), channel_id=1, replica_groups=mesh['row'=8,'col'=4] {'row'}, use_global_device_ids=true, to_apply=%region_11.12 | all-reduce | flops 16384 | bytes 65536 | tf_op jit(solution)/shard_map/pmax | solution.py:104
  273.6 33.0 %psum.14 = bf16[16384]{0:T(1024)(128)(2,1)S(1)} all-reduce(bf16[16384]{0:T(1024)(128)(2,1)S(1)} %fusion.33), channel_id=1, replica_groups=mesh['row'=8,'col'=4] {'row'}, use_global_device_ids=true, to_apply=%region_12.13 | all-reduce | flops 16384 | bytes 65536 | tf_op jit(solution)/shard_map/psum | solution.py:105
  306.7 85.1 %while.75 = (s32[]{:T(128)}, f32[16,4,128]{2,1,0:T(4,128)S(1)}, f32[16,4,128]{2,1,0:T(4,128)S(1)}, pred[16,4,4]{2,1,0:T(4,128)(4,1)S(1)}, s32[16,4,4]{2,1,0:T(4,...) while((s32[]{:T(128)}, f32[16,4,128]{2,1,0:T(4,128)S(1)}, ...), condition=%wide.region_16.17_spmd, body=%wide.region_13.16_spmd.sunk | while | flops 35913776 | bytes 3286177 | solution.py:70
  306.9 2.8 gather_fusion.5
  354.7 2.8 gather_fusion.5
  391.8 5.4 all-gather.2
  397.2 5.6 %all-gather.3 = f32[4,1,8192]{2,1,0:T(1,128)S(1)} all-gather(f32[1,1,8192]{2,1,0:T(1,128)S(1)} %bitcast.315), channel_id=1, replica_groups=mesh['row'=8,'col'=4] {'col'}, dimensions={0}, use_global_device_ids=true | all-gather | bytes 163840 | tf_op jit(solution)/shard_map/all_gather | solution.py:16
  403.5 68.3 %while.77 = (s32[]{:T(128)}, f32[16,4,4,128]{3,2,1,0:T(4,128)S(1)}, f32[16,4,4,128]{3,2,1,0:T(4,128)S(1)}, pred[16,4,4]{2,1,0:T(4,128)(4,1)S(1)}, f32[16,4,128]{...) while((s32[]{:T(128)}, f32[16,4,4,128]{3,2,1,0:T(4,128)S(1)}, ...), condition=%wide.region_22.23_spmd, body=%wide.region_19.22_spmd.sunk | while | flops 35652656 | bytes 3310689 | solution.py:88
  416.4 2.8 gather_fusion.8
  429.2 2.8 gather_fusion.8
  442.1 2.8 gather_fusion.8
  474.0 33.0 %pmax.15 = bf16[16384]{0:T(1024)(128)(2,1)S(1)} all-reduce(bf16[16384]{0:T(1024)(128)(2,1)S(1)} %bitcast_convert_fusion), channel_id=1, replica_groups=mesh['row'=8,'col'=4] {'row'}, use_global_device_ids=true, to_apply=%region_24.25 | all-reduce | flops 16384 | bytes 65536 | tf_op jit(solution)/shard_map/pmax | solution.py:104
  507.4 33.0 %psum.15 = bf16[16384]{0:T(1024)(128)(2,1)S(1)} all-reduce(bf16[16384]{0:T(1024)(128)(2,1)S(1)} %fusion.34), channel_id=1, replica_groups=mesh['row'=8,'col'=4] {'row'}, use_global_device_ids=true, to_apply=%region_25.26 | all-reduce | flops 16384 | bytes 65536 | tf_op jit(solution)/shard_map/psum | solution.py:105
  (723 shorter events, 269.9 us)
Async XLA Ops:
  7.2 55.0 %all-gather.6.cloned.1.call-start = ((), (), s32[]{:S(2)}) async-start(), calls=%async_computation | async-start | bytes 2359296 | tf_op jit(solution)/shard_map/all_gather | solution.py:32
  14.1 57.3 %copy-start = (f32[16384]{0:T(1024)S(1)}, f32[16384]{0:T(1024)}, u32[]{:S(2)}) copy-start(f32[16384]{0:T(1024)} %param.23) | copy-start | bytes 196612
  71.4 96.5 %copy-start.2 = (f32[8192]{0:T(1024)S(1)}, f32[8192]{0:T(1024)}, u32[]{:S(2)}) copy-start(f32[8192]{0:T(1024)} %param.21) | copy-start | bytes 98308
  168.1 138.6 %copy-start.1 = (f32[16384]{0:T(1024)S(1)}, f32[16384]{0:T(1024)}, u32[]{:S(2)}) copy-start(f32[16384]{0:T(1024)} %param.22) | copy-start | bytes 196612
  471.8 69.3 %copy-start.3 = (f32[16,4,128]{2,1,0:T(4,128)}, f32[16,4,128]{2,1,0:T(4,128)S(1)}, u32[]{:S(2)}) copy-start(f32[16,4,128]{2,1,0:T(4,128)S(1)} %get-tuple-element.1039) | copy-start | bytes 98308
Sparse Core Ops, SparseCore 0:
  10.2 51.9 all-gather.5
where the time goes:
time: 551 us; the launch traced here: 548 us
  local copies, waits for them, and re-layouts  254 us (46%)
  blocking collectives  156 us (28%)
  waiting for transfers between devices  48.7 us (9%)
  matrix products  47.5 us (9%)
  other arithmetic  24.6 us (4%)
  between operations  14.3 us (3%)
    gather x64, local copies, waits for them, and re-layouts, costs_of(): tiles = target_blocks[ids_part]  181 us
    pmax x2, blocking collectives, target_update(): lax.pmax(cell_peak.astype(jnp.bfloat16), 'row').astype(cell_peak.dtype)  67.7 us
    psum x2, blocking collectives, target_update(): lax.psum((cell_total * jnp.exp(cell_peak - peak_all)).astype(jnp.bfloat16...  66.1 us
    all_gather x1, waiting for transfers between devices, shards(): gathered = lax.all_gather(emb_target, 'row', axis=0, tiled=True)  48.1 us
    dot_general x64, matrix products, costs_of(): jnp.einsum('sid,skjd->skij', src_part, tiles, preferred_element_type=jnp....  46.8 us
    gather x64, local copies, waits for them, and re-layouts, costs_of(): target_sq[ids_part][:, :, None, :]  36 us
    all_gather x4, blocking collectives, combined_all(): pieces = jax.tree.map(lambda part: lax.all_gather(part, axis), value)  21.9 us
    gather x32, local copies, waits for them, and re-layouts, source_one_turn(): pot_blocks[ids_part][:, :, None, :] - costs_of(src_part, sq_part, ids_part)  18 us
  transfers between devices with their start and end apart: 1, of which 1 were waited for; matrix products, arithmetic and copies ran while one was open for 1% of the time, Pallas kernels for 0%

commit v1 on v0

v1 whole, which is shorter than its diff:
```python
import functools

import jax
import jax.numpy as jnp
from jax import lax
from jax.experimental import pallas as pl
from jax.experimental.pallas import tpu as pltpu
from jax.sharding import PartitionSpec as P

BLOCK = 128
eps = 0.05
scale = 1.4426950408889634 / eps
unit = eps * 0.6931471805599453
floor = -1e30
group = 4


def merge(first, second):
    peak = jnp.maximum(first, second)
    gap = jnp.minimum(first, second) - peak
    return peak + unit * jnp.log2(1.0 + jnp.exp2(gap * scale))


def squares(block):
    wide = block.astype(jnp.float32)
    return jnp.sum(wide * wide, axis=0, keepdims=True)


def split_rows(pot):
    first = pot.astype(jnp.bfloat16).astype(jnp.float32)
    rest = pot - first
    second = rest.astype(jnp.bfloat16).astype(jnp.float32)
    third = rest - second
    rows = lax.broadcasted_iota(jnp.int32, (64, BLOCK), 0)
    out = jnp.where(rows == 0, first, jnp.where(rows == 1, second, jnp.where(rows == 2, third, 0.0)))
    return out.astype(jnp.bfloat16)


def one_rows():
    rows = lax.broadcasted_iota(jnp.int32, (64, BLOCK), 0)
    return jnp.where(rows < 3, 1.0, 0.0).astype(jnp.bfloat16)


def fill(count, step):
    def body(i, _):
        for k in range(4):
            step(i * 4 + k)
        return 0

    lax.fori_loop(0, count // 4, body, 0)


def tiles_lse(meta, slots, lhs, rhs, peaks, sums, top, tot, out):
    live = meta[0]

    def tile_step(i, _):
        for k in range(group):
            p = i * group + k
            z = jnp.dot(lhs[meta[2 + p]], rhs[meta[2 + slots + p]], preferred_element_type=jnp.float32)
            z = z.reshape(BLOCK // 8, 8, BLOCK)
            peak = jnp.max(z, axis=0)
            peaks[p] = peak
            sums[p] = jnp.sum(jnp.exp2((z - peak) * scale), axis=0)
        return 0

    lax.fori_loop(0, (live + group - 1) // group, tile_step, 0)
    top[...] = jnp.full(top.shape, floor, jnp.float32)
    tot[...] = jnp.full(tot.shape, 0.125, jnp.float32)

    def peak_step(p, carry):
        last, run = carry
        b = meta[2 + slots + p]
        run = jnp.where(b == last, jnp.maximum(run, peaks[p]), peaks[p])
        top[b] = run
        return b, run

    zero = jnp.zeros((8, BLOCK), jnp.float32)
    lax.fori_loop(0, live, peak_step, (jnp.int32(-1), zero))
    top[...] = jnp.broadcast_to(jnp.max(top[...], axis=1, keepdims=True), top.shape)

    def sum_step(p, carry):
        last, run = carry
        b = meta[2 + slots + p]
        part = sums[p] * jnp.exp2((peaks[p] - top[b]) * scale)
        run = jnp.where(b == last, run + part, part)
        tot[b] = run
        return b, run

    lax.fori_loop(0, live, sum_step, (jnp.int32(-1), zero))
    out[...] = top[:, 0, :] + unit * jnp.log2(jnp.sum(tot[...], axis=1))


def load_targets(meta, chunks, yt, sems):
    n = len(chunks)
    copies = []
    for k, chunk in enumerate(chunks):
        owner = lax.rem(meta[1] + n - k, n)
        copies.append(pltpu.make_async_copy(chunk, yt.at[owner], sems.at[k]))
    for copy in copies:
        copy.start()
    return copies


def target_block(yt, per, t):
    return yt[t // per, :, pl.ds(pl.multiple_of(lax.rem(t, per) * BLOCK, BLOCK), BLOCK)]


def source_kernel(n, first, slots, *refs):
    meta, xt, pot_in = refs[:3]
    refs = refs[3:]
    if not first:
        other, mass, ysq = refs[:3]
        refs = refs[3:]
    chunks, refs = refs[:n], refs[n:]
    if first:
        out, ysq, refs = refs[0], refs[1], refs[2:]
    else:
        out, refs = refs[0], refs[1:]
    yt, sems, lhs, rhs, peaks, sums, top, tot = refs
    copies = load_targets(meta, chunks, yt, sems)
    ones = one_rows()

    def fill_rhs(b):
        rhs[b, :64] = xt[:, pl.ds(pl.multiple_of(b * BLOCK, BLOCK), BLOCK)]
        rhs[b, 64:] = ones

    fill(rhs.shape[0], fill_rhs)
    for copy in copies:
        copy.wait()
    per = yt.shape[2] // BLOCK

    def fill_lhs(a):
        block = target_block(yt, per, a)
        if first:
            sq = squares(block)
            ysq[pl.ds(a, 1), :] = sq
            pot = pot_in[pl.ds(a, 1), :] - 0.5 * sq
        else:
            lse = merge(pot_in[pl.ds(a, 1), :], other[pl.ds(a, 1), :])
            pot = unit * jnp.log2(mass[pl.ds(a, 1), :]) - lse
        lhs[a] = jnp.concatenate([block, split_rows(pot)], axis=0).T

    fill(lhs.shape[0], fill_lhs)
    tiles_lse(meta, slots, lhs, rhs, peaks, sums, top, tot, out)


def target_kernel(n, slots, meta, xt, mine, other, mass, *refs):
    chunks, refs = refs[:n], refs[n:]
    out, pot_out, yt, sems, lhs, rhs, peaks, sums, top, tot = refs
    copies = load_targets(meta, chunks, yt, sems)
    ones = one_rows()

    def fill_lhs(a):
        block = xt[:, pl.ds(pl.multiple_of(a * BLOCK, BLOCK), BLOCK)]
        lse = merge(mine[pl.ds(a, 1), :], other[pl.ds(a, 1), :])
        pot = unit * jnp.log2(mass[pl.ds(a, 1), :]) - lse
        pot_out[pl.ds(a, 1), :] = pot + 0.5 * squares(block)
        lhs[a] = jnp.concatenate([block, split_rows(pot)], axis=0).T

    fill(lhs.shape[0], fill_lhs)
    for copy in copies:
        copy.wait()
    per = yt.shape[2] // BLOCK

    def fill_rhs(b):
        rhs[b, :64] = target_block(yt, per, b)
        rhs[b, 64:] = ones

    fill(rhs.shape[0], fill_rhs)
    tiles_lse(meta, slots, lhs, rhs, peaks, sums, top, tot, out)


def call(kernel, meta, dense, chunks, outs, blocks_a, blocks_b, slots, name):
    n = len(chunks)
    vmem = pl.BlockSpec(memory_space=pltpu.VMEM)
    return pl.pallas_call(
        kernel,
        out_shape=[jax.ShapeDtypeStruct(shape, jnp.float32) for shape in outs],
        in_specs=[pl.BlockSpec(memory_space=pltpu.SMEM)]
        + [vmem] * len(dense)
        + [pl.BlockSpec(memory_space=pl.ANY)] * n,
        out_specs=[vmem] * len(outs),
        scratch_shapes=[
            pltpu.VMEM((n,) + chunks[0].shape, jnp.bfloat16),
            pltpu.SemaphoreType.DMA((n,)),
            pltpu.VMEM((blocks_a, BLOCK, BLOCK), jnp.bfloat16),
            pltpu.VMEM((blocks_b, BLOCK, BLOCK), jnp.bfloat16),
            pltpu.VMEM((slots + group, 8, BLOCK), jnp.float32),
            pltpu.VMEM((slots + group, 8, BLOCK), jnp.float32),
            pltpu.VMEM((blocks_b, 8, BLOCK), jnp.float32),
            pltpu.VMEM((blocks_b, 8, BLOCK), jnp.float32),
        ],
        compiler_params=pltpu.CompilerParams(vmem_limit_bytes=48 * 1024 * 1024),
        name=name,
    )(meta, *dense, *chunks)


def exchange(value, axis, n):
    step = 1
    while True:
        other = lax.ppermute(value, axis, [(i, i ^ step) for i in range(n)])
        step *= 2
        if step >= n:
            return value, other
        value = merge(value, other)


def tile_list(code, alive, parts):
    slots = code.shape[0]
    code = jnp.where(alive, code, (1 << 30) + jnp.arange(slots, dtype=jnp.int32))
    rank = jnp.sum((code[None, :] < code[:, None]).astype(jnp.int32), axis=1)
    places = jnp.arange(slots, dtype=jnp.int32)
    hit = (rank[None, :] == places[:, None]) & alive[None, :]
    ordered = jnp.sum(jnp.where(hit, code[None, :], 0), axis=1)
    return ordered // parts, ordered % parts


def shards(rows, cols, emb_source, emb_target, source_mass, target_mass, start_potential, support, count):
    xt = emb_source.T
    mine = emb_target.T
    chunks = [mine]
    for k in range(1, rows):
        chunks.append(lax.ppermute(mine, "row", [(i, (i + k) % rows) for i in range(rows)]))
    sources = emb_source.shape[0] // BLOCK
    targets = start_potential.shape[0] // BLOCK
    depth = support.shape[2]
    slots = sources * depth
    t_ids = support.reshape(slots)
    r_ids = jnp.arange(slots, dtype=jnp.int32) // depth
    alive = (jnp.arange(depth, dtype=jnp.int32)[None, :] < count.reshape(sources, 1)).reshape(slots)
    live = jnp.sum(alive.astype(jnp.int32))
    me = lax.axis_index("row").astype(jnp.int32)
    head = jnp.stack([live, me])
    pad = jnp.zeros((group,), jnp.int32)
    s_b, s_a = tile_list(r_ids * targets + t_ids, alive, targets)
    t_b, t_a = tile_list(t_ids * sources + r_ids, alive, sources)
    width = slots + group
    s_meta = jnp.concatenate([head, s_a, pad, s_b, pad])
    t_meta = jnp.concatenate([head, t_a, pad, t_b, pad])
    s_mass = source_mass.reshape(sources, BLOCK)
    t_mass = target_mass.reshape(targets, BLOCK)
    s_shape, t_shape = (sources, BLOCK), (targets, BLOCK)

    lse, ysq = call(
        functools.partial(source_kernel, rows, True, width), s_meta,
        [xt, start_potential.reshape(t_shape)], chunks, [s_shape, t_shape],
        targets, sources, slots, "source_first",
    )
    pair = exchange(lse, "col", cols)
    lse, _ = call(
        functools.partial(target_kernel, rows, width), t_meta,
        [xt, *pair, s_mass], chunks, [t_shape, s_shape], sources, targets, slots, "target_first",
    )
    pair = exchange(lse, "row", rows)
    (lse,) = call(
        functools.partial(source_kernel, rows, False, width), s_meta,
        [xt, *pair, t_mass, ysq], chunks, [s_shape], targets, sources, slots, "source_second",
    )
    pair = exchange(lse, "col", cols)
    lse, second_f = call(
        functools.partial(target_kernel, rows, width), t_meta,
        [xt, *pair, s_mass], chunks, [t_shape, s_shape], sources, targets, slots, "target_second",
    )
    pair = exchange(lse, "row", rows)
    second_g = eps * jnp.log(t_mass) - merge(*pair) + 0.5 * ysq
    return second_f.reshape(-1), second_g.reshape(-1)


def solution(mesh):
    in_specs = (
        P("row", None),
        P(("col", "row"), None),
        P("row"),
        P("col"),
        P("col"),
        P("row", "col", None),
        P("row", "col"),
    )
    out_specs = (P("row"), P("col"))
    body = functools.partial(shards, mesh.shape["row"], mesh.shape["col"])
    return jax.shard_map(body, mesh=mesh, in_specs=in_specs, out_specs=out_specs, check_vma=False)
```

time: 551 us -> 165 us (0.30)
  local copies, waits for them, and re-layouts: 254 us -> 4.53 us
  blocking collectives: 156 us -> 0 us
  Pallas kernels: 0 us -> 70.7 us
  matrix products: 47.5 us -> 0 us
  waiting for transfers between devices: 48.7 us -> 73 us
  other arithmetic: 24.6 us -> 2.12 us
  starting transfers between devices: 0.04 us -> 13.8 us
  between operations: 14.3 us -> 0.82 us
    gather x162 -> x0, local copies, waits for them, and re-layouts: 237 us -> none  [the longest x64 181 us: costs_of(): tiles = target_blocks[ids_part]]
    ppermute x0 -> x17, waiting for transfers between devices: none -> 73 us  [the longest x7 38.9 us: shards(): lax.ppermute(mine, 'row', [(i, (i + k) % rows) for i in range(rows)])]
    pallas_call x0 -> x4, Pallas kernels: none -> 70.7 us  [call(): pl.pallas_call(kernel, out_shape=[jax.ShapeDtypeStruct(shape, jnp.float32...]
    pmax x2 -> x0, blocking collectives: 67.7 us -> none  [target_update(): lax.pmax(cell_peak.astype(jnp.bfloat16), 'row').astype(cell_peak.dtype)]
    psum x2 -> x0, blocking collectives: 66.1 us -> none  [target_update(): lax.psum((cell_total * jnp.exp(cell_peak - peak_all)).astype(jnp.bfloat16...]
    all_gather x1 -> x0, waiting for transfers between devices: 48.1 us -> none  [shards(): gathered = lax.all_gather(emb_target, 'row', axis=0, tiled=True)]
    dot_general x66 -> x0, matrix products: 47.5 us -> none  [the longest x64 46.8 us: costs_of(): jnp.einsum('sid,skjd->skij', src_part, tiles, preferred_element_type=jnp....]
    all_gather x4 -> x0, blocking collectives: 21.9 us -> none  [combined_all(): pieces = jax.tree.map(lambda part: lax.all_gather(part, axis), value)]
  transfers between devices with their start and end apart: 1 -> 17, of which waited for: 1 -> 15; matrix products, arithmetic and copies ran while one was open for 1% -> 2% of each run, Pallas kernels for 0% -> 0%
where the time goes in v1:
time: 165 us
  waiting for transfers between devices  73 us (44%)
  Pallas kernels  70.7 us (43%)
  starting transfers between devices  13.8 us (8%)
  local copies, waits for them, and re-layouts  4.53 us (3%)
  other arithmetic  2.12 us (1%)
    pallas_call x4, Pallas kernels, call(): pl.pallas_call(kernel, out_shape=[jax.ShapeDtypeStruct(shape, jnp.float32...  70.7 us
    ppermute x7, waiting for transfers between devices, shards(): lax.ppermute(mine, 'row', [(i, (i + k) % rows) for i in range(rows)])  38.9 us
    ppermute x10, waiting for transfers between devices, exchange(): other = lax.ppermute(value, axis, [(i, i ^ step) for i in range(n)])  34.1 us
    ppermute x7, starting transfers between devices, shards(): lax.ppermute(mine, 'row', [(i, (i + k) % rows) for i in range(rows)])  9.5 us
    ppermute x10, starting transfers between devices, exchange(): other = lax.ppermute(value, axis, [(i, i ^ step) for i in range(n)])  4.25 us
  transfers between devices with their start and end apart: 17, of which 15 were waited for; matrix products, arithmetic and copies ran while one was open for 2% of the time, Pallas kernels for 0%

profile of v1, /device:TPU:0, one launch (start us, length us, event | category | flops | bytes accessed | tf_op | source)
XLA Modules:
  0.0 164.9 jit_solution(6127900354060027571)
XLA Ops:
  0.6 6.1 %collective-permute-start.6 = (bf16[64,2048]{1,0:T(8,128)(2,1)}, bf16[64,2048]{1,0:T(8,128)(2,1)S(1)}, u32[]{:S(2)}, u32[]{:S(2)}) collective-permute-start(bf16[64,2048]{1,0:T(8,128)(2,1)} %bitcast.18), channel_id=1, source_target_pairs={{0,28},{4,0},{8,4},{12,8},{16,12},{20,16},{24,20},{28,24},{1,29},{... | collective-permute-start | bytes 786440 | tf_op jit(solution)/shard_map/ppermute | solution.py:223
  6.7 0.4 collective-permute-start.5
  7.2 3.0 %collective-permute-start.3 = (bf16[64,2048]{1,0:T(8,128)(2,1)}, bf16[64,2048]{1,0:T(8,128)(2,1)S(1)}, u32[]{:S(2)}, u32[]{:S(2)}) collective-permute-start(bf16[64,2048]{1,0:T(8,128)(2,1)} %bitcast.21), channel_id=1, source_target_pairs={{0,16},{4,20},{8,24},{12,28},{16,0},{20,4},{24,8},{28,12},{1,17},{... | collective-permute-start | bytes 786440 | tf_op jit(solution)/shard_map/ppermute | solution.py:223
  10.3 0.6 copy-done.7
  11.1 0.3 convert_reduce_fusion
  11.6 2.3 %collective-permute-done.6.refs_10_.refs_7_.refs_13_ = bf16[64,2048]{1,0:T(8,128)(2,1)S(1)} collective-permute-done((bf16[64,2048]{1,0:T(8,128)(2,1)}, bf16[64,2048]{1,0:T(8,128)(2,1)S(1)}, u32[]{:S(2)}, u32[]{:S(2)}) %collective-permute-start.6) | collective-permute-done | bytes 262176 | tf_op jit(solution)/shard_map/ppermute | solution.py:223
  13.8 5.6 %collective-permute-done.5.refs_9_.refs_6_.refs_12_ = bf16[64,2048]{1,0:T(8,128)(2,1)S(1)} collective-permute-done((bf16[64,2048]{1,0:T(8,128)(2,1)}, bf16[64,2048]{1,0:T(8,128)(2,1)S(1)}, u32[]{:S(2)}, u32[]{:S(2)}) %collective-permute-start.5) | collective-permute-done | bytes 262176 | tf_op jit(solution)/shard_map/ppermute | solution.py:223
  19.4 0.7 convert_reduce_fusion.2
  20.2 0.7 concatenate.9.refs_0_
  20.9 4.2 %collective-permute-done.4.refs_8_.refs_5_.refs_11_ = bf16[64,2048]{1,0:T(8,128)(2,1)S(1)} collective-permute-done((bf16[64,2048]{1,0:T(8,128)(2,1)}, bf16[64,2048]{1,0:T(8,128)(2,1)S(1)}, u32[]{:S(2)}, u32[]{:S(2)}) %collective-permute-start.4) | collective-permute-done | bytes 262176 | tf_op jit(solution)/shard_map/ppermute | solution.py:223
  25.1 26.6 %collective-permute-done.3.refs_7_.refs_4_.refs_10_ = bf16[64,2048]{1,0:T(8,128)(2,1)S(1)} collective-permute-done((bf16[64,2048]{1,0:T(8,128)(2,1)}, bf16[64,2048]{1,0:T(8,128)(2,1)S(1)}, u32[]{:S(2)}, u32[]{:S(2)}) %collective-permute-start.3) | collective-permute-done | bytes 262176 | tf_op jit(solution)/shard_map/ppermute | solution.py:223
  51.9 1.2 copy-done
  53.2 0.9 copy-done.2
  54.1 17.9 %source_first.1 = (f32[64,128]{1,0:T(8,128)S(1)}, f32[128,128]{1,0:T(8,128)S(1)}) custom-call(s32[522]{0:T(1024)S(1)} %concatenate.9.refs_0_, bf16[64,8192]{1,0:T(8,128)(2,1)S(1)} %bitcast.14, f32[128,128]{1,0:T(8,128)S(1)} %bitcast.32, bf16[64,2048]{1,0:T(8,128)(2,1)S(1)} %bitcast.25, bf16[64,2048]{1,0:T(8,128)(2,1)S(1)} %collective-permute-done.refs_4_.refs_1_.refs_7_, ...), custom_call_target="tpu_custom_call" | custom-call | tf_op jit(solution)/shard_map/source_first/pallas_call | solution.py:176
  72.1 1.2 collective-permute-done.7
  73.3 1.3 collective-permute-start.8
  74.6 0.7 concatenate.8.meta
  75.4 2.0 %collective-permute-done.8.other = f32[64,128]{1,0:T(8,128)S(1)} collective-permute-done((f32[64,128]{1,0:T(8,128)S(1)}, f32[64,128]{1,0:T(8,128)S(1)}, u32[]{:S(2)}, u32[]{:S(2)}) %collective-permute-start.8) | collective-permute-done | bytes 32800 | tf_op jit(solution)/shard_map/ppermute | solution.py:201
  77.3 17.4 %target_first.1 = (f32[128,128]{1,0:T(8,128)S(1)}, f32[64,128]{1,0:T(8,128)}) custom-call(s32[522]{0:T(1024)S(1)} %concatenate.8.meta, bf16[64,8192]{1,0:T(8,128)(2,1)S(1)} %bitcast.15, f32[64,128]{1,0:T(8,128)S(1)} %multiply_add_fusion.5.mine, f32[64,128]{1,0:T(8,128)S(1)} %collective-permute-done.8.other, f32[64,128]{1,0:T(8,128)S(1)} %bitcast.30, ...), custom_call_target="tpu_custom_call" | custom-call | tf_op jit(solution)/shard_map/target_first/pallas_call | solution.py:176
  94.8 4.3 %collective-permute-done.9 = f32[128,128]{1,0:T(8,128)S(1)} collective-permute-done((f32[128,128]{1,0:T(8,128)S(1)}, f32[128,128]{1,0:T(8,128)S(1)}, u32[]{:S(2)}, u32[]{:S(2)}) %collective-permute-start.9) | collective-permute-done | bytes 65568 | tf_op jit(solution)/shard_map/ppermute | solution.py:201
  99.2 4.3 %collective-permute-done.10 = f32[128,128]{1,0:T(8,128)S(1)} collective-permute-done((f32[128,128]{1,0:T(8,128)S(1)}, f32[128,128]{1,0:T(8,128)S(1)}, u32[]{:S(2)}, u32[]{:S(2)}) %collective-permute-start.10) | collective-permute-done | bytes 65568 | tf_op jit(solution)/shard_map/ppermute | solution.py:201
  103.5 1.9 %collective-permute-start.11 = (f32[128,128]{1,0:T(8,128)S(1)}, f32[128,128]{1,0:T(8,128)S(1)}, u32[]{:S(2)}, u32[]{:S(2)}) collective-permute-start(f32[128,128]{1,0:T(8,128)S(1)} %multiply_add_fusion.2.refs_2_), channel_id=1, source_target_pairs={{0,16},{4,20},{8,24},{12,28},{16,0},{20,4},{24,8},{28,12},{1,17},{... | collective-permute-start | bytes 196616 | tf_op jit(solution)/shard_map/ppermute | solution.py:201
  105.4 3.5 %collective-permute-done.11.refs_3_ = f32[128,128]{1,0:T(8,128)S(1)} collective-permute-done((f32[128,128]{1,0:T(8,128)S(1)}, f32[128,128]{1,0:T(8,128)S(1)}, u32[]{:S(2)}, u32[]{:S(2)}) %collective-permute-start.11) | collective-permute-done | bytes 65568 | tf_op jit(solution)/shard_map/ppermute | solution.py:201
  108.9 17.9 %source_second.1 = f32[64,128]{1,0:T(8,128)S(1)} custom-call(s32[522]{0:T(1024)S(1)} %concatenate.9.refs_0_, bf16[64,8192]{1,0:T(8,128)(2,1)S(1)} %bitcast.16, f32[128,128]{1,0:T(8,128)S(1)} %multiply_add_fusion.2.refs_2_, f32[128,128]{1,0:T(8,128)S(1)} %collective-permute-done.11.refs_3_, f32[128,128]{1,0:T(8,128)S(1)} %bitcast.29, ...), custom_call_target="tpu_custom_call" | custom-call | tf_op jit(solution)/shard_map/source_second/pallas_call | solution.py:176
  126.9 1.2 collective-permute-done.12
  128.1 0.6 collective-permute-start.13
  128.7 3.4 %collective-permute-done.13.other = f32[64,128]{1,0:T(8,128)S(1)} collective-permute-done((f32[64,128]{1,0:T(8,128)S(1)}, f32[64,128]{1,0:T(8,128)S(1)}, u32[]{:S(2)}, u32[]{:S(2)}) %collective-permute-start.13) | collective-permute-done | bytes 32800 | tf_op jit(solution)/shard_map/ppermute | solution.py:201
  132.1 17.4 %target_second.1 = (f32[128,128]{1,0:T(8,128)S(1)}, f32[64,128]{1,0:T(8,128)}) custom-call(s32[522]{0:T(1024)S(1)} %concatenate.8.meta, bf16[64,8192]{1,0:T(8,128)(2,1)S(1)} %bitcast.17, f32[64,128]{1,0:T(8,128)S(1)} %multiply_add_fusion.4.mine, f32[64,128]{1,0:T(8,128)S(1)} %collective-permute-done.13.other, f32[64,128]{1,0:T(8,128)S(1)} %bitcast.31, ...), custom_call_target="tpu_custom_call" | custom-call | tf_op jit(solution)/shard_map/target_second/pallas_call | solution.py:176
  149.6 4.3 %collective-permute-done.14 = f32[128,128]{1,0:T(8,128)S(1)} collective-permute-done((f32[128,128]{1,0:T(8,128)S(1)}, f32[128,128]{1,0:T(8,128)S(1)}, u32[]{:S(2)}, u32[]{:S(2)}) %collective-permute-start.14) | collective-permute-done | bytes 65568 | tf_op jit(solution)/shard_map/ppermute | solution.py:201
  154.0 5.0 %collective-permute-done.15 = f32[128,128]{1,0:T(8,128)S(1)} collective-permute-done((f32[128,128]{1,0:T(8,128)S(1)}, f32[128,128]{1,0:T(8,128)S(1)}, u32[]{:S(2)}, u32[]{:S(2)}) %collective-permute-start.15) | collective-permute-done | bytes 65568 | tf_op jit(solution)/shard_map/ppermute | solution.py:201
  159.0 5.2 %collective-permute-done.16 = f32[128,128]{1,0:T(8,128)S(1)} collective-permute-done((f32[128,128]{1,0:T(8,128)S(1)}, f32[128,128]{1,0:T(8,128)S(1)}, u32[]{:S(2)}, u32[]{:S(2)}) %collective-permute-start.16) | collective-permute-done | bytes 65568 | tf_op jit(solution)/shard_map/ppermute | solution.py:201
  164.2 0.7 add_bitcast_fusion
  (44 shorter events, 1.6 us)
Async XLA Ops:
  0.6 9.5 %copy-start.8 = (s32[64,1]{0,1:T(1,128)S(1)}, s32[64,1]{0,1:T(1,128)}, u32[]{:S(2)}) copy-start(s32[64,1]{0,1:T(1,128)} %param.13) | copy-start | bytes 772
  0.6 13.2 %collective-permute-start.6 = (bf16[64,2048]{1,0:T(8,128)(2,1)}, bf16[64,2048]{1,0:T(8,128)(2,1)S(1)}, u32[]{:S(2)}, u32[]{:S(2)}) collective-permute-start(bf16[64,2048]{1,0:T(8,128)(2,1)} %bitcast.18), channel_id=1, source_target_pairs={{0,28},{4,0},{8,4},{12,8},{16,12},{20,16},{24,20},{28,24},{1,29},{... | collective-permute-start | bytes 786440 | tf_op jit(solution)/shard_map/ppermute | solution.py:223
  6.7 12.7 %collective-permute-start.5 = (bf16[64,2048]{1,0:T(8,128)(2,1)}, bf16[64,2048]{1,0:T(8,128)(2,1)S(1)}, u32[]{:S(2)}, u32[]{:S(2)}) collective-permute-start(bf16[64,2048]{1,0:T(8,128)(2,1)} %bitcast.19), channel_id=1, source_target_pairs={{0,24},{4,28},{8,0},{12,4},{16,8},{20,12},{24,16},{28,20},{1,25},{... | collective-permute-start | bytes 786440 | tf_op jit(solution)/shard_map/ppermute | solution.py:223
  7.1 17.9 %collective-permute-start.4 = (bf16[64,2048]{1,0:T(8,128)(2,1)}, bf16[64,2048]{1,0:T(8,128)(2,1)S(1)}, u32[]{:S(2)}, u32[]{:S(2)}) collective-permute-start(bf16[64,2048]{1,0:T(8,128)(2,1)} %bitcast.20), channel_id=1, source_target_pairs={{0,20},{4,24},{8,28},{12,0},{16,4},{20,8},{24,12},{28,16},{1,21},{... | collective-permute-start | bytes 786440 | tf_op jit(solution)/shard_map/ppermute | solution.py:223
  7.2 44.5 %collective-permute-start.3 = (bf16[64,2048]{1,0:T(8,128)(2,1)}, bf16[64,2048]{1,0:T(8,128)(2,1)S(1)}, u32[]{:S(2)}, u32[]{:S(2)}) collective-permute-start(bf16[64,2048]{1,0:T(8,128)(2,1)} %bitcast.21), channel_id=1, source_target_pairs={{0,16},{4,20},{8,24},{12,28},{16,0},{20,4},{24,8},{28,12},{1,17},{... | collective-permute-start | bytes 786440 | tf_op jit(solution)/shard_map/ppermute | solution.py:223
  10.1 41.8 %collective-permute-start.2 = (bf16[64,2048]{1,0:T(8,128)(2,1)}, bf16[64,2048]{1,0:T(8,128)(2,1)S(1)}, u32[]{:S(2)}, u32[]{:S(2)}) collective-permute-start(bf16[64,2048]{1,0:T(8,128)(2,1)} %bitcast.22), channel_id=1, source_target_pairs={{0,12},{4,16},{8,20},{12,24},{16,28},{20,0},{24,4},{28,8},{1,13},{... | collective-permute-start | bytes 786440 | tf_op jit(solution)/shard_map/ppermute | solution.py:223
  10.2 0.7 copy-start.7
  10.9 41.0 %copy-start.6 = (f32[16384]{0:T(1024)S(1)}, f32[16384]{0:T(1024)}, u32[]{:S(2)}) copy-start(f32[16384]{0:T(1024)} %param.11) | copy-start | bytes 196612
  13.8 38.1 %collective-permute-start.1 = (bf16[64,2048]{1,0:T(8,128)(2,1)}, bf16[64,2048]{1,0:T(8,128)(2,1)S(1)}, u32[]{:S(2)}, u32[]{:S(2)}) collective-permute-start(bf16[64,2048]{1,0:T(8,128)(2,1)} %bitcast.23), channel_id=1, source_target_pairs={{0,8},{4,12},{8,16},{12,20},{16,24},{20,28},{24,0},{28,4},{1,9},{5... | collective-permute-start | bytes 786440 | tf_op jit(solution)/shard_map/ppermute | solution.py:223
  19.4 32.5 %collective-permute-start = (bf16[64,2048]{1,0:T(8,128)(2,1)}, bf16[64,2048]{1,0:T(8,128)(2,1)S(1)}, u32[]{:S(2)}, u32[]{:S(2)}) collective-permute-start(bf16[64,2048]{1,0:T(8,128)(2,1)} %bitcast.24), channel_id=1, source_target_pairs={{0,4},{4,8},{8,12},{12,16},{16,20},{20,24},{24,28},{28,0},{1,5},{5... | collective-permute-start | bytes 786440 | tf_op jit(solution)/shard_map/ppermute | solution.py:223
  51.9 1.2 copy-start
  53.2 0.9 copy-start.2
  54.1 23.2 %copy-start.1 = (bf16[8192,64]{0,1:T(8,128)(2,1)S(1)}, bf16[8192,64]{0,1:T(8,128)(2,1)}, u32[]{:S(2)}) copy-start(bf16[8192,64]{0,1:T(8,128)(2,1)} %param.7) | copy-start | bytes 3145732
  54.1 23.2 %copy-start.3 = (bf16[2048,64]{0,1:T(8,128)(2,1)S(1)}, bf16[2048,64]{0,1:T(8,128)(2,1)}, u32[]{:S(2)}) copy-start(bf16[2048,64]{0,1:T(8,128)(2,1)} %param.8) | copy-start | bytes 786436
  72.0 1.3 collective-permute-start.7
  73.3 4.0 %copy-start.5 = (f32[8192]{0:T(1024)S(1)}, f32[8192]{0:T(1024)}, u32[]{:S(2)}) copy-start(f32[8192]{0:T(1024)} %param.9) | copy-start | bytes 98308
  73.3 4.0 %collective-permute-start.8 = (f32[64,128]{1,0:T(8,128)S(1)}, f32[64,128]{1,0:T(8,128)S(1)}, u32[]{:S(2)}, u32[]{:S(2)}) collective-permute-start(f32[64,128]{1,0:T(8,128)S(1)} %multiply_add_fusion.5.mine), channel_id=1, source_target_pairs={{0,2},{1,3},{2,0},{3,1},{4,6},{5,7},{6,4},{7,5},{8,10},{9,11},{10,... | collective-permute-start | bytes 98312 | tf_op jit(solution)/shard_map/ppermute | solution.py:201
  94.8 4.3 %collective-permute-start.9 = (f32[128,128]{1,0:T(8,128)S(1)}, f32[128,128]{1,0:T(8,128)S(1)}, u32[]{:S(2)}, u32[]{:S(2)}) collective-permute-start(f32[128,128]{1,0:T(8,128)S(1)} %get-tuple-element.8), channel_id=1, source_target_pairs={{0,4},{4,0},{8,12},{12,8},{16,20},{20,16},{24,28},{28,24},{1,5},{5... | collective-permute-start | bytes 196616 | tf_op jit(solution)/shard_map/ppermute | solution.py:201
  99.1 9.8 %copy-start.4 = (f32[16384]{0:T(1024)S(1)}, f32[16384]{0:T(1024)}, u32[]{:S(2)}) copy-start(f32[16384]{0:T(1024)} %param.10) | copy-start | bytes 196612
  99.1 4.3 %collective-permute-start.10 = (f32[128,128]{1,0:T(8,128)S(1)}, f32[128,128]{1,0:T(8,128)S(1)}, u32[]{:S(2)}, u32[]{:S(2)}) collective-permute-start(f32[128,128]{1,0:T(8,128)S(1)} %multiply_add_fusion.3), channel_id=1, source_target_pairs={{0,8},{4,12},{8,0},{12,4},{16,24},{20,28},{24,16},{28,20},{1,9},{5... | collective-permute-start | bytes 196616 | tf_op jit(solution)/shard_map/ppermute | solution.py:201
  103.5 5.4 %collective-permute-start.11 = (f32[128,128]{1,0:T(8,128)S(1)}, f32[128,128]{1,0:T(8,128)S(1)}, u32[]{:S(2)}, u32[]{:S(2)}) collective-permute-start(f32[128,128]{1,0:T(8,128)S(1)} %multiply_add_fusion.2.refs_2_), channel_id=1, source_target_pairs={{0,16},{4,20},{8,24},{12,28},{16,0},{20,4},{24,8},{28,12},{1,17},{... | collective-permute-start | bytes 196616 | tf_op jit(solution)/shard_map/ppermute | solution.py:201
  126.8 1.3 collective-permute-start.12
  128.1 4.0 %collective-permute-start.13 = (f32[64,128]{1,0:T(8,128)S(1)}, f32[64,128]{1,0:T(8,128)S(1)}, u32[]{:S(2)}, u32[]{:S(2)}) collective-permute-start(f32[64,128]{1,0:T(8,128)S(1)} %multiply_add_fusion.4.mine), channel_id=1, source_target_pairs={{0,2},{1,3},{2,0},{3,1},{4,6},{5,7},{6,4},{7,5},{8,10},{9,11},{10,... | collective-permute-start | bytes 98312 | tf_op jit(solution)/shard_map/ppermute | solution.py:201
  149.5 4.3 %collective-permute-start.14 = (f32[128,128]{1,0:T(8,128)S(1)}, f32[128,128]{1,0:T(8,128)S(1)}, u32[]{:S(2)}, u32[]{:S(2)}) collective-permute-start(f32[128,128]{1,0:T(8,128)S(1)} %get-tuple-element.11), channel_id=1, source_target_pairs={{0,4},{4,0},{8,12},{12,8},{16,20},{20,16},{24,28},{28,24},{1,5},{5... | collective-permute-start | bytes 196616 | tf_op jit(solution)/shard_map/ppermute | solution.py:201
  153.9 5.0 %collective-permute-start.15 = (f32[128,128]{1,0:T(8,128)S(1)}, f32[128,128]{1,0:T(8,128)S(1)}, u32[]{:S(2)}, u32[]{:S(2)}) collective-permute-start(f32[128,128]{1,0:T(8,128)S(1)} %multiply_add_fusion.1), channel_id=1, source_target_pairs={{0,8},{4,12},{8,0},{12,4},{16,24},{20,28},{24,16},{28,20},{1,9},{5... | collective-permute-start | bytes 196616 | tf_op jit(solution)/shard_map/ppermute | solution.py:201
  159.0 5.2 %collective-permute-start.16 = (f32[128,128]{1,0:T(8,128)S(1)}, f32[128,128]{1,0:T(8,128)S(1)}, u32[]{:S(2)}, u32[]{:S(2)}) collective-permute-start(f32[128,128]{1,0:T(8,128)S(1)} %multiply_add_fusion), channel_id=1, source_target_pairs={{0,16},{4,20},{8,24},{12,28},{16,0},{20,4},{24,8},{28,12},{1,17},{... | collective-permute-start | bytes 196616 | tf_op jit(solution)/shard_map/ppermute | solution.py:201

commit v2 on v1

--- a/solution.py
+++ b/solution.py
@@ -12,7 +12,7 @@
 scale = 1.4426950408889634 / eps
 unit = eps * 0.6931471805599453
 floor = -1e30
-group = 4
+group = 16
 
 
 def merge(first, second):
@@ -43,11 +43,11 @@
 
 def fill(count, step):
     def body(i, _):
-        for k in range(4):
-            step(i * 4 + k)
+        for k in range(16):
+            step(i * 16 + k)
         return 0
 
-    lax.fori_loop(0, count // 4, body, 0)
+    lax.fori_loop(0, count // 16, body, 0)
 
 
 def tiles_lse(meta, slots, lhs, rhs, peaks, sums, top, tot, out):
@@ -67,27 +67,36 @@
     top[...] = jnp.full(top.shape, floor, jnp.float32)
     tot[...] = jnp.full(tot.shape, 0.125, jnp.float32)
 
-    def peak_step(p, carry):
+    def peak_step(i, carry):
         last, run = carry
-        b = meta[2 + slots + p]
-        run = jnp.where(b == last, jnp.maximum(run, peaks[p]), peaks[p])
-        top[b] = run
-        return b, run
+        for k in range(group):
+            p = i * group + k
+            b = meta[2 + slots + p]
+            run = jnp.where(b == last, jnp.maximum(run, peaks[p]), peaks[p])
+            top[b] = run
+            last = b
+        return last, run
 
     zero = jnp.zeros((8, BLOCK), jnp.float32)
-    lax.fori_loop(0, live, peak_step, (jnp.int32(-1), zero))
+    turns = (live + group - 1) // group
+    lax.fori_loop(0, turns, peak_step, (jnp.int32(-1), zero))
     top[...] = jnp.broadcast_to(jnp.max(top[...], axis=1, keepdims=True), top.shape)
 
-    def sum_step(p, carry):
+    def sum_step(i, carry):
         last, run = carry
-        b = meta[2 + slots + p]
-        part = sums[p] * jnp.exp2((peaks[p] - top[b]) * scale)
-        run = jnp.where(b == last, run + part, part)
-        tot[b] = run
-        return b, run
-
-    lax.fori_loop(0, live, sum_step, (jnp.int32(-1), zero))
-    out[...] = top[:, 0, :] + unit * jnp.log2(jnp.sum(tot[...], axis=1))
+        for k in range(group):
+            p = i * group + k
+            b = meta[2 + slots + p]
+            part = sums[p] * jnp.exp2((peaks[p] - top[b]) * scale)
+            run = jnp.where(b == last, run + part, part)
+            tot[b] = run
+            last = b
+        return last, run
+
+    lax.fori_loop(0, turns, sum_step, (jnp.int32(-1), zero))
+    blocks = out.shape[0]
+    lse = top[:, 0, :] + unit * jnp.log2(jnp.sum(tot[...], axis=1))
+    out[...] = lse[:blocks]
 
 
 def load_targets(meta, chunks, yt, sems):
@@ -124,7 +133,7 @@
         rhs[b, :64] = xt[:, pl.ds(pl.multiple_of(b * BLOCK, BLOCK), BLOCK)]
         rhs[b, 64:] = ones
 
-    fill(rhs.shape[0], fill_rhs)
+    fill(rhs.shape[0] - 1, fill_rhs)
     for copy in copies:
         copy.wait()
     per = yt.shape[2] // BLOCK
@@ -166,7 +175,7 @@
         rhs[b, :64] = target_block(yt, per, b)
         rhs[b, 64:] = ones
 
-    fill(rhs.shape[0], fill_rhs)
+    fill(rhs.shape[0] - 1, fill_rhs)
     tiles_lse(meta, slots, lhs, rhs, peaks, sums, top, tot, out)
 
 
@@ -184,11 +193,11 @@
             pltpu.VMEM((n,) + chunks[0].shape, jnp.bfloat16),
             pltpu.SemaphoreType.DMA((n,)),
             pltpu.VMEM((blocks_a, BLOCK, BLOCK), jnp.bfloat16),
-            pltpu.VMEM((blocks_b, BLOCK, BLOCK), jnp.bfloat16),
+            pltpu.VMEM((blocks_b + 1, BLOCK, BLOCK), jnp.bfloat16),
             pltpu.VMEM((slots + group, 8, BLOCK), jnp.float32),
             pltpu.VMEM((slots + group, 8, BLOCK), jnp.float32),
-            pltpu.VMEM((blocks_b, 8, BLOCK), jnp.float32),
-            pltpu.VMEM((blocks_b, 8, BLOCK), jnp.float32),
+            pltpu.VMEM((blocks_b + 1, 8, BLOCK), jnp.float32),
+            pltpu.VMEM((blocks_b + 1, 8, BLOCK), jnp.float32),
         ],
         compiler_params=pltpu.CompilerParams(vmem_limit_bytes=48 * 1024 * 1024),
         name=name,
@@ -205,13 +214,13 @@
         value = merge(value, other)
 
 
-def tile_list(code, alive, parts):
+def tile_list(code, alive, parts, after):
     slots = code.shape[0]
     code = jnp.where(alive, code, (1 << 30) + jnp.arange(slots, dtype=jnp.int32))
     rank = jnp.sum((code[None, :] < code[:, None]).astype(jnp.int32), axis=1)
     places = jnp.arange(slots, dtype=jnp.int32)
     hit = (rank[None, :] == places[:, None]) & alive[None, :]
-    ordered = jnp.sum(jnp.where(hit, code[None, :], 0), axis=1)
+    ordered = jnp.sum(jnp.where(hit, code[None, :] - after, 0), axis=1) + after
     return ordered // parts, ordered % parts
 
 
@@ -232,11 +241,11 @@
     me = lax.axis_index("row").astype(jnp.int32)
     head = jnp.stack([live, me])
     pad = jnp.zeros((group,), jnp.int32)
-    s_b, s_a = tile_list(r_ids * targets + t_ids, alive, targets)
-    t_b, t_a = tile_list(t_ids * sources + r_ids, alive, sources)
+    s_b, s_a = tile_list(r_ids * targets + t_ids, alive, targets, sources * targets)
+    t_b, t_a = tile_list(t_ids * sources + r_ids, alive, sources, sources * targets)
     width = slots + group
-    s_meta = jnp.concatenate([head, s_a, pad, s_b, pad])
-    t_meta = jnp.concatenate([head, t_a, pad, t_b, pad])
+    s_meta = jnp.concatenate([head, s_a, pad, s_b, pad + sources])
+    t_meta = jnp.concatenate([head, t_a, pad, t_b, pad + targets])
     s_mass = source_mass.reshape(sources, BLOCK)
     t_mass = target_mass.reshape(targets, BLOCK)
     s_shape, t_shape = (sources, BLOCK), (targets, BLOCK)

time: 165 us -> 127 us (0.77)
  Pallas kernels: 70.7 us -> 32.6 us
  starting transfers between devices: 13.8 us -> 18.9 us
  waiting for transfers between devices: 73 us -> 67.9 us
    pallas_call x4, Pallas kernels: 70.7 us -> 32.6 us  [call(): pl.pallas_call(kernel, out_shape=[jax.ShapeDtypeStruct(shape, jnp.float32...]
    ppermute x10, starting transfers between devices: 4.25 us -> 9.44 us  [exchange(): other = lax.ppermute(value, axis, [(i, i ^ step) for i in range(n)])]
    ppermute x10, waiting for transfers between devices: 34.1 us -> 29 us  [exchange(): other = lax.ppermute(value, axis, [(i, i ^ step) for i in range(n)])]
where the time goes in v2:
time: 127 us
  waiting for transfers between devices  67.9 us (53%)
  Pallas kernels  32.6 us (26%)
  starting transfers between devices  18.9 us (15%)
  local copies, waits for them, and re-layouts  4.54 us (4%)
  other arithmetic  2.12 us (2%)
    ppermute x7, waiting for transfers between devices, shards(): lax.ppermute(mine, 'row', [(i, (i + k) % rows) for i in range(rows)])  38.9 us
    pallas_call x4, Pallas kernels, call(): pl.pallas_call(kernel, out_shape=[jax.ShapeDtypeStruct(shape, jnp.float32...  32.6 us
    ppermute x10, waiting for transfers between devices, exchange(): other = lax.ppermute(value, axis, [(i, i ^ step) for i in range(n)])  29 us
    ppermute x7, starting transfers between devices, shards(): lax.ppermute(mine, 'row', [(i, (i + k) % rows) for i in range(rows)])  9.5 us
    ppermute x10, starting transfers between devices, exchange(): other = lax.ppermute(value, axis, [(i, i ^ step) for i in range(n)])  9.44 us
    unnamed x19, local copies, waits for them, and re-layouts  2.86 us
  transfers between devices with their start and end apart: 17, of which 15 were waited for; matrix products, arithmetic and copies ran while one was open for 2% of the time, Pallas kernels for 0%

profile of v2, /device:TPU:0, one launch (start us, length us, event | category | flops | bytes accessed | tf_op | source)
XLA Modules:
  0.0 126.9 jit_solution(16988683315863358599)
XLA Ops:
  0.6 6.1 %collective-permute-start.6 = (bf16[64,2048]{1,0:T(8,128)(2,1)}, bf16[64,2048]{1,0:T(8,128)(2,1)S(1)}, u32[]{:S(2)}, u32[]{:S(2)}) collective-permute-start(bf16[64,2048]{1,0:T(8,128)(2,1)} %bitcast.18), channel_id=1, source_target_pairs={{0,28},{4,0},{8,4},{12,8},{16,12},{20,16},{24,20},{28,24},{1,29},{... | collective-permute-start | bytes 786440 | tf_op jit(solution)/shard_map/ppermute | solution.py:232
  7.2 3.0 %collective-permute-start.3 = (bf16[64,2048]{1,0:T(8,128)(2,1)}, bf16[64,2048]{1,0:T(8,128)(2,1)S(1)}, u32[]{:S(2)}, u32[]{:S(2)}) collective-permute-start(bf16[64,2048]{1,0:T(8,128)(2,1)} %bitcast.21), channel_id=1, source_target_pairs={{0,16},{4,20},{8,24},{12,28},{16,0},{20,4},{24,8},{28,12},{1,17},{... | collective-permute-start | bytes 786440 | tf_op jit(solution)/shard_map/ppermute | solution.py:232
  10.3 0.6 copy-done.7
  11.6 2.3 %collective-permute-done.6.refs_10_.refs_7_.refs_13_ = bf16[64,2048]{1,0:T(8,128)(2,1)S(1)} collective-permute-done((bf16[64,2048]{1,0:T(8,128)(2,1)}, bf16[64,2048]{1,0:T(8,128)(2,1)S(1)}, u32[]{:S(2)}, u32[]{:S(2)}) %collective-permute-start.6) | collective-permute-done | bytes 262176 | tf_op jit(solution)/shard_map/ppermute | solution.py:232
  13.8 5.6 %collective-permute-done.5.refs_9_.refs_6_.refs_12_ = bf16[64,2048]{1,0:T(8,128)(2,1)S(1)} collective-permute-done((bf16[64,2048]{1,0:T(8,128)(2,1)}, bf16[64,2048]{1,0:T(8,128)(2,1)S(1)}, u32[]{:S(2)}, u32[]{:S(2)}) %collective-permute-start.5) | collective-permute-done | bytes 262176 | tf_op jit(solution)/shard_map/ppermute | solution.py:232
  19.4 0.7 convert_reduce_fusion.2
  20.2 0.7 concatenate.9.refs_0_
  20.9 4.2 %collective-permute-done.4.refs_8_.refs_5_.refs_11_ = bf16[64,2048]{1,0:T(8,128)(2,1)S(1)} collective-permute-done((bf16[64,2048]{1,0:T(8,128)(2,1)}, bf16[64,2048]{1,0:T(8,128)(2,1)S(1)}, u32[]{:S(2)}, u32[]{:S(2)}) %collective-permute-start.4) | collective-permute-done | bytes 262176 | tf_op jit(solution)/shard_map/ppermute | solution.py:232
  25.1 26.6 %collective-permute-done.3.refs_7_.refs_4_.refs_10_ = bf16[64,2048]{1,0:T(8,128)(2,1)S(1)} collective-permute-done((bf16[64,2048]{1,0:T(8,128)(2,1)}, bf16[64,2048]{1,0:T(8,128)(2,1)S(1)}, u32[]{:S(2)}, u32[]{:S(2)}) %collective-permute-start.3) | collective-permute-done | bytes 262176 | tf_op jit(solution)/shard_map/ppermute | solution.py:232
  51.9 1.2 copy-done
  53.2 0.9 copy-done.2
  54.1 8.0 %source_first.1 = (f32[64,128]{1,0:T(8,128)S(1)}, f32[128,128]{1,0:T(8,128)S(1)}) custom-call(s32[546]{0:T(1024)S(1)} %concatenate.9.refs_0_, bf16[64,8192]{1,0:T(8,128)(2,1)S(1)} %bitcast.14, f32[128,128]{1,0:T(8,128)S(1)} %bitcast.32, bf16[64,2048]{1,0:T(8,128)(2,1)S(1)} %bitcast.25, bf16[64,2048]{1,0:T(8,128)(2,1)S(1)} %collective-permute-done.refs_4_.refs_1_.refs_7_, ...), custom_call_target="tpu_custom_call" | custom-call | tf_op jit(solution)/shard_map/source_first/pallas_call | solution.py:185
  62.2 1.2 collective-permute-done.7
  63.4 1.6 %collective-permute-start.8 = (f32[64,128]{1,0:T(8,128)S(1)}, f32[64,128]{1,0:T(8,128)S(1)}, u32[]{:S(2)}, u32[]{:S(2)}) collective-permute-start(f32[64,128]{1,0:T(8,128)S(1)} %multiply_add_fusion.5.mine), channel_id=1, source_target_pairs={{0,2},{1,3},{2,0},{3,1},{4,6},{5,7},{6,4},{7,5},{8,10},{9,11},{10,... | collective-permute-start | bytes 98312 | tf_op jit(solution)/shard_map/ppermute | solution.py:210
  65.0 0.7 concatenate.8.meta
  65.7 1.7 %collective-permute-done.8.other = f32[64,128]{1,0:T(8,128)S(1)} collective-permute-done((f32[64,128]{1,0:T(8,128)S(1)}, f32[64,128]{1,0:T(8,128)S(1)}, u32[]{:S(2)}, u32[]{:S(2)}) %collective-permute-start.8) | collective-permute-done | bytes 32800 | tf_op jit(solution)/shard_map/ppermute | solution.py:210
  67.4 8.3 %target_first.1 = (f32[128,128]{1,0:T(8,128)S(1)}, f32[64,128]{1,0:T(8,128)}) custom-call(s32[546]{0:T(1024)S(1)} %concatenate.8.meta, bf16[64,8192]{1,0:T(8,128)(2,1)S(1)} %bitcast.15, f32[64,128]{1,0:T(8,128)S(1)} %multiply_add_fusion.5.mine, f32[64,128]{1,0:T(8,128)S(1)} %collective-permute-done.8.other, f32[64,128]{1,0:T(8,128)S(1)} %bitcast.30, ...), custom_call_target="tpu_custom_call" | custom-call | tf_op jit(solution)/shard_map/target_first/pallas_call | solution.py:185
  75.8 4.3 %collective-permute-done.9 = f32[128,128]{1,0:T(8,128)S(1)} collective-permute-done((f32[128,128]{1,0:T(8,128)S(1)}, f32[128,128]{1,0:T(8,128)S(1)}, u32[]{:S(2)}, u32[]{:S(2)}) %collective-permute-start.9) | collective-permute-done | bytes 65568 | tf_op jit(solution)/shard_map/ppermute | solution.py:210
  80.1 0.8 collective-permute-start.10
  80.9 3.5 %collective-permute-done.10 = f32[128,128]{1,0:T(8,128)S(1)} collective-permute-done((f32[128,128]{1,0:T(8,128)S(1)}, f32[128,128]{1,0:T(8,128)S(1)}, u32[]{:S(2)}, u32[]{:S(2)}) %collective-permute-start.10) | collective-permute-done | bytes 65568 | tf_op jit(solution)/shard_map/ppermute | solution.py:210
  84.5 3.1 %collective-permute-start.11 = (f32[128,128]{1,0:T(8,128)S(1)}, f32[128,128]{1,0:T(8,128)S(1)}, u32[]{:S(2)}, u32[]{:S(2)}) collective-permute-start(f32[128,128]{1,0:T(8,128)S(1)} %multiply_add_fusion.2.refs_2_), channel_id=1, source_target_pairs={{0,16},{4,20},{8,24},{12,28},{16,0},{20,4},{24,8},{28,12},{1,17},{... | collective-permute-start | bytes 196616 | tf_op jit(solution)/shard_map/ppermute | solution.py:210
  87.6 2.9 %collective-permute-done.11.refs_3_ = f32[128,128]{1,0:T(8,128)S(1)} collective-permute-done((f32[128,128]{1,0:T(8,128)S(1)}, f32[128,128]{1,0:T(8,128)S(1)}, u32[]{:S(2)}, u32[]{:S(2)}) %collective-permute-start.11) | collective-permute-done | bytes 65568 | tf_op jit(solution)/shard_map/ppermute | solution.py:210
  90.5 8.0 %source_second.1 = f32[64,128]{1,0:T(8,128)S(1)} custom-call(s32[546]{0:T(1024)S(1)} %concatenate.9.refs_0_, bf16[64,8192]{1,0:T(8,128)(2,1)S(1)} %bitcast.16, f32[128,128]{1,0:T(8,128)S(1)} %multiply_add_fusion.2.refs_2_, f32[128,128]{1,0:T(8,128)S(1)} %collective-permute-done.11.refs_3_, f32[128,128]{1,0:T(8,128)S(1)} %bitcast.29, ...), custom_call_target="tpu_custom_call" | custom-call | tf_op jit(solution)/shard_map/source_second/pallas_call | solution.py:185
  98.6 1.2 collective-permute-done.12
  99.8 1.6 %collective-permute-start.13 = (f32[64,128]{1,0:T(8,128)S(1)}, f32[64,128]{1,0:T(8,128)S(1)}, u32[]{:S(2)}, u32[]{:S(2)}) collective-permute-start(f32[64,128]{1,0:T(8,128)S(1)} %multiply_add_fusion.4.mine), channel_id=1, source_target_pairs={{0,2},{1,3},{2,0},{3,1},{4,6},{5,7},{6,4},{7,5},{8,10},{9,11},{10,... | collective-permute-start | bytes 98312 | tf_op jit(solution)/shard_map/ppermute | solution.py:210
  101.4 2.4 %collective-permute-done.13.other = f32[64,128]{1,0:T(8,128)S(1)} collective-permute-done((f32[64,128]{1,0:T(8,128)S(1)}, f32[64,128]{1,0:T(8,128)S(1)}, u32[]{:S(2)}, u32[]{:S(2)}) %collective-permute-start.13) | collective-permute-done | bytes 32800 | tf_op jit(solution)/shard_map/ppermute | solution.py:210
  103.8 8.3 %target_second.1 = (f32[128,128]{1,0:T(8,128)S(1)}, f32[64,128]{1,0:T(8,128)}) custom-call(s32[546]{0:T(1024)S(1)} %concatenate.8.meta, bf16[64,8192]{1,0:T(8,128)(2,1)S(1)} %bitcast.17, f32[64,128]{1,0:T(8,128)S(1)} %multiply_add_fusion.4.mine, f32[64,128]{1,0:T(8,128)S(1)} %collective-permute-done.13.other, f32[64,128]{1,0:T(8,128)S(1)} %bitcast.31, ...), custom_call_target="tpu_custom_call" | custom-call | tf_op jit(solution)/shard_map/target_second/pallas_call | solution.py:185
  112.2 4.3 %collective-permute-done.14 = f32[128,128]{1,0:T(8,128)S(1)} collective-permute-done((f32[128,128]{1,0:T(8,128)S(1)}, f32[128,128]{1,0:T(8,128)S(1)}, u32[]{:S(2)}, u32[]{:S(2)}) %collective-permute-start.14) | collective-permute-done | bytes 65568 | tf_op jit(solution)/shard_map/ppermute | solution.py:210
  116.6 4.3 %collective-permute-done.15 = f32[128,128]{1,0:T(8,128)S(1)} collective-permute-done((f32[128,128]{1,0:T(8,128)S(1)}, f32[128,128]{1,0:T(8,128)S(1)}, u32[]{:S(2)}, u32[]{:S(2)}) %collective-permute-start.15) | collective-permute-done | bytes 65568 | tf_op jit(solution)/shard_map/ppermute | solution.py:210
  120.9 2.1 %collective-permute-start.16 = (f32[128,128]{1,0:T(8,128)S(1)}, f32[128,128]{1,0:T(8,128)S(1)}, u32[]{:S(2)}, u32[]{:S(2)}) collective-permute-start(f32[128,128]{1,0:T(8,128)S(1)} %multiply_add_fusion), channel_id=1, source_target_pairs={{0,16},{4,20},{8,24},{12,28},{16,0},{20,4},{24,8},{28,12},{1,17},{... | collective-permute-start | bytes 196616 | tf_op jit(solution)/shard_map/ppermute | solution.py:210
  122.9 3.3 %collective-permute-done.16 = f32[128,128]{1,0:T(8,128)S(1)} collective-permute-done((f32[128,128]{1,0:T(8,128)S(1)}, f32[128,128]{1,0:T(8,128)S(1)}, u32[]{:S(2)}, u32[]{:S(2)}) %collective-permute-start.16) | collective-permute-done | bytes 65568 | tf_op jit(solution)/shard_map/ppermute | solution.py:210
  126.2 0.7 add_bitcast_fusion
  (46 shorter events, 2.1 us)
Async XLA Ops:
  0.6 9.5 %copy-start.8 = (s32[64,1]{0,1:T(1,128)S(1)}, s32[64,1]{0,1:T(1,128)}, u32[]{:S(2)}) copy-start(s32[64,1]{0,1:T(1,128)} %param.13) | copy-start | bytes 772
  0.6 13.2 %collective-permute-start.6 = (bf16[64,2048]{1,0:T(8,128)(2,1)}, bf16[64,2048]{1,0:T(8,128)(2,1)S(1)}, u32[]{:S(2)}, u32[]{:S(2)}) collective-permute-start(bf16[64,2048]{1,0:T(8,128)(2,1)} %bitcast.18), channel_id=1, source_target_pairs={{0,28},{4,0},{8,4},{12,8},{16,12},{20,16},{24,20},{28,24},{1,29},{... | collective-permute-start | bytes 786440 | tf_op jit(solution)/shard_map/ppermute | solution.py:232
  6.7 12.7 %collective-permute-start.5 = (bf16[64,2048]{1,0:T(8,128)(2,1)}, bf16[64,2048]{1,0:T(8,128)(2,1)S(1)}, u32[]{:S(2)}, u32[]{:S(2)}) collective-permute-start(bf16[64,2048]{1,0:T(8,128)(2,1)} %bitcast.19), channel_id=1, source_target_pairs={{0,24},{4,28},{8,0},{12,4},{16,8},{20,12},{24,16},{28,20},{1,25},{... | collective-permute-start | bytes 786440 | tf_op jit(solution)/shard_map/ppermute | solution.py:232
  7.1 17.9 %collective-permute-start.4 = (bf16[64,2048]{1,0:T(8,128)(2,1)}, bf16[64,2048]{1,0:T(8,128)(2,1)S(1)}, u32[]{:S(2)}, u32[]{:S(2)}) collective-permute-start(bf16[64,2048]{1,0:T(8,128)(2,1)} %bitcast.20), channel_id=1, source_target_pairs={{0,20},{4,24},{8,28},{12,0},{16,4},{20,8},{24,12},{28,16},{1,21},{... | collective-permute-start | bytes 786440 | tf_op jit(solution)/shard_map/ppermute | solution.py:232
  7.2 44.5 %collective-permute-start.3 = (bf16[64,2048]{1,0:T(8,128)(2,1)}, bf16[64,2048]{1,0:T(8,128)(2,1)S(1)}, u32[]{:S(2)}, u32[]{:S(2)}) collective-permute-start(bf16[64,2048]{1,0:T(8,128)(2,1)} %bitcast.21), channel_id=1, source_target_pairs={{0,16},{4,20},{8,24},{12,28},{16,0},{20,4},{24,8},{28,12},{1,17},{... | collective-permute-start | bytes 786440 | tf_op jit(solution)/shard_map/ppermute | solution.py:232
  10.1 41.8 %collective-permute-start.2 = (bf16[64,2048]{1,0:T(8,128)(2,1)}, bf16[64,2048]{1,0:T(8,128)(2,1)S(1)}, u32[]{:S(2)}, u32[]{:S(2)}) collective-permute-start(bf16[64,2048]{1,0:T(8,128)(2,1)} %bitcast.22), channel_id=1, source_target_pairs={{0,12},{4,16},{8,20},{12,24},{16,28},{20,0},{24,4},{28,8},{1,13},{... | collective-permute-start | bytes 786440 | tf_op jit(solution)/shard_map/ppermute | solution.py:232
  10.2 0.7 copy-start.7
  10.9 41.0 %copy-start.6 = (f32[16384]{0:T(1024)S(1)}, f32[16384]{0:T(1024)}, u32[]{:S(2)}) copy-start(f32[16384]{0:T(1024)} %param.11) | copy-start | bytes 196612
  13.8 38.1 %collective-permute-start.1 = (bf16[64,2048]{1,0:T(8,128)(2,1)}, bf16[64,2048]{1,0:T(8,128)(2,1)S(1)}, u32[]{:S(2)}, u32[]{:S(2)}) collective-permute-start(bf16[64,2048]{1,0:T(8,128)(2,1)} %bitcast.23), channel_id=1, source_target_pairs={{0,8},{4,12},{8,16},{12,20},{16,24},{20,28},{24,0},{28,4},{1,9},{5... | collective-permute-start | bytes 786440 | tf_op jit(solution)/shard_map/ppermute | solution.py:232
  19.4 32.5 %collective-permute-start = (bf16[64,2048]{1,0:T(8,128)(2,1)}, bf16[64,2048]{1,0:T(8,128)(2,1)S(1)}, u32[]{:S(2)}, u32[]{:S(2)}) collective-permute-start(bf16[64,2048]{1,0:T(8,128)(2,1)} %bitcast.24), channel_id=1, source_target_pairs={{0,4},{4,8},{8,12},{12,16},{16,20},{20,24},{24,28},{28,0},{1,5},{5... | collective-permute-start | bytes 786440 | tf_op jit(solution)/shard_map/ppermute | solution.py:232
  51.9 1.2 copy-start
  53.2 0.9 copy-start.2
  54.1 13.3 %copy-start.1 = (bf16[8192,64]{0,1:T(8,128)(2,1)S(1)}, bf16[8192,64]{0,1:T(8,128)(2,1)}, u32[]{:S(2)}) copy-start(bf16[8192,64]{0,1:T(8,128)(2,1)} %param.7) | copy-start | bytes 3145732
  54.1 13.3 %copy-start.3 = (bf16[2048,64]{0,1:T(8,128)(2,1)S(1)}, bf16[2048,64]{0,1:T(8,128)(2,1)}, u32[]{:S(2)}) copy-start(bf16[2048,64]{0,1:T(8,128)(2,1)} %param.8) | copy-start | bytes 786436
  62.1 1.3 %collective-permute-start.7 = (f32[64,128]{1,0:T(8,128)S(1)}, f32[64,128]{1,0:T(8,128)S(1)}, u32[]{:S(2)}, u32[]{:S(2)}) collective-permute-start(f32[64,128]{1,0:T(8,128)S(1)} %get-tuple-element.7), channel_id=1, source_target_pairs={{0,1},{1,0},{2,3},{3,2},{4,5},{5,4},{6,7},{7,6},{8,9},{9,8},{10,11... | collective-permute-start | bytes 98312 | tf_op jit(solution)/shard_map/ppermute | solution.py:210
  63.4 4.0 %copy-start.5 = (f32[8192]{0:T(1024)S(1)}, f32[8192]{0:T(1024)}, u32[]{:S(2)}) copy-start(f32[8192]{0:T(1024)} %param.9) | copy-start | bytes 98308
  63.4 4.0 %collective-permute-start.8 = (f32[64,128]{1,0:T(8,128)S(1)}, f32[64,128]{1,0:T(8,128)S(1)}, u32[]{:S(2)}, u32[]{:S(2)}) collective-permute-start(f32[64,128]{1,0:T(8,128)S(1)} %multiply_add_fusion.5.mine), channel_id=1, source_target_pairs={{0,2},{1,3},{2,0},{3,1},{4,6},{5,7},{6,4},{7,5},{8,10},{9,11},{10,... | collective-permute-start | bytes 98312 | tf_op jit(solution)/shard_map/ppermute | solution.py:210
  75.7 4.3 %collective-permute-start.9 = (f32[128,128]{1,0:T(8,128)S(1)}, f32[128,128]{1,0:T(8,128)S(1)}, u32[]{:S(2)}, u32[]{:S(2)}) collective-permute-start(f32[128,128]{1,0:T(8,128)S(1)} %get-tuple-element.8), channel_id=1, source_target_pairs={{0,4},{4,0},{8,12},{12,8},{16,20},{20,16},{24,28},{28,24},{1,5},{5... | collective-permute-start | bytes 196616 | tf_op jit(solution)/shard_map/ppermute | solution.py:210
  80.1 10.5 %copy-start.4 = (f32[16384]{0:T(1024)S(1)}, f32[16384]{0:T(1024)}, u32[]{:S(2)}) copy-start(f32[16384]{0:T(1024)} %param.10) | copy-start | bytes 196612
  80.1 4.3 %collective-permute-start.10 = (f32[128,128]{1,0:T(8,128)S(1)}, f32[128,128]{1,0:T(8,128)S(1)}, u32[]{:S(2)}, u32[]{:S(2)}) collective-permute-start(f32[128,128]{1,0:T(8,128)S(1)} %multiply_add_fusion.3), channel_id=1, source_target_pairs={{0,8},{4,12},{8,0},{12,4},{16,24},{20,28},{24,16},{28,20},{1,9},{5... | collective-permute-start | bytes 196616 | tf_op jit(solution)/shard_map/ppermute | solution.py:210
  84.5 6.1 %collective-permute-start.11 = (f32[128,128]{1,0:T(8,128)S(1)}, f32[128,128]{1,0:T(8,128)S(1)}, u32[]{:S(2)}, u32[]{:S(2)}) collective-permute-start(f32[128,128]{1,0:T(8,128)S(1)} %multiply_add_fusion.2.refs_2_), channel_id=1, source_target_pairs={{0,16},{4,20},{8,24},{12,28},{16,0},{20,4},{24,8},{28,12},{1,17},{... | collective-permute-start | bytes 196616 | tf_op jit(solution)/shard_map/ppermute | solution.py:210
  98.5 1.3 %collective-permute-start.12 = (f32[64,128]{1,0:T(8,128)S(1)}, f32[64,128]{1,0:T(8,128)S(1)}, u32[]{:S(2)}, u32[]{:S(2)}) collective-permute-start(f32[64,128]{1,0:T(8,128)S(1)} %source_second.1), channel_id=1, source_target_pairs={{0,1},{1,0},{2,3},{3,2},{4,5},{5,4},{6,7},{7,6},{8,9},{9,8},{10,11... | collective-permute-start | bytes 98312 | tf_op jit(solution)/shard_map/ppermute | solution.py:210
  99.8 4.0 %collective-permute-start.13 = (f32[64,128]{1,0:T(8,128)S(1)}, f32[64,128]{1,0:T(8,128)S(1)}, u32[]{:S(2)}, u32[]{:S(2)}) collective-permute-start(f32[64,128]{1,0:T(8,128)S(1)} %multiply_add_fusion.4.mine), channel_id=1, source_target_pairs={{0,2},{1,3},{2,0},{3,1},{4,6},{5,7},{6,4},{7,5},{8,10},{9,11},{10,... | collective-permute-start | bytes 98312 | tf_op jit(solution)/shard_map/ppermute | solution.py:210
  112.1 4.3 %collective-permute-start.14 = (f32[128,128]{1,0:T(8,128)S(1)}, f32[128,128]{1,0:T(8,128)S(1)}, u32[]{:S(2)}, u32[]{:S(2)}) collective-permute-start(f32[128,128]{1,0:T(8,128)S(1)} %get-tuple-element.11), channel_id=1, source_target_pairs={{0,4},{4,0},{8,12},{12,8},{16,20},{20,16},{24,28},{28,24},{1,5},{5... | collective-permute-start | bytes 196616 | tf_op jit(solution)/shard_map/ppermute | solution.py:210
  116.5 4.3 %collective-permute-start.15 = (f32[128,128]{1,0:T(8,128)S(1)}, f32[128,128]{1,0:T(8,128)S(1)}, u32[]{:S(2)}, u32[]{:S(2)}) collective-permute-start(f32[128,128]{1,0:T(8,128)S(1)} %multiply_add_fusion.1), channel_id=1, source_target_pairs={{0,8},{4,12},{8,0},{12,4},{16,24},{20,28},{24,16},{28,20},{1,9},{5... | collective-permute-start | bytes 196616 | tf_op jit(solution)/shard_map/ppermute | solution.py:210
  120.9 5.4 %collective-permute-start.16 = (f32[128,128]{1,0:T(8,128)S(1)}, f32[128,128]{1,0:T(8,128)S(1)}, u32[]{:S(2)}, u32[]{:S(2)}) collective-permute-start(f32[128,128]{1,0:T(8,128)S(1)} %multiply_add_fusion), channel_id=1, source_target_pairs={{0,16},{4,20},{8,24},{12,28},{16,0},{20,4},{24,8},{28,12},{1,17},{... | collective-permute-start | bytes 196616 | tf_op jit(solution)/shard_map/ppermute | solution.py:210

commit v3 on v2

v3 whole, which is shorter than its diff:
```python
import functools

import jax
import jax.numpy as jnp
from jax import lax
from jax.experimental import pallas as pl
from jax.experimental.pallas import tpu as pltpu
from jax.sharding import PartitionSpec as P

BLOCK = 128
eps = 0.05
scale = 1.4426950408889634 / eps
unit = eps * 0.6931471805599453
floor = -1e30
group = 8
turn = 2 * group
pad = 2 * turn


def merge(first, second):
    peak = jnp.maximum(first, second)
    gap = jnp.minimum(first, second) - peak
    return peak + unit * jnp.log2(1.0 + jnp.exp2(gap * scale))


def squares(block):
    wide = block.astype(jnp.float32)
    return jnp.sum(wide * wide, axis=0, keepdims=True)


def split_rows(pot):
    first = pot.astype(jnp.bfloat16).astype(jnp.float32)
    rest = pot - first
    second = rest.astype(jnp.bfloat16).astype(jnp.float32)
    third = rest - second
    rows = lax.broadcasted_iota(jnp.int32, (64, BLOCK), 0)
    out = jnp.where(rows == 0, first, jnp.where(rows == 1, second, jnp.where(rows == 2, third, 0.0)))
    return out.astype(jnp.bfloat16)


def one_rows():
    rows = lax.broadcasted_iota(jnp.int32, (64, BLOCK), 0)
    return jnp.where(rows < 3, 1.0, 0.0).astype(jnp.bfloat16)


def fill(count, step):
    def body(i, _):
        for k in range(16):
            step(i * 16 + k)
        return 0

    lax.fori_loop(0, count // 16, body, 0)


def tiles_lse(meta, slots, lhs, rhs, even, odd, peaks, sums, top, tot, out):
    turns = (meta[0] + turn - 1) // turn

    def dots(into, start):
        for k in range(group):
            a, b = meta[1 + start + k], meta[1 + slots + start + k]
            into[k] = jnp.dot(lhs[a], rhs[b], preferred_element_type=jnp.float32)

    def reduce(held, start):
        for k in range(group):
            z = held[k].reshape(BLOCK // 8, 8, BLOCK)
            peak = jnp.max(z, axis=0)
            peaks[start + k] = peak
            sums[start + k] = jnp.sum(jnp.exp2((z - peak) * scale), axis=0)

    def tile_step(i, _):
        start = i * turn
        dots(odd, start + group)
        reduce(even, start)
        dots(even, start + turn)
        reduce(odd, start + group)
        return 0

    dots(even, 0)
    lax.fori_loop(0, turns, tile_step, 0)
    top[...] = jnp.full(top.shape, floor, jnp.float32)
    tot[...] = jnp.full(tot.shape, 0.125, jnp.float32)

    def peak_step(i, carry):
        last, run = carry
        for k in range(turn):
            p = i * turn + k
            b = meta[1 + slots + p]
            run = jnp.where(b == last, jnp.maximum(run, peaks[p]), peaks[p])
            top[b] = run
            last = b
        return last, run

    zero = jnp.zeros((8, BLOCK), jnp.float32)
    lax.fori_loop(0, turns, peak_step, (jnp.int32(-1), zero))
    top[...] = jnp.broadcast_to(jnp.max(top[...], axis=1, keepdims=True), top.shape)

    def sum_step(i, carry):
        last, run = carry
        for k in range(turn):
            p = i * turn + k
            b = meta[1 + slots + p]
            part = sums[p] * jnp.exp2((peaks[p] - top[b]) * scale)
            run = jnp.where(b == last, run + part, part)
            tot[b] = run
            last = b
        return last, run

    lax.fori_loop(0, turns, sum_step, (jnp.int32(-1), zero))
    blocks = out.shape[0]
    lse = top[:, 0, :] + unit * jnp.log2(jnp.sum(tot[...], axis=1))
    out[...] = lse[:blocks]


def load_parts(parts, places, held, sems):
    copies = []
    for k, part in enumerate(parts):
        copies.append(pltpu.make_async_copy(part, held.at[places[k]], sems.at[k]))
        copies[-1].start()
    return copies


def block_of(held, i):
    per = held.shape[2] // BLOCK
    return held[i // per, :, pl.ds(pl.multiple_of(lax.rem(i, per) * BLOCK, BLOCK), BLOCK)]


def half_kernel(first, slots, n_src, n_tgt, source_side, *refs):
    (meta, places), refs = refs[:2], refs[2:]
    if first:
        (pot_in,), refs = refs[:1], refs[1:]
    else:
        (mine, other, mass), refs = refs[:3], refs[3:]
    srcs, refs = refs[:n_src], refs[n_src:]
    tgts, refs = refs[:n_tgt], refs[n_tgt:]
    (out, extra), refs = refs[:2], refs[2:]
    xs, ys, xsem, ysem, lhs, rhs, even, odd, peaks, sums, top, tot = refs
    half = xs.shape[2]
    pieces = [srcs[0].at[:, :half], srcs[0].at[:, half:]] + list(srcs[1:])
    x_copies = load_parts(pieces, [places[k] for k in range(n_src + 1)], xs, xsem)
    y_copies = load_parts(tgts, [places[n_src + 1 + k] for k in range(n_tgt)], ys, ysem)
    ones = one_rows()
    if source_side:
        a_held, a_copies, b_held, b_copies = ys, y_copies, xs, x_copies
    else:
        a_held, a_copies, b_held, b_copies = xs, x_copies, ys, y_copies

    def fill_rhs(b):
        rhs[b, :64] = block_of(b_held, b)
        rhs[b, 64:] = ones

    def fill_lhs(a):
        block = block_of(a_held, a)
        if first:
            sq = squares(block)
            extra[pl.ds(a, 1), :] = sq
            pot = pot_in[pl.ds(a, 1), :] - 0.5 * sq
        else:
            lse = merge(mine[pl.ds(a, 1), :], other[pl.ds(a, 1), :])
            pot = unit * jnp.log2(mass[pl.ds(a, 1), :]) - lse
            extra[pl.ds(a, 1), :] = pot
        lhs[a] = jnp.concatenate([block, split_rows(pot)], axis=0).T

    for copy in b_copies:
        copy.wait()
    fill(rhs.shape[0] - 1, fill_rhs)
    for copy in a_copies:
        copy.wait()
    fill(lhs.shape[0], fill_lhs)
    tiles_lse(meta, slots, lhs, rhs, even, odd, peaks, sums, top, tot, out)


def half_pass(source_side, meta, places, dense, srcs, tgts, sources, targets, slots, name):
    blocks_a, blocks_b = (targets, sources) if source_side else (sources, targets)
    vmem = pl.BlockSpec(memory_space=pltpu.VMEM)
    n_src, n_tgt = len(srcs), len(tgts)
    half = srcs[1].shape[1]
    shape = jax.ShapeDtypeStruct
    return pl.pallas_call(
        functools.partial(half_kernel, len(dense) == 1, slots + pad, n_src, n_tgt, source_side),
        out_shape=[shape((blocks_b, BLOCK), jnp.float32), shape((blocks_a, BLOCK), jnp.float32)],
        in_specs=[pl.BlockSpec(memory_space=pltpu.SMEM)] * 2
        + [vmem] * len(dense)
        + [pl.BlockSpec(memory_space=pl.ANY)] * (n_src + n_tgt),
        out_specs=[vmem, vmem],
        scratch_shapes=[
            pltpu.VMEM((n_src + 1, 64, half), jnp.bfloat16),
            pltpu.VMEM((n_tgt,) + tgts[0].shape, jnp.bfloat16),
            pltpu.SemaphoreType.DMA((n_src + 1,)),
            pltpu.SemaphoreType.DMA((n_tgt,)),
            pltpu.VMEM((blocks_a, BLOCK, BLOCK), jnp.bfloat16),
            pltpu.VMEM((blocks_b + 1, BLOCK, BLOCK), jnp.bfloat16),
            pltpu.VMEM((group, BLOCK, BLOCK), jnp.float32),
            pltpu.VMEM((group, BLOCK, BLOCK), jnp.float32),
            pltpu.VMEM((slots + turn, 8, BLOCK), jnp.float32),
            pltpu.VMEM((slots + turn, 8, BLOCK), jnp.float32),
            pltpu.VMEM((blocks_b + 1, 8, BLOCK), jnp.float32),
            pltpu.VMEM((blocks_b + 1, 8, BLOCK), jnp.float32),
        ],
        compiler_params=pltpu.CompilerParams(vmem_limit_bytes=48 * 1024 * 1024),
        name=name,
    )(meta, places, *dense, *srcs, *tgts)


def swap(value, axis, n, bit):
    return lax.ppermute(value, axis, [(i, i ^ bit) for i in range(n)])


def exchange(value, hops):
    for k, hop in enumerate(hops):
        other = swap(value, *hop)
        if k + 1 < len(hops):
            value = merge(value, other)
    return value, other


def tile_list(code, alive, parts, after):
    slots = code.shape[0]
    code = jnp.where(alive, code, (1 << 30) + jnp.arange(slots, dtype=jnp.int32))
    rank = jnp.sum((code[None, :] < code[:, None]).astype(jnp.int32), axis=1)
    places = jnp.arange(slots, dtype=jnp.int32)
    hit = (rank[None, :] == places[:, None]) & alive[None, :]
    ordered = jnp.sum(jnp.where(hit, code[None, :] - after, 0), axis=1) + after
    return ordered // parts, ordered % parts


def shards(rows, cols, emb_source, emb_target, source_mass, target_mass, start_potential, support, count):
    row = lax.axis_index("row").astype(jnp.int32)
    side, level = row % 2, row // 2
    core = lax.axis_index("col").astype(jnp.int32) % 2
    levels = rows // 2
    per = emb_target.shape[0] // BLOCK
    own_sources = emb_source.shape[0] // BLOCK
    sources, targets = 2 * own_sources, levels * per

    order = list(range(0, levels, 2)) + list(range(levels - 1 - levels % 2, 0, -2))
    after = {order[k]: order[(k + 1) % levels] for k in range(levels)}
    onward = [(2 * z + s, 2 * after[z] + s) for z in range(levels) for s in range(2)]
    back = [(b, a) for a, b in onward]
    place = jnp.asarray([order.index(z) for z in range(levels)], jnp.int32)[level]
    ring = jnp.asarray(order, jnp.int32)
    tgts, tgt_places = [emb_target.T], [level]
    ahead = behind = tgts[0]
    for step in range(1, levels // 2 + 1):
        ahead = lax.ppermute(ahead, "row", onward)
        tgts.append(ahead)
        tgt_places.append(ring[(place - step) % levels])
        if 2 * step < levels:
            behind = lax.ppermute(behind, "row", back)
            tgts.append(behind)
            tgt_places.append(ring[(place + step) % levels])

    xt = emb_source.T
    half = xt.shape[1] // 2
    part = lax.dynamic_slice(xt, (jnp.int32(0), core * half), (xt.shape[0], half))
    part = swap(part, "row", rows, 1)
    srcs = [xt, part, swap(part, "col", cols, 1)]
    far = 2 - 2 * side
    src_places = [2 * side, 2 * side + 1, far + core, far + 1 - core]
    places = jnp.stack(src_places + tgt_places)

    def both(mine):
        theirs = swap(mine, "row", rows, 1)
        return jnp.concatenate([jnp.where(side == 0, mine, theirs), jnp.where(side == 0, theirs, mine)])

    def of_side(whole):
        return lax.dynamic_index_in_dim(whole.reshape(levels, 2, per, BLOCK), side, 1, False).reshape(targets, BLOCK)

    depth = support.shape[2]
    slots = sources * depth
    named = support.reshape(own_sources, depth)
    named = jnp.where(jnp.arange(depth, dtype=jnp.int32)[None, :] < count, named, -1)
    named = both(named).reshape(slots)
    alive = (named >= 0) & ((named // per) % 2 == side)
    t_ids = (named // (2 * per)) * per + named % per
    s_ids = jnp.arange(slots, dtype=jnp.int32) // depth
    live = jnp.sum(alive.astype(jnp.int32)).reshape(1)
    blank = jnp.zeros((pad,), jnp.int32)
    s_b, s_a = tile_list(s_ids * targets + t_ids, alive, targets, sources * targets)
    t_b, t_a = tile_list(t_ids * sources + s_ids, alive, sources, sources * targets)
    s_meta = jnp.concatenate([live, s_a, blank, s_b, blank + sources])
    t_meta = jnp.concatenate([live, t_a, blank, t_b, blank + targets])
    s_mass = both(source_mass.reshape(own_sources, BLOCK))
    t_mass = of_side(target_mass)

    def sources_pass(dense, name):
        return half_pass(True, s_meta, places, dense, srcs, tgts, sources, targets, slots, name)

    def targets_pass(dense, name):
        return half_pass(False, t_meta, places, dense, srcs, tgts, sources, targets, slots, name)

    col_bits = [1 << k for k in range((cols - 1).bit_length())]
    row_bits = [1 << k for k in range((rows - 1).bit_length())]
    s_hops = [("col", cols, bit) for bit in col_bits] + [("row", rows, 1)]
    t_hops = [("row", rows, bit) for bit in row_bits[1:]]

    lse, ysq = sources_pass([of_side(start_potential)], "source_first")
    lse, _ = targets_pass([*exchange(lse, s_hops), s_mass], "target_first")
    lse, _ = sources_pass([*exchange(lse, t_hops), t_mass], "source_second")
    lse, pot = targets_pass([*exchange(lse, s_hops), s_mass], "target_second")
    second_g = eps * jnp.log(t_mass) - merge(*exchange(lse, t_hops)) + 0.5 * ysq
    other_g = swap(second_g, "row", rows, 1)
    first_g = jnp.where(side == 0, second_g, other_g).reshape(levels, 1, per, BLOCK)
    last_g = jnp.where(side == 0, other_g, second_g).reshape(levels, 1, per, BLOCK)
    second_g = jnp.concatenate([first_g, last_g], axis=1)
    xsq = squares(xt).reshape(own_sources, BLOCK)
    second_f = lax.dynamic_slice(pot, (side * own_sources, jnp.int32(0)), (own_sources, BLOCK)) + 0.5 * xsq
    return second_f.reshape(-1), second_g.reshape(-1)


def solution(mesh):
    in_specs = (
        P("row", None),
        P(("col", "row"), None),
        P("row"),
        P("col"),
        P("col"),
        P("row", "col", None),
        P("row", "col"),
    )
    out_specs = (P("row"), P("col"))
    body = functools.partial(shards, mesh.shape["row"], mesh.shape["col"])
    return jax.shard_map(body, mesh=mesh, in_specs=in_specs, out_specs=out_specs, check_vma=False)
```

time: 127 us -> 109 us (0.86)
  waiting for transfers between devices: 67.9 us -> 35.9 us
  starting transfers between devices: 18.9 us -> 23.7 us
  other arithmetic: 2.12 us -> 4.99 us
  between operations: 0.82 us -> 2.93 us
  Pallas kernels: 32.6 us -> 34.4 us
  local copies, waits for them, and re-layouts: 4.54 us -> 6.09 us
    ppermute x17 -> x18, waiting for transfers between devices: 67.9 us -> 35.9 us  [the longest x15 31 us: swap(): return lax.ppermute(value, axis, [(i, i ^ bit) for i in range(n)])]
    ppermute x17 -> x18, starting transfers between devices: 18.9 us -> 23.7 us  [the longest x15 16.9 us: swap(): return lax.ppermute(value, axis, [(i, i ^ bit) for i in range(n)])]
    unnamed x19 -> x18, local copies, waits for them, and re-layouts: 2.86 us -> 0.05 us
    dynamic_slice x0 -> x5, local copies, waits for them, and re-layouts: none -> 2.35 us  [the longest x1 1.08 us: shards(): lax.dynamic_slice(xt, (jnp.int32(0), core * half), (xt.shape[0], half))]
    another operation x3 -> x1, local copies, waits for them, and re-layouts: 0.01 us -> 2.01 us  [shards(): places = jnp.stack(src_places + tgt_places)]
    pallas_call x4, Pallas kernels: 32.6 us -> 34.4 us  [half_pass(): pl.pallas_call(functools.partial(half_kernel, len(dense) == 1, slots + pa...]
    select_n x0 -> x4, other arithmetic: none -> 1.46 us  [the longest x2 0.77 us: both(): jnp.where(side == 0, mine, theirs)]
  transfers between devices with their start and end apart: 17 -> 18, of which waited for: 15 -> 13; matrix products, arithmetic and copies ran while one was open for 2% -> 9% of each run, Pallas kernels for 0% -> 0%
where the time goes in v3:
time: 109 us; the launch traced here: 108 us
  waiting for transfers between devices  35.9 us (33%)
  Pallas kernels  34.4 us (32%)
  starting transfers between devices  23.7 us (22%)
  local copies, waits for them, and re-layouts  6.09 us (6%)
  other arithmetic  4.99 us (5%)
  between operations  2.93 us (3%)
    pallas_call x4, Pallas kernels, half_pass(): pl.pallas_call(functools.partial(half_kernel, len(dense) == 1, slots + pa...  34.4 us
    ppermute x15, waiting for transfers between devices, swap(): return lax.ppermute(value, axis, [(i, i ^ bit) for i in range(n)])  31 us
    ppermute x15, starting transfers between devices, swap(): return lax.ppermute(value, axis, [(i, i ^ bit) for i in range(n)])  16.9 us
    ppermute x2, starting transfers between devices, shards(): ahead = lax.ppermute(ahead, 'row', onward)  6.78 us
    ppermute x2, waiting for transfers between devices, shards(): ahead = lax.ppermute(ahead, 'row', onward)  4.95 us
  transfers between devices with their start and end apart: 18, of which 13 were waited for; matrix products, arithmetic and copies ran while one was open for 9% of the time, Pallas kernels for 0%

profile of v3, /device:TPU:0, one launch (start us, length us, event | category | flops | bytes accessed | tf_op | source)
XLA Modules:
  0.0 108.0 jit_solution(2106894606235479930)
XLA Ops:
  0.7 4.1 %collective-permute-start.3 = (bf16[64,2048]{1,0:T(8,128)(2,1)}, bf16[64,2048]{1,0:T(8,128)(2,1)S(1)}, u32[]{:S(2)}, u32[]{:S(2)}) collective-permute-start(bf16[64,2048]{1,0:T(8,128)(2,1)} %bitcast.45), channel_id=1, source_target_pairs={{0,16},{4,20},{8,0},{12,4},{16,24},{20,28},{24,8},{28,12},{1,17},{... | collective-permute-start | bytes 786440 | tf_op jit(solution)/shard_map/ppermute | solution.py:244
  4.8 1.1 dynamic-slice_bitcast_fusion
  5.9 1.6 %collective-permute-start.1 = (bf16[64,4096]{1,0:T(8,128)(2,1)S(1)}, bf16[64,4096]{1,0:T(8,128)(2,1)S(1)}, u32[]{:S(2)}, u32[]{:S(2)}) collective-permute-start(bf16[64,4096]{1,0:T(8,128)(2,1)S(1)} %dynamic-slice_bitcast_fusion), channel_id=1, source_target_pairs={{0,4},{4,0},{8,12},{12,8},{16,20},{20,16},{24,28},{28,24},{1,5},{5... | collective-permute-start | bytes 1572872 | tf_op jit(solution)/shard_map/ppermute | solution.py:205
  12.0 2.0 %stack.23.refs_1_ = s32[8]{0:T(128)S(1)} concatenate(s32[1]{0:T(128)} %bitcast.3, s32[1]{0:T(128)} %bitcast.4, s32[1]{0:T(128)} %bitcast.5, s32[1]{0:T(128)} %bitcast.6, s32[1]{0:T(128)} %bitcast.7, s32[1]{0:T(128)} %get-tuple-element.35, s32[1]{0:T(128)} %get-tuple-element.36, s32[1]{0:T(128)} %get-tuple-element.34), dimensions={0} | concatenate | bytes 64 | tf_op jit(solution)/shard_map/stack | solution.py:259
  14.0 5.4 %collective-permute-done = s32[64,4]{0,1:T(4,128)S(1)} collective-permute-done((s32[64,4]{0,1:T(4,128)S(1)}, s32[64,4]{0,1:T(4,128)S(1)}, u32[]{:S(2)}, u32[]{:S(2)}) %collective-permute-start) | collective-permute-done | bytes 1056 | tf_op jit(solution)/shard_map/ppermute | solution.py:205
  21.0 2.7 %collective-permute-start.5 = (bf16[64,2048]{1,0:T(8,128)(2,1)S(1)}, bf16[64,2048]{1,0:T(8,128)(2,1)S(1)}, u32[]{:S(2)}, u32[]{:S(2)}) collective-permute-start(bf16[64,2048]{1,0:T(8,128)(2,1)S(1)} %collective-permute-done.3.refs_7_.refs_9_), channel_id=1, source_target_pairs={{0,16},{4,20},{8,0},{12,4},{16,24},{20,28},{24,8},{28,12},{1,17},{... | collective-permute-start | bytes 786440 | tf_op jit(solution)/shard_map/ppermute | solution.py:244
  24.2 0.7 concatenate.17.refs_0_
  24.9 4.9 %collective-permute-done.5.refs_9_.refs_11_ = bf16[64,2048]{1,0:T(8,128)(2,1)S(1)} collective-permute-done((bf16[64,2048]{1,0:T(8,128)(2,1)S(1)}, bf16[64,2048]{1,0:T(8,128)(2,1)S(1)}, u32[]{:S(2)}, u32[]{:S(2)}) %collective-permute-start.5) | collective-permute-done | bytes 262176 | tf_op jit(solution)/shard_map/ppermute | solution.py:244
  29.9 8.2 %source_first.1 = (f32[128,128]{1,0:T(8,128)S(1)}, f32[64,128]{1,0:T(8,128)S(1)}) custom-call(s32[1089]{0:T(1024)S(1)} %concatenate.17.refs_0_, s32[8]{0:T(128)S(1)} %stack.23.refs_1_, f32[64,128]{1,0:T(8,128)S(1)} %bitcast.52, bf16[64,8192]{1,0:T(8,128)(2,1)S(1)} %bitcast.41, bf16[64,4096]{1,0:T(8,128)(2,1)S(1)} %collective-permute-done.1.refs_4_.refs_6_, ...), custom_call_target="tpu_custom_call" | custom-call | tf_op jit(solution)/shard_map/source_first/pallas_call | solution.py:178
  38.2 1.6 %collective-permute-start.9 = (f32[64,128]{1,0:T(8,128)S(1)}, f32[64,128]{1,0:T(8,128)}, u32[]{:S(2)}, u32[]{:S(2)}) collective-permute-start(f32[64,128]{1,0:T(8,128)S(1)} %bitcast.56), channel_id=1, source_target_pairs={{0,4},{4,0},{8,12},{12,8},{16,20},{20,16},{24,28},{28,24},{1,5},{5... | collective-permute-start | bytes 98312 | tf_op jit(solution)/shard_map/ppermute | solution.py:205
  40.6 1.6 %collective-permute-start.7 = (f32[128,128]{1,0:T(8,128)S(1)}, f32[128,128]{1,0:T(8,128)S(1)}, u32[]{:S(2)}, u32[]{:S(2)}) collective-permute-start(f32[128,128]{1,0:T(8,128)S(1)} %multiply_add_fusion.3), channel_id=1, source_target_pairs={{0,2},{1,3},{2,0},{3,1},{4,6},{5,7},{6,4},{7,5},{8,10},{9,11},{10,... | collective-permute-start | bytes 196616 | tf_op jit(solution)/shard_map/ppermute | solution.py:205
  42.3 0.8 broadcast_select_fusion.3
  43.1 1.8 %collective-permute-done.7 = f32[128,128]{1,0:T(8,128)S(1)} collective-permute-done((f32[128,128]{1,0:T(8,128)S(1)}, f32[128,128]{1,0:T(8,128)S(1)}, u32[]{:S(2)}, u32[]{:S(2)}) %collective-permute-start.7) | collective-permute-done | bytes 65568 | tf_op jit(solution)/shard_map/ppermute | solution.py:205
  45.5 3.8 %collective-permute-done.8.refs_3_ = f32[128,128]{1,0:T(8,128)S(1)} collective-permute-done((f32[128,128]{1,0:T(8,128)S(1)}, f32[128,128]{1,0:T(8,128)S(1)}, u32[]{:S(2)}, u32[]{:S(2)}) %collective-permute-start.8) | collective-permute-done | bytes 65568 | tf_op jit(solution)/shard_map/ppermute | solution.py:205
  49.3 9.0 %target_first.1 = (f32[64,128]{1,0:T(8,128)S(1)}, f32[128,128]{1,0:T(8,128)}) custom-call(s32[1089]{0:T(1024)S(1)} %concatenate.16.refs_0_, s32[8]{0:T(128)S(1)} %stack.23.refs_1_, f32[128,128]{1,0:T(8,128)S(1)} %multiply_add_fusion.2.refs_2_, f32[128,128]{1,0:T(8,128)S(1)} %collective-permute-done.8.refs_3_, f32[128,128]{1,0:T(8,128)S(1)} %pad_maximum_fusion.refs_4_, ...), custom_call_target="tpu_custom_call" | custom-call | tf_op jit(solution)/shard_map/target_first/pallas_call | solution.py:178
  58.3 2.0 %collective-permute-start.10 = (f32[64,128]{1,0:T(8,128)S(1)}, f32[64,128]{1,0:T(8,128)S(1)}, u32[]{:S(2)}, u32[]{:S(2)}) collective-permute-start(f32[64,128]{1,0:T(8,128)S(1)} %get-tuple-element.9), channel_id=1, source_target_pairs={{0,8},{4,12},{8,0},{12,4},{16,24},{20,28},{24,16},{28,20},{1,9},{5... | collective-permute-start | bytes 98312 | tf_op jit(solution)/shard_map/ppermute | solution.py:205
  60.3 2.0 %collective-permute-done.10 = f32[64,128]{1,0:T(8,128)S(1)} collective-permute-done((f32[64,128]{1,0:T(8,128)S(1)}, f32[64,128]{1,0:T(8,128)S(1)}, u32[]{:S(2)}, u32[]{:S(2)}) %collective-permute-start.10) | collective-permute-done | bytes 32800 | tf_op jit(solution)/shard_map/ppermute | solution.py:205
  62.3 2.6 %collective-permute-start.11 = (f32[64,128]{1,0:T(8,128)S(1)}, f32[64,128]{1,0:T(8,128)S(1)}, u32[]{:S(2)}, u32[]{:S(2)}) collective-permute-start(f32[64,128]{1,0:T(8,128)S(1)} %multiply_add_fusion.6.refs_2_), channel_id=1, source_target_pairs={{0,16},{4,20},{8,24},{12,28},{16,0},{20,4},{24,8},{28,12},{1,17},{... | collective-permute-start | bytes 98312 | tf_op jit(solution)/shard_map/ppermute | solution.py:205
  65.0 2.2 %collective-permute-done.11.refs_3_ = f32[64,128]{1,0:T(8,128)S(1)} collective-permute-done((f32[64,128]{1,0:T(8,128)S(1)}, f32[64,128]{1,0:T(8,128)S(1)}, u32[]{:S(2)}, u32[]{:S(2)}) %collective-permute-start.11) | collective-permute-done | bytes 32800 | tf_op jit(solution)/shard_map/ppermute | solution.py:205
  67.2 8.6 %source_second.1 = (f32[128,128]{1,0:T(8,128)S(1)}, f32[64,128]{1,0:T(8,128)}) custom-call(s32[1089]{0:T(1024)S(1)} %concatenate.17.refs_0_, s32[8]{0:T(128)S(1)} %stack.23.refs_1_, f32[64,128]{1,0:T(8,128)S(1)} %multiply_add_fusion.6.refs_2_, f32[64,128]{1,0:T(8,128)S(1)} %collective-permute-done.11.refs_3_, f32[64,128]{1,0:T(8,128)S(1)} %bitcast.51, ...), custom_call_target="tpu_custom_call" | custom-call | tf_op jit(solution)/shard_map/source_second/pallas_call | solution.py:178
  75.9 1.2 %collective-permute-done.12 = f32[128,128]{1,0:T(8,128)S(1)} collective-permute-done((f32[128,128]{1,0:T(8,128)S(1)}, f32[128,128]{1,0:T(8,128)S(1)}, u32[]{:S(2)}, u32[]{:S(2)}) %collective-permute-start.12) | collective-permute-done | bytes 65568 | tf_op jit(solution)/shard_map/ppermute | solution.py:205
  77.2 1.6 %collective-permute-start.13 = (f32[128,128]{1,0:T(8,128)S(1)}, f32[128,128]{1,0:T(8,128)S(1)}, u32[]{:S(2)}, u32[]{:S(2)}) collective-permute-start(f32[128,128]{1,0:T(8,128)S(1)} %multiply_add_fusion.1), channel_id=1, source_target_pairs={{0,2},{1,3},{2,0},{3,1},{4,6},{5,7},{6,4},{7,5},{8,10},{9,11},{10,... | collective-permute-start | bytes 196616 | tf_op jit(solution)/shard_map/ppermute | solution.py:205
  78.8 2.8 %collective-permute-done.13 = f32[128,128]{1,0:T(8,128)S(1)} collective-permute-done((f32[128,128]{1,0:T(8,128)S(1)}, f32[128,128]{1,0:T(8,128)S(1)}, u32[]{:S(2)}, u32[]{:S(2)}) %collective-permute-start.13) | collective-permute-done | bytes 65568 | tf_op jit(solution)/shard_map/ppermute | solution.py:205
  81.6 0.9 collective-permute-start.14
  82.4 3.5 %collective-permute-done.14.refs_3_ = f32[128,128]{1,0:T(8,128)S(1)} collective-permute-done((f32[128,128]{1,0:T(8,128)S(1)}, f32[128,128]{1,0:T(8,128)S(1)}, u32[]{:S(2)}, u32[]{:S(2)}) %collective-permute-start.14) | collective-permute-done | bytes 65568 | tf_op jit(solution)/shard_map/ppermute | solution.py:205
  85.9 8.5 %target_second.1 = (f32[64,128]{1,0:T(8,128)S(1)}, f32[128,128]{1,0:T(8,128)S(1)}) custom-call(s32[1089]{0:T(1024)S(1)} %concatenate.16.refs_0_, s32[8]{0:T(128)S(1)} %stack.23.refs_1_, f32[128,128]{1,0:T(8,128)S(1)} %multiply_add_fusion.refs_2_, f32[128,128]{1,0:T(8,128)S(1)} %collective-permute-done.14.refs_3_, f32[128,128]{1,0:T(8,128)S(1)} %pad_maximum_fusion.refs_4_, ...), custom_call_target="tpu_custom_call" | custom-call | tf_op jit(solution)/shard_map/target_second/pallas_call | solution.py:178
  94.4 1.2 %collective-permute-start.15 = (f32[64,128]{1,0:T(8,128)S(1)}, f32[64,128]{1,0:T(8,128)S(1)}, u32[]{:S(2)}, u32[]{:S(2)}) collective-permute-start(f32[64,128]{1,0:T(8,128)S(1)} %get-tuple-element.12), channel_id=1, source_target_pairs={{0,8},{4,12},{8,0},{12,4},{16,24},{20,28},{24,16},{28,20},{1,9},{5... | collective-permute-start | bytes 98312 | tf_op jit(solution)/shard_map/ppermute | solution.py:205
  95.6 2.8 %collective-permute-done.15 = f32[64,128]{1,0:T(8,128)S(1)} collective-permute-done((f32[64,128]{1,0:T(8,128)S(1)}, f32[64,128]{1,0:T(8,128)S(1)}, u32[]{:S(2)}, u32[]{:S(2)}) %collective-permute-start.15) | collective-permute-done | bytes 32800 | tf_op jit(solution)/shard_map/ppermute | solution.py:205
  98.4 1.8 %collective-permute-start.16 = (f32[64,128]{1,0:T(8,128)S(1)}, f32[64,128]{1,0:T(8,128)S(1)}, u32[]{:S(2)}, u32[]{:S(2)}) collective-permute-start(f32[64,128]{1,0:T(8,128)S(1)} %multiply_add_fusion.5), channel_id=1, source_target_pairs={{0,16},{4,20},{8,24},{12,28},{16,0},{20,4},{24,8},{28,12},{1,17},{... | collective-permute-start | bytes 98312 | tf_op jit(solution)/shard_map/ppermute | solution.py:205
  100.4 2.8 %collective-permute-done.16 = f32[64,128]{1,0:T(8,128)S(1)} collective-permute-done((f32[64,128]{1,0:T(8,128)S(1)}, f32[64,128]{1,0:T(8,128)S(1)}, u32[]{:S(2)}, u32[]{:S(2)}) %collective-permute-start.16) | collective-permute-done | bytes 32800 | tf_op jit(solution)/shard_map/ppermute | solution.py:205
  103.3 0.9 collective-permute-start.17
  104.8 2.5 %collective-permute-done.17 = f32[64,128]{1,0:T(8,128)S(1)} collective-permute-done((f32[64,128]{1,0:T(8,128)S(1)}, f32[64,128]{1,0:T(8,128)S(1)}, u32[]{:S(2)}, u32[]{:S(2)}) %collective-permute-start.17) | collective-permute-done | bytes 32800 | tf_op jit(solution)/shard_map/ppermute | solution.py:205
  (61 shorter events, 8.0 us)
Async XLA Ops:
  0.6 10.6 %copy-start = (f32[16384]{0:T(1024)S(1)}, f32[16384]{0:T(1024)}, u32[]{:S(2)}) copy-start(f32[16384]{0:T(1024)} %param.13) | copy-start | bytes 196612
  0.6 8.0 %copy-start.8 = (s32[4]{0:T(128)S(1)}, s32[4]{0:T(128)}, u32[]{:S(2)}) copy-start(s32[4]{0:T(128)} %constant.233.clone) | copy-start | bytes 52
  0.7 10.7 %copy-start.6 = (s32[4]{0:T(128)S(1)}, s32[4]{0:T(128)}, u32[]{:S(2)}) copy-start(s32[4]{0:T(128)} %constant.234.clone) | copy-start | bytes 52
  0.7 29.2 %copy-start.2 = (bf16[2048,64]{0,1:T(8,128)(2,1)S(1)}, bf16[2048,64]{0,1:T(8,128)(2,1)}, u32[]{:S(2)}) copy-start(bf16[2048,64]{0,1:T(8,128)(2,1)} %param.10) | copy-start | bytes 786436
  0.7 29.2 %copy-start.1 = (bf16[8192,64]{0,1:T(8,128)(2,1)S(1)}, bf16[8192,64]{0,1:T(8,128)(2,1)}, u32[]{:S(2)}) copy-start(bf16[8192,64]{0,1:T(8,128)(2,1)} %param.9) | copy-start | bytes 3145732
  0.7 18.7 %copy-start.7 = (s32[64,1]{0,1:T(1,128)S(1)}, s32[64,1]{0,1:T(1,128)}, u32[]{:S(2)}) copy-start(s32[64,1]{0,1:T(1,128)} %param.15) | copy-start | bytes 772
  0.7 18.7 %copy-start.5 = (s32[64,1,4]{0,2,1:T(4,128)S(1)}, s32[64,1,4]{0,2,1:T(4,128)}, u32[]{:S(2)}) copy-start(s32[64,1,4]{0,2,1:T(4,128)} %param.14) | copy-start | bytes 3076
  0.7 20.2 %collective-permute-start.3 = (bf16[64,2048]{1,0:T(8,128)(2,1)}, bf16[64,2048]{1,0:T(8,128)(2,1)S(1)}, u32[]{:S(2)}, u32[]{:S(2)}) collective-permute-start(bf16[64,2048]{1,0:T(8,128)(2,1)} %bitcast.45), channel_id=1, source_target_pairs={{0,16},{4,20},{8,0},{12,4},{16,24},{20,28},{24,8},{28,12},{1,17},{... | collective-permute-start | bytes 786440 | tf_op jit(solution)/shard_map/ppermute | solution.py:244
  4.8 20.1 %collective-permute-start.4 = (bf16[64,2048]{1,0:T(8,128)(2,1)}, bf16[64,2048]{1,0:T(8,128)(2,1)S(1)}, u32[]{:S(2)}, u32[]{:S(2)}) collective-permute-start(bf16[64,2048]{1,0:T(8,128)(2,1)} %bitcast.46), channel_id=1, source_target_pairs={{16,0},{20,4},{0,8},{4,12},{24,16},{28,20},{8,24},{12,28},{17,1},{... | collective-permute-start | bytes 786440 | tf_op jit(solution)/shard_map/ppermute | solution.py:248
  5.9 14.7 %collective-permute-start.1 = (bf16[64,4096]{1,0:T(8,128)(2,1)S(1)}, bf16[64,4096]{1,0:T(8,128)(2,1)S(1)}, u32[]{:S(2)}, u32[]{:S(2)}) collective-permute-start(bf16[64,4096]{1,0:T(8,128)(2,1)S(1)} %dynamic-slice_bitcast_fusion), channel_id=1, source_target_pairs={{0,4},{4,0},{8,12},{12,8},{16,20},{20,16},{24,28},{28,24},{1,5},{5... | collective-permute-start | bytes 1572872 | tf_op jit(solution)/shard_map/ppermute | solution.py:205
  8.2 11.2 %collective-permute-start = (s32[64,4]{0,1:T(4,128)S(1)}, s32[64,4]{0,1:T(4,128)S(1)}, u32[]{:S(2)}, u32[]{:S(2)}) collective-permute-start(s32[64,4]{0,1:T(4,128)S(1)} %bitcast_select_fusion), channel_id=1, source_target_pairs={{0,4},{4,0},{8,12},{12,8},{16,20},{20,16},{24,28},{28,24},{1,5},{5... | collective-permute-start | bytes 3080 | tf_op jit(solution)/shard_map/ppermute | solution.py:205
  20.6 9.3 %collective-permute-start.2 = (bf16[64,4096]{1,0:T(8,128)(2,1)S(1)}, bf16[64,4096]{1,0:T(8,128)(2,1)S(1)}, u32[]{:S(2)}, u32[]{:S(2)}) collective-permute-start(bf16[64,4096]{1,0:T(8,128)(2,1)S(1)} %collective-permute-done.1.refs_4_.refs_6_), channel_id=1, source_target_pairs={{0,1},{1,0},{2,3},{3,2},{4,5},{5,4},{6,7},{7,6},{8,9},{9,8},{10,11... | collective-permute-start | bytes 1572872 | tf_op jit(solution)/shard_map/ppermute | solution.py:205
  21.0 8.9 %collective-permute-start.5 = (bf16[64,2048]{1,0:T(8,128)(2,1)S(1)}, bf16[64,2048]{1,0:T(8,128)(2,1)S(1)}, u32[]{:S(2)}, u32[]{:S(2)}) collective-permute-start(bf16[64,2048]{1,0:T(8,128)(2,1)S(1)} %collective-permute-done.3.refs_7_.refs_9_), channel_id=1, source_target_pairs={{0,16},{4,20},{8,0},{12,4},{16,24},{20,28},{24,8},{28,12},{1,17},{... | collective-permute-start | bytes 786440 | tf_op jit(solution)/shard_map/ppermute | solution.py:244
  29.9 8.3 %copy-start.3 = (f32[8192]{0:T(1024)S(1)}, f32[8192]{0:T(1024)}, u32[]{:S(2)}) copy-start(f32[8192]{0:T(1024)} %param.11) | copy-start | bytes 98308
  38.1 2.4 %collective-permute-start.6 = (f32[128,128]{1,0:T(8,128)S(1)}, f32[128,128]{1,0:T(8,128)S(1)}, u32[]{:S(2)}, u32[]{:S(2)}) collective-permute-start(f32[128,128]{1,0:T(8,128)S(1)} %get-tuple-element.8), channel_id=1, source_target_pairs={{0,1},{1,0},{2,3},{3,2},{4,5},{5,4},{6,7},{7,6},{8,9},{9,8},{10,11... | collective-permute-start | bytes 196616 | tf_op jit(solution)/shard_map/ppermute | solution.py:205
  38.2 4.1 %collective-permute-start.9 = (f32[64,128]{1,0:T(8,128)S(1)}, f32[64,128]{1,0:T(8,128)}, u32[]{:S(2)}, u32[]{:S(2)}) collective-permute-start(f32[64,128]{1,0:T(8,128)S(1)} %bitcast.56), channel_id=1, source_target_pairs={{0,4},{4,0},{8,12},{12,8},{16,20},{20,16},{24,28},{28,24},{1,5},{5... | collective-permute-start | bytes 98312 | tf_op jit(solution)/shard_map/ppermute | solution.py:205
  40.6 4.3 %collective-permute-start.7 = (f32[128,128]{1,0:T(8,128)S(1)}, f32[128,128]{1,0:T(8,128)S(1)}, u32[]{:S(2)}, u32[]{:S(2)}) collective-permute-start(f32[128,128]{1,0:T(8,128)S(1)} %multiply_add_fusion.3), channel_id=1, source_target_pairs={{0,2},{1,3},{2,0},{3,1},{4,6},{5,7},{6,4},{7,5},{8,10},{9,11},{10,... | collective-permute-start | bytes 196616 | tf_op jit(solution)/shard_map/ppermute | solution.py:205
  44.9 4.3 %collective-permute-start.8 = (f32[128,128]{1,0:T(8,128)S(1)}, f32[128,128]{1,0:T(8,128)S(1)}, u32[]{:S(2)}, u32[]{:S(2)}) collective-permute-start(f32[128,128]{1,0:T(8,128)S(1)} %multiply_add_fusion.2.refs_2_), channel_id=1, source_target_pairs={{0,4},{4,0},{8,12},{12,8},{16,20},{20,16},{24,28},{28,24},{1,5},{5... | collective-permute-start | bytes 196616 | tf_op jit(solution)/shard_map/ppermute | solution.py:205
  45.5 19.4 %copy-start.4 = (f32[16384]{0:T(1024)S(1)}, f32[16384]{0:T(1024)}, u32[]{:S(2)}) copy-start(f32[16384]{0:T(1024)} %param.12) | copy-start | bytes 196612
  58.3 4.0 %collective-permute-start.10 = (f32[64,128]{1,0:T(8,128)S(1)}, f32[64,128]{1,0:T(8,128)S(1)}, u32[]{:S(2)}, u32[]{:S(2)}) collective-permute-start(f32[64,128]{1,0:T(8,128)S(1)} %get-tuple-element.9), channel_id=1, source_target_pairs={{0,8},{4,12},{8,0},{12,4},{16,24},{20,28},{24,16},{28,20},{1,9},{5... | collective-permute-start | bytes 98312 | tf_op jit(solution)/shard_map/ppermute | solution.py:205
  62.3 4.9 %collective-permute-start.11 = (f32[64,128]{1,0:T(8,128)S(1)}, f32[64,128]{1,0:T(8,128)S(1)}, u32[]{:S(2)}, u32[]{:S(2)}) collective-permute-start(f32[64,128]{1,0:T(8,128)S(1)} %multiply_add_fusion.6.refs_2_), channel_id=1, source_target_pairs={{0,16},{4,20},{8,24},{12,28},{16,0},{20,4},{24,8},{28,12},{1,17},{... | collective-permute-start | bytes 98312 | tf_op jit(solution)/shard_map/ppermute | solution.py:205
  75.8 1.3 %collective-permute-start.12 = (f32[128,128]{1,0:T(8,128)S(1)}, f32[128,128]{1,0:T(8,128)S(1)}, u32[]{:S(2)}, u32[]{:S(2)}) collective-permute-start(f32[128,128]{1,0:T(8,128)S(1)} %get-tuple-element.10), channel_id=1, source_target_pairs={{0,1},{1,0},{2,3},{3,2},{4,5},{5,4},{6,7},{7,6},{8,9},{9,8},{10,11... | collective-permute-start | bytes 196616 | tf_op jit(solution)/shard_map/ppermute | solution.py:205
  77.2 4.3 %collective-permute-start.13 = (f32[128,128]{1,0:T(8,128)S(1)}, f32[128,128]{1,0:T(8,128)S(1)}, u32[]{:S(2)}, u32[]{:S(2)}) collective-permute-start(f32[128,128]{1,0:T(8,128)S(1)} %multiply_add_fusion.1), channel_id=1, source_target_pairs={{0,2},{1,3},{2,0},{3,1},{4,6},{5,7},{6,4},{7,5},{8,10},{9,11},{10,... | collective-permute-start | bytes 196616 | tf_op jit(solution)/shard_map/ppermute | solution.py:205
  81.6 4.3 %collective-permute-start.14 = (f32[128,128]{1,0:T(8,128)S(1)}, f32[128,128]{1,0:T(8,128)S(1)}, u32[]{:S(2)}, u32[]{:S(2)}) collective-permute-start(f32[128,128]{1,0:T(8,128)S(1)} %multiply_add_fusion.refs_2_), channel_id=1, source_target_pairs={{0,4},{4,0},{8,12},{12,8},{16,20},{20,16},{24,28},{28,24},{1,5},{5... | collective-permute-start | bytes 196616 | tf_op jit(solution)/shard_map/ppermute | solution.py:205
  94.4 4.0 %collective-permute-start.15 = (f32[64,128]{1,0:T(8,128)S(1)}, f32[64,128]{1,0:T(8,128)S(1)}, u32[]{:S(2)}, u32[]{:S(2)}) collective-permute-start(f32[64,128]{1,0:T(8,128)S(1)} %get-tuple-element.12), channel_id=1, source_target_pairs={{0,8},{4,12},{8,0},{12,4},{16,24},{20,28},{24,16},{28,20},{1,9},{5... | collective-permute-start | bytes 98312 | tf_op jit(solution)/shard_map/ppermute | solution.py:205
  98.4 4.9 %collective-permute-start.16 = (f32[64,128]{1,0:T(8,128)S(1)}, f32[64,128]{1,0:T(8,128)S(1)}, u32[]{:S(2)}, u32[]{:S(2)}) collective-permute-start(f32[64,128]{1,0:T(8,128)S(1)} %multiply_add_fusion.5), channel_id=1, source_target_pairs={{0,16},{4,20},{8,24},{12,28},{16,0},{20,4},{24,8},{28,12},{1,17},{... | collective-permute-start | bytes 98312 | tf_op jit(solution)/shard_map/ppermute | solution.py:205
  103.3 4.0 %collective-permute-start.17 = (f32[64,128]{1,0:T(8,128)S(1)}, f32[64,128]{1,0:T(8,128)S(1)}, u32[]{:S(2)}, u32[]{:S(2)}) collective-permute-start(f32[64,128]{1,0:T(8,128)S(1)} %multiply_add_fusion.4), channel_id=1, source_target_pairs={{0,4},{4,0},{8,12},{12,8},{16,20},{20,16},{24,28},{28,24},{1,5},{5... | collective-permute-start | bytes 98312 | tf_op jit(solution)/shard_map/ppermute | solution.py:205

commit v4 on v3

v4 whole, which is shorter than its diff:
```python
import functools

import jax
import jax.numpy as jnp
from jax import lax
from jax.experimental import pallas as pl
from jax.experimental.pallas import tpu as pltpu
from jax.sharding import PartitionSpec as P

BLOCK = 128
eps = 0.05
scale = 1.4426950408889634 / eps
unit = eps * 0.6931471805599453
floor = -1e30
turn = 16
longest = 64
pad = turn


def merge(first, second, third=None, fourth=None):
    peak = jnp.maximum(first, second)
    if third is not None:
        peak = jnp.maximum(peak, jnp.maximum(third, fourth))
    total = jnp.exp2((first - peak) * scale) + jnp.exp2((second - peak) * scale)
    if third is not None:
        total += jnp.exp2((third - peak) * scale) + jnp.exp2((fourth - peak) * scale)
    return peak + unit * jnp.log2(total)


def squares(block):
    wide = block.astype(jnp.float32)
    return jnp.sum(wide * wide, axis=0, keepdims=True)


def split_rows(pot):
    first = pot.astype(jnp.bfloat16).astype(jnp.float32)
    rest = pot - first
    second = rest.astype(jnp.bfloat16).astype(jnp.float32)
    third = rest - second
    rows = lax.broadcasted_iota(jnp.int32, (16, BLOCK), 0)
    out = jnp.where(rows == 0, first, jnp.where(rows == 1, second, jnp.where(rows == 2, third, 0.0)))
    return out.astype(jnp.bfloat16)


def one_rows():
    rows = lax.broadcasted_iota(jnp.int32, (16, BLOCK), 0)
    return jnp.where(rows < 3, 1.0, 0.0).astype(jnp.bfloat16)


def fill(count, step):
    def body(i, _):
        for k in range(16):
            step(i * 16 + k)
        return 0

    lax.fori_loop(0, count // 16, body, 0)


def tiles_lse(meta, a_at, b_at, lhs, tails, rhs, peaks, sums, top, tot, out):
    turns = (meta[0] + turn - 1) // turn
    ones = one_rows()
    last = rhs.shape[0] - 1

    def tiles(first, count):
        for k in range(count):
            p = first + k
            a, b = meta[a_at + p], meta[b_at + p]
            left = jnp.concatenate([lhs[a], tails[a]], axis=0)
            right = jnp.concatenate([rhs[jnp.minimum(b, last)], ones], axis=0)
            z = lax.dot_general(left, right, (((0,), (0,)), ((), ())), preferred_element_type=jnp.float32)
            z = z.reshape(BLOCK // 8, 8, BLOCK)
            peak = jnp.max(z, axis=0)
            peaks[p] = peak
            sums[p] = jnp.sum(jnp.exp2((z - peak) * scale), axis=0)

    def loop(first, count, size):
        def body(i, _):
            tiles(first + i * size, size)
            return 0

        lax.fori_loop(0, count, body, 0)
        return first + count * size

    many = turns // (longest // turn)
    left_over = turns - many * (longest // turn)
    done = loop(0, many, longest)
    done = loop(done, left_over // 2, 2 * turn)
    loop(done, lax.rem(left_over, 2), turn)
    top[...] = jnp.full(top.shape, floor, jnp.float32)
    tot[...] = jnp.full(tot.shape, 0.125, jnp.float32)

    def peak_step(i, carry):
        last, run = carry
        for k in range(turn):
            p = i * turn + k
            b = meta[b_at + p]
            run = jnp.where(b == last, jnp.maximum(run, peaks[p]), peaks[p])
            top[b] = run
            last = b
        return last, run

    zero = jnp.zeros((8, BLOCK), jnp.float32)
    lax.fori_loop(0, turns, peak_step, (jnp.int32(-1), zero))
    top[...] = jnp.broadcast_to(jnp.max(top[...], axis=1, keepdims=True), top.shape)

    def sum_step(i, carry):
        last, run = carry
        for k in range(turn):
            p = i * turn + k
            b = meta[b_at + p]
            part = sums[p] * jnp.exp2((peaks[p] - top[b]) * scale)
            run = jnp.where(b == last, run + part, part)
            tot[b] = run
            last = b
        return last, run

    lax.fori_loop(0, turns, sum_step, (jnp.int32(-1), zero))
    blocks = out.shape[0]
    lse = top[:, 0, :] + unit * jnp.log2(jnp.sum(tot[...], axis=1))
    out[...] = lse[:blocks]


def load_parts(parts, places, held, sems):
    copies = []
    for k, part in enumerate(parts):
        copies.append(pltpu.make_async_copy(part, held.at[places[k]], sems.at[k]))
        copies[-1].start()
    return copies


def block_of(held, i):
    per = held.shape[2] // BLOCK
    return held[i // per, :, pl.ds(pl.multiple_of(lax.rem(i, per) * BLOCK, BLOCK), BLOCK)]


def first_kernel(a_at, b_at, n_src, n_tgt, meta, places, pot_in, *refs):
    srcs, refs = refs[:n_src], refs[n_src:]
    tgts, refs = refs[:n_tgt], refs[n_tgt:]
    out, ysq, xb, yb, xs, ys, xsem, ysem, tails, peaks, sums, top, tot = refs
    half = xs.shape[2]
    pieces = [srcs[0].at[:, :half], srcs[0].at[:, half:]] + list(srcs[1:])
    x_copies = load_parts(pieces, [places[k] for k in range(n_src + 1)], xs, xsem)
    y_copies = load_parts(tgts, [places[n_src + 1 + k] for k in range(n_tgt)], ys, ysem)

    def fill_x(b):
        xb[b] = block_of(xs, b)

    def fill_y(a):
        block = block_of(ys, a)
        yb[a] = block
        sq = squares(block)
        ysq[pl.ds(a, 1), :] = sq
        tails[a] = split_rows(pot_in[pl.ds(a, 1), :] - 0.5 * sq)

    for copy in x_copies:
        copy.wait()
    fill(xb.shape[0], fill_x)
    for copy in y_copies:
        copy.wait()
    fill(yb.shape[0], fill_y)
    tiles_lse(meta, a_at, b_at, yb, tails, xb, peaks, sums, top, tot, out)


def later_kernel(a_at, b_at, n_parts, meta, *refs):
    parts, refs = refs[:n_parts], refs[n_parts:]
    mass, lhs, rhs, out, pot_out, tails, peaks, sums, top, tot = refs

    def fill_tails(a):
        lse = merge(*[part[pl.ds(a, 1), :] for part in parts])
        pot = unit * jnp.log2(mass[pl.ds(a, 1), :]) - lse
        pot_out[pl.ds(a, 1), :] = pot
        tails[a] = split_rows(pot)

    fill(lhs.shape[0], fill_tails)
    tiles_lse(meta, a_at, b_at, lhs, tails, rhs, peaks, sums, top, tot, out)


vmem = pl.BlockSpec(memory_space=pltpu.VMEM)
smem = pl.BlockSpec(memory_space=pltpu.SMEM)
far_off = pl.BlockSpec(memory_space=pltpu.HBM)


def tile_scratch(blocks_a, blocks_b, slots):
    return [
        pltpu.VMEM((blocks_a, 16, BLOCK), jnp.bfloat16),
        pltpu.VMEM((slots + pad, 8, BLOCK), jnp.float32),
        pltpu.VMEM((slots + pad, 8, BLOCK), jnp.float32),
        pltpu.VMEM((blocks_b + 1, 8, BLOCK), jnp.float32),
        pltpu.VMEM((blocks_b + 1, 8, BLOCK), jnp.float32),
    ]


def first_pass(meta, places, pot, srcs, tgts, sources, targets, slots, name):
    n_src, n_tgt = len(srcs), len(tgts)
    half = srcs[1].shape[1]
    shape = jax.ShapeDtypeStruct
    return pl.pallas_call(
        functools.partial(first_kernel, 1, 1 + slots + pad, n_src, n_tgt),
        out_shape=[
            shape((sources, BLOCK), jnp.float32),
            shape((targets, BLOCK), jnp.float32),
            shape((sources, 64, BLOCK), jnp.bfloat16),
            shape((targets, 64, BLOCK), jnp.bfloat16),
        ],
        in_specs=[smem, smem, vmem] + [far_off] * (n_src + n_tgt),
        out_specs=[vmem] * 4,
        scratch_shapes=[
            pltpu.VMEM((n_src + 1, 64, half), jnp.bfloat16),
            pltpu.VMEM((n_tgt,) + tgts[0].shape, jnp.bfloat16),
            pltpu.SemaphoreType.DMA((n_src + 1,)),
            pltpu.SemaphoreType.DMA((n_tgt,)),
        ]
        + tile_scratch(targets, sources, slots),
        compiler_params=pltpu.CompilerParams(vmem_limit_bytes=32 * 1024 * 1024),
        name=name,
    )(meta, places, pot, *srcs, *tgts)


def later_pass(meta, parts, mass, lhs, rhs, slots, order, name):
    blocks_a, blocks_b = lhs.shape[0], rhs.shape[0]
    shape = jax.ShapeDtypeStruct
    width = slots + pad
    a_at = 1 + 2 * order * width
    return pl.pallas_call(
        functools.partial(later_kernel, a_at, a_at + width, len(parts)),
        out_shape=[shape((blocks_b, BLOCK), jnp.float32), shape((blocks_a, BLOCK), jnp.float32)],
        in_specs=[smem] + [vmem] * (len(parts) + 3),
        out_specs=[vmem, vmem],
        scratch_shapes=tile_scratch(blocks_a, blocks_b, slots),
        compiler_params=pltpu.CompilerParams(vmem_limit_bytes=32 * 1024 * 1024),
        name=name,
    )(meta, *parts, mass, lhs, rhs)


def swap(value, rows, cols, row_bit, col_bit):
    if not col_bit:
        return lax.ppermute(value, "row", [(i, i ^ row_bit) for i in range(rows)])
    if not row_bit:
        return lax.ppermute(value, "col", [(i, i ^ col_bit) for i in range(cols)])
    pairs = [(i * cols + j, (i ^ row_bit) * cols + (j ^ col_bit)) for i in range(rows) for j in range(cols)]
    return lax.ppermute(value, ("row", "col"), pairs)


def exchange(value, hops, swap_by):
    for hop in hops[:-2]:
        value = merge(value, swap_by(value, *hop))
    if len(hops) == 1:
        return [value, swap_by(value, *hops[0])]
    first, second = hops[-2:]
    diagonal = (first[0] | second[0], first[1] | second[1])
    return [value, swap_by(value, *first), swap_by(value, *second), swap_by(value, *diagonal)]


def tile_list(code, alive, parts, after):
    slots = code.shape[0]
    code = jnp.where(alive, code, (1 << 30) + jnp.arange(slots, dtype=jnp.int32))
    rank = jnp.sum((code[None, :] < code[:, None]).astype(jnp.int32), axis=1)
    places = jnp.arange(slots, dtype=jnp.int32)
    hit = (rank[None, :] == places[:, None]) & alive[None, :]
    ordered = jnp.sum(jnp.where(hit, code[None, :] - after, 0), axis=1) + after
    return ordered // parts, ordered % parts


def shards(rows, cols, emb_source, emb_target, source_mass, target_mass, start_potential, support, count):
    row = lax.axis_index("row").astype(jnp.int32)
    side, level = row % 2, row // 2
    core = lax.axis_index("col").astype(jnp.int32) % 2
    levels = rows // 2
    per = emb_target.shape[0] // BLOCK
    own_sources = emb_source.shape[0] // BLOCK
    sources, targets = 2 * own_sources, levels * per

    order = list(range(0, levels, 2)) + list(range(levels - 1 - levels % 2, 0, -2))
    after = {order[k]: order[(k + 1) % levels] for k in range(levels)}
    onward = [(2 * z + s, 2 * after[z] + s) for z in range(levels) for s in range(2)]
    back = [(b, a) for a, b in onward]
    place = jnp.asarray([order.index(z) for z in range(levels)], jnp.int32)[level]
    ring = jnp.asarray(order, jnp.int32)
    tgts, tgt_places = [emb_target.T], [level]
    ahead = behind = tgts[0]
    for step in range(1, levels // 2 + 1):
        ahead = lax.ppermute(ahead, "row", onward)
        tgts.append(ahead)
        tgt_places.append(ring[(place - step) % levels])
        if 2 * step < levels:
            behind = lax.ppermute(behind, "row", back)
            tgts.append(behind)
            tgt_places.append(ring[(place + step) % levels])

    swap_by = lambda value, row_bit, col_bit: swap(value, rows, cols, row_bit, col_bit)
    depth = support.shape[2]
    slots = sources * depth
    named = support.reshape(own_sources, depth)
    named = jnp.where(jnp.arange(depth, dtype=jnp.int32)[None, :] < count, named, -1)
    mine = jnp.concatenate([source_mass.reshape(own_sources, BLOCK), named.astype(jnp.float32)], axis=1)

    xt, mine = lax.optimization_barrier((emb_source.T, mine))
    theirs = swap_by(mine, 1, 0)
    half = xt.shape[1] // 2
    part = lax.dynamic_slice(xt, (jnp.int32(0), core * half), (xt.shape[0], half))
    part = swap_by(part, 1, 0)
    srcs = [xt, part, swap_by(part, 0, 1)]
    far = 2 - 2 * side
    src_places = [2 * side, 2 * side + 1, far + core, far + 1 - core]
    places = jnp.stack(src_places + tgt_places)

    theirs, tgts[1] = lax.optimization_barrier((theirs, tgts[1]))
    pair = jnp.concatenate([jnp.where(side == 0, mine, theirs), jnp.where(side == 0, theirs, mine)])
    s_mass = pair[:, :BLOCK]
    named = pair[:, BLOCK:].astype(jnp.int32).reshape(slots)

    def of_side(whole):
        return lax.dynamic_index_in_dim(whole.reshape(levels, 2, per, BLOCK), side, 1, False).reshape(targets, BLOCK)

    alive = (named >= 0) & ((named // per) % 2 == side)
    t_ids = (named // (2 * per)) * per + named % per
    s_ids = jnp.arange(slots, dtype=jnp.int32) // depth
    live = jnp.sum(alive.astype(jnp.int32)).reshape(1)
    blank = jnp.zeros((pad,), jnp.int32)
    s_b, s_a = tile_list(s_ids * targets + t_ids, alive, targets, sources * targets)
    t_b, t_a = tile_list(t_ids * sources + s_ids, alive, sources, sources * targets)
    meta = jnp.concatenate([live, s_a, blank, s_b, blank + sources, t_a, blank, t_b, blank + targets])
    t_mass = of_side(target_mass)

    col_bits = [1 << k for k in range((cols - 1).bit_length())]
    row_bits = [1 << k for k in range((rows - 1).bit_length())]
    s_hops = [(0, bit) for bit in col_bits] + [(1, 0)]
    t_hops = [(bit, 0) for bit in row_bits[1:]]

    lse, ysq, xb, yb = first_pass(
        meta, places, of_side(start_potential), srcs, tgts, sources, targets, slots, "source_first"
    )
    lse, _ = later_pass(meta, exchange(lse, s_hops, swap_by), s_mass, xb, yb, slots, 1, "target_first")
    lse, _ = later_pass(meta, exchange(lse, t_hops, swap_by), t_mass, yb, xb, slots, 0, "source_second")
    lse, pot = later_pass(meta, exchange(lse, s_hops, swap_by), s_mass, xb, yb, slots, 1, "target_second")

    lse = lse - (eps * jnp.log(t_mass) + 0.5 * ysq)
    for hop in t_hops[:-1]:
        lse = merge(lse, swap_by(lse, *hop))
    last = t_hops[-1][0]
    own = merge(lse, swap_by(lse, last, 0)).reshape(levels, 1, per, BLOCK)
    other = merge(swap_by(lse, 1, 0), swap_by(lse, last | 1, 0)).reshape(levels, 1, per, BLOCK)
    second_g = -jnp.concatenate([jnp.where(side == 0, own, other), jnp.where(side == 0, other, own)], axis=1)
    xsq = squares(xt).reshape(own_sources, BLOCK)
    second_f = lax.dynamic_slice(pot, (side * own_sources, jnp.int32(0)), (own_sources, BLOCK)) + 0.5 * xsq
    return second_f.reshape(-1), second_g.reshape(-1)


def solution(mesh):
    in_specs = (
        P("row", None),
        P(("col", "row"), None),
        P("row"),
        P("col"),
        P("col"),
        P("row", "col", None),
        P("row", "col"),
    )
    out_specs = (P("row"), P("col"))
    body = functools.partial(shards, mesh.shape["row"], mesh.shape["col"])
    return jax.shard_map(body, mesh=mesh, in_specs=in_specs, out_specs=out_specs, check_vma=False)
```

time: 109 us -> 86.6 us (0.79); the launches traced: 108 us -> 86.8 us
  waiting for transfers between devices: 35.9 us -> 22.9 us
  Pallas kernels: 34.4 us -> 24.3 us
  local copies, waits for them, and re-layouts: 6.09 us -> 7.34 us
    pallas_call x4, Pallas kernels: 34.4 us -> 24.3 us  [the longest x3 17.6 us: later_pass(): pl.pallas_call(functools.partial(later_kernel, a_at, a_at + width, len(pa...]
    ppermute x15 -> x18, waiting for transfers between devices: 31 us -> 21.1 us  [the longest x11 14.9 us: swap(): return lax.ppermute(value, 'row', [(i, i ^ row_bit) for i in range(rows)])]
    ppermute x2, starting transfers between devices: 6.78 us -> 2.86 us  [shards(): ahead = lax.ppermute(ahead, 'row', onward)]
    ppermute x2, waiting for transfers between devices: 4.95 us -> 1.84 us  [shards(): ahead = lax.ppermute(ahead, 'row', onward)]
    ppermute x1, starting transfers between devices: 0.01 us -> 3.08 us  [shards(): behind = lax.ppermute(behind, 'row', back)]
    ppermute x15 -> x18, starting transfers between devices: 16.9 us -> 18.7 us  [the longest x11 11.7 us: swap(): return lax.ppermute(value, 'row', [(i, i ^ row_bit) for i in range(rows)])]
    select_n x4 -> x2, other arithmetic: 1.46 us -> 0.06 us  [the longest x1 0.05 us: shards(): jnp.where(side == 0, own, other)]
  transfers between devices with their start and end apart: 18 -> 21, of which waited for: 13 -> 15; matrix products, arithmetic and copies ran while one was open for 9% -> 13% of each run, Pallas kernels for 0% -> 0%
where the time goes in v4:
time: 86.6 us; the launch traced here: 86.8 us
  starting transfers between devices  24.6 us (28%)
  Pallas kernels  24.3 us (28%)
  waiting for transfers between devices  22.9 us (26%)
  local copies, waits for them, and re-layouts  7.34 us (8%)
  other arithmetic  4.98 us (6%)
  between operations  2.55 us (3%)
    pallas_call x3, Pallas kernels, later_pass(): pl.pallas_call(functools.partial(later_kernel, a_at, a_at + width, len(pa...  17.6 us
    ppermute x11, waiting for transfers between devices, swap(): return lax.ppermute(value, 'row', [(i, i ^ row_bit) for i in range(rows)])  14.9 us
    ppermute x11, starting transfers between devices, swap(): return lax.ppermute(value, 'row', [(i, i ^ row_bit) for i in range(rows)])  11.7 us
    pallas_call x1, Pallas kernels, first_pass(): pl.pallas_call(functools.partial(first_kernel, 1, 1 + slots + pad, n_src,...  6.68 us
    ppermute x2, starting transfers between devices, swap(): return lax.ppermute(value, ('row', 'col'), pairs)  4.25 us
    ppermute x2, waiting for transfers between devices, swap(): return lax.ppermute(value, ('row', 'col'), pairs)  3.42 us
    ppermute x1, starting transfers between devices, shards(): behind = lax.ppermute(behind, 'row', back)  3.08 us
    ppermute x2, starting transfers between devices, shards(): ahead = lax.ppermute(ahead, 'row', onward)  2.86 us
  transfers between devices with their start and end apart: 21, of which 15 were waited for; matrix products, arithmetic and copies ran while one was open for 13% of the time, Pallas kernels for 0%

profile of v4, /device:TPU:0, one launch (start us, length us, event | category | flops | bytes accessed | tf_op | source)
XLA Modules:
  0.0 86.8 jit_solution(9680333975050648032)
XLA Ops:
  0.7 3.1 %collective-permute-start.4 = (bf16[64,2048]{1,0:T(8,128)(2,1)}, bf16[64,2048]{1,0:T(8,128)(2,1)S(1)}, u32[]{:S(2)}, u32[]{:S(2)}) collective-permute-start(bf16[64,2048]{1,0:T(8,128)(2,1)} %bitcast.40), channel_id=1, source_target_pairs={{16,0},{20,4},{0,8},{4,12},{24,16},{28,20},{8,24},{12,28},{17,1},{... | collective-permute-start | bytes 786440 | tf_op jit(solution)/shard_map/ppermute | solution.py:286
  3.7 1.1 %collective-permute-start.1 = (bf16[64,2048]{1,0:T(8,128)(2,1)}, bf16[64,2048]{1,0:T(8,128)(2,1)S(1)}, u32[]{:S(2)}, u32[]{:S(2)}) collective-permute-start(bf16[64,2048]{1,0:T(8,128)(2,1)} %bitcast.41), channel_id=1, source_target_pairs={{0,16},{4,20},{8,0},{12,4},{16,24},{20,28},{24,8},{28,12},{1,17},{... | collective-permute-start | bytes 786440 | tf_op jit(solution)/shard_map/ppermute | solution.py:282
  7.1 1.8 %collective-permute-start = (f32[64,132]{1,0:T(8,128)S(1)}, f32[64,132]{1,0:T(8,128)S(1)}, u32[]{:S(2)}, u32[]{:S(2)}) collective-permute-start(f32[64,132]{1,0:T(8,128)S(1)} %pad_maximum_fusion.1), channel_id=1, source_target_pairs={{0,4},{4,0},{8,12},{12,8},{16,20},{20,16},{24,28},{28,24},{1,5},{5... | collective-permute-start | bytes 101384 | tf_op jit(solution)/shard_map/ppermute | solution.py:237
  8.9 1.1 %constant_dynamic-slice_fusion.1 = bf16[64,4096]{1,0:T(8,128)(2,1)S(1)} fusion(bf16[64,8192]{1,0:T(8,128)(2,1)} %bitcast.36, s32[]{:T(128)S(6)} %select_n.314), kind=kLoop, calls=%fused_computation.113 | loop fusion | bytes 1048580 | tf_op jit(solution)/shard_map/dynamic_slice | solution.py:300
  10.3 1.2 %dynamic_slice.25 = s32[1]{0:T(128)} dynamic-slice(s32[4]{0:T(128)} %constant.231.clone, s32[]{:T(128)S(6)} %select_n.306), dynamic_slice_sizes={1} | dynamic-slice | bytes 12 | tf_op jit(solution)/shard_map/dynamic_slice | solution.py:277
  13.3 1.4 %fusion.43 = (s32[1]{0:T(128)}, s32[1]{0:T(128)}, s32[1]{0:T(128)}) fusion(s32[4]{0:T(128)} %constant.232.clone, s32[]{:T(128)S(6)} %select_n.312, s32[]{:T(128)S(6)} %select_n.308, s32[]{:T(128)S(6)} %select_n.310), kind=kLoop, calls=%fused_computation.115 | loop fusion | bytes 36 | tf_op jit(solution)/shard_map/dynamic_slice | solution.py:284
  14.7 2.0 %stack.23.places = s32[8]{0:T(128)S(1)} concatenate(s32[1]{0:T(128)} %bitcast.6, s32[1]{0:T(128)} %bitcast.7, s32[1]{0:T(128)} %bitcast.8, s32[1]{0:T(128)} %bitcast.9, s32[1]{0:T(128)} %bitcast.10, s32[1]{0:T(128)} %get-tuple-element.45, s32[1]{0:T(128)} %get-tuple-element.46, s32[1]{0:T(128)} %get-tuple-element.44), dimensions={0} | concatenate | bytes 64 | tf_op jit(solution)/shard_map/stack | solution.py:305
  17.7 1.8 %collective-permute-start.5 = (bf16[64,2048]{1,0:T(8,128)(2,1)S(1)}, bf16[64,2048]{1,0:T(8,128)(2,1)S(1)}, u32[]{:S(2)}, u32[]{:S(2)}) collective-permute-start(bf16[64,2048]{1,0:T(8,128)(2,1)S(1)} %collective-permute-done.1.refs_4_), channel_id=1, source_target_pairs={{0,16},{4,20},{8,0},{12,4},{16,24},{20,28},{24,8},{28,12},{1,17},{... | collective-permute-start | bytes 786440 | tf_op jit(solution)/shard_map/ppermute | solution.py:282
  19.8 3.1 %collective-permute-done.2.refs_1_ = bf16[64,4096]{1,0:T(8,128)(2,1)S(1)} collective-permute-done((bf16[64,4096]{1,0:T(8,128)(2,1)S(1)}, bf16[64,4096]{1,0:T(8,128)(2,1)S(1)}, u32[]{:S(2)}, u32[]{:S(2)}) %collective-permute-start.2) | collective-permute-done | bytes 524320 | tf_op jit(solution)/shard_map/ppermute | solution.py:237
  24.4 1.6 %collective-permute-done.5.refs_6_ = bf16[64,2048]{1,0:T(8,128)(2,1)S(1)} collective-permute-done((bf16[64,2048]{1,0:T(8,128)(2,1)S(1)}, bf16[64,2048]{1,0:T(8,128)(2,1)S(1)}, u32[]{:S(2)}, u32[]{:S(2)}) %collective-permute-start.5) | collective-permute-done | bytes 262176 | tf_op jit(solution)/shard_map/ppermute | solution.py:282
  26.0 6.7 %source_first.1 = (f32[128,128]{1,0:T(8,128)S(1)}, f32[64,128]{1,0:T(8,128)S(1)}, bf16[128,64,128]{2,1,0:T(8,128)(2,1)S(1)}, bf16[64,64,128]{2,1,0:T(8,128)(2,1)S(1)}) custom-call(s32[2113]{0:T(1024)S(1)} %concatenate.14.meta, s32[8]{0:T(128)S(1)} %stack.23.places, f32[64,128]{1,0:T(8,128)S(1)} %bitcast.43, bf16[64,8192]{1,0:T(8,128)(2,1)S(1)} %bitcast.37, ...), custom_call_target="tpu_custom_call" | custom-call | tf_op jit(solution)/shard_map/source_first/pallas_call | solution.py:197
  32.8 1.2 %collective-permute-done.6 = f32[128,128]{1,0:T(8,128)S(1)} collective-permute-done((f32[128,128]{1,0:T(8,128)S(1)}, f32[128,128]{1,0:T(8,128)S(1)}, u32[]{:S(2)}, u32[]{:S(2)}) %collective-permute-start.6) | collective-permute-done | bytes 65568 | tf_op jit(solution)/shard_map/ppermute | solution.py:239
  34.1 2.6 %collective-permute-start.9 = (f32[128,128]{1,0:T(8,128)S(1)}, f32[128,128]{1,0:T(8,128)S(1)}, u32[]{:S(2)}, u32[]{:S(2)}) collective-permute-start(f32[128,128]{1,0:T(8,128)S(1)} %multiply_add_fusion.1.refs_0_), channel_id=1, source_target_pairs={{0,6},{1,7},{2,4},{3,5},{4,2},{5,3},{6,0},{7,1},{8,14},{9,15},{10,... | collective-permute-start | bytes 196616 | tf_op jit(solution)/shard_map/ppermute | solution.py:241
  37.7 1.7 %collective-permute-done.9.refs_3_ = f32[128,128]{1,0:T(8,128)S(1)} collective-permute-done((f32[128,128]{1,0:T(8,128)S(1)}, f32[128,128]{1,0:T(8,128)S(1)}, u32[]{:S(2)}, u32[]{:S(2)}) %collective-permute-start.9) | collective-permute-done | bytes 65568 | tf_op jit(solution)/shard_map/ppermute | solution.py:241
  39.3 1.6 %collective-permute-done.8.refs_2_ = f32[128,128]{1,0:T(8,128)S(1)} collective-permute-done((f32[128,128]{1,0:T(8,128)S(1)}, f32[128,128]{1,0:T(8,128)S(1)}, u32[]{:S(2)}, u32[]{:S(2)}) %collective-permute-start.8) | collective-permute-done | bytes 65568 | tf_op jit(solution)/shard_map/ppermute | solution.py:237
  40.9 6.1 %target_first.1 = (f32[64,128]{1,0:T(8,128)S(1)}, f32[128,128]{1,0:T(8,128)}) custom-call(s32[2113]{0:T(1024)S(1)} %concatenate.14.meta, f32[128,128]{1,0:T(8,128)S(1)} %multiply_add_fusion.1.refs_0_, f32[128,128]{1,0:T(8,128)S(1)} %collective-permute-done.7.refs_1_, f32[128,128]{1,0:T(8,128)S(1)} %collective-permute-done.8.refs_2_, ...), custom_call_target="tpu_custom_call" | custom-call | tf_op jit(solution)/shard_map/target_first/pallas_call | solution.py:224
  47.1 2.8 %collective-permute-start.12 = (f32[64,128]{1,0:T(8,128)S(1)}, f32[64,128]{1,0:T(8,128)S(1)}, u32[]{:S(2)}, u32[]{:S(2)}) collective-permute-start(f32[64,128]{1,0:T(8,128)S(1)} %get-tuple-element.21.refs_0_), channel_id=1, source_target_pairs={{0,24},{4,28},{8,16},{12,20},{16,8},{20,12},{24,0},{28,4},{1,25},{... | collective-permute-start | bytes 98312 | tf_op jit(solution)/shard_map/ppermute | solution.py:237
  49.9 1.6 %collective-permute-start.10 = (f32[64,128]{1,0:T(8,128)S(1)}, f32[64,128]{1,0:T(8,128)S(1)}, u32[]{:S(2)}, u32[]{:S(2)}) collective-permute-start(f32[64,128]{1,0:T(8,128)S(1)} %get-tuple-element.21.refs_0_), channel_id=1, source_target_pairs={{0,8},{4,12},{8,0},{12,4},{16,24},{20,28},{24,16},{28,20},{1,9},{5... | collective-permute-start | bytes 98312 | tf_op jit(solution)/shard_map/ppermute | solution.py:237
  51.4 1.5 %collective-permute-done.12.refs_3_ = f32[64,128]{1,0:T(8,128)S(1)} collective-permute-done((f32[64,128]{1,0:T(8,128)S(1)}, f32[64,128]{1,0:T(8,128)S(1)}, u32[]{:S(2)}, u32[]{:S(2)}) %collective-permute-start.12) | collective-permute-done | bytes 32800 | tf_op jit(solution)/shard_map/ppermute | solution.py:237
  53.0 1.7 %collective-permute-done.11.refs_2_ = f32[64,128]{1,0:T(8,128)S(1)} collective-permute-done((f32[64,128]{1,0:T(8,128)S(1)}, f32[64,128]{1,0:T(8,128)S(1)}, u32[]{:S(2)}, u32[]{:S(2)}) %collective-permute-start.11) | collective-permute-done | bytes 32800 | tf_op jit(solution)/shard_map/ppermute | solution.py:237
  54.7 5.8 %source_second.1 = (f32[128,128]{1,0:T(8,128)S(1)}, f32[64,128]{1,0:T(8,128)}) custom-call(s32[2113]{0:T(1024)S(1)} %concatenate.14.meta, f32[64,128]{1,0:T(8,128)S(1)} %get-tuple-element.21.refs_0_, f32[64,128]{1,0:T(8,128)S(1)} %collective-permute-done.10.refs_1_, f32[64,128]{1,0:T(8,128)S(1)} %collective-permute-done.11.refs_2_, ...), custom_call_target="tpu_custom_call" | custom-call | tf_op jit(solution)/shard_map/source_second/pallas_call | solution.py:224
  60.4 1.3 %collective-permute-done.13 = f32[128,128]{1,0:T(8,128)S(1)} collective-permute-done((f32[128,128]{1,0:T(8,128)S(1)}, f32[128,128]{1,0:T(8,128)S(1)}, u32[]{:S(2)}, u32[]{:S(2)}) %collective-permute-start.13) | collective-permute-done | bytes 65568 | tf_op jit(solution)/shard_map/ppermute | solution.py:239
  61.7 1.7 %collective-permute-start.16 = (f32[128,128]{1,0:T(8,128)S(1)}, f32[128,128]{1,0:T(8,128)S(1)}, u32[]{:S(2)}, u32[]{:S(2)}) collective-permute-start(f32[128,128]{1,0:T(8,128)S(1)} %multiply_add_fusion.refs_0_), channel_id=1, source_target_pairs={{0,6},{1,7},{2,4},{3,5},{4,2},{5,3},{6,0},{7,1},{8,14},{9,15},{10,... | collective-permute-start | bytes 196616 | tf_op jit(solution)/shard_map/ppermute | solution.py:241
  63.6 1.7 %collective-permute-start.14 = (f32[128,128]{1,0:T(8,128)S(1)}, f32[128,128]{1,0:T(8,128)S(1)}, u32[]{:S(2)}, u32[]{:S(2)}) collective-permute-start(f32[128,128]{1,0:T(8,128)S(1)} %multiply_add_fusion.refs_0_), channel_id=1, source_target_pairs={{0,2},{1,3},{2,0},{3,1},{4,6},{5,7},{6,4},{7,5},{8,10},{9,11},{10,... | collective-permute-start | bytes 196616 | tf_op jit(solution)/shard_map/ppermute | solution.py:239
  65.3 1.7 %collective-permute-done.16.refs_3_ = f32[128,128]{1,0:T(8,128)S(1)} collective-permute-done((f32[128,128]{1,0:T(8,128)S(1)}, f32[128,128]{1,0:T(8,128)S(1)}, u32[]{:S(2)}, u32[]{:S(2)}) %collective-permute-start.16) | collective-permute-done | bytes 65568 | tf_op jit(solution)/shard_map/ppermute | solution.py:241
  67.0 1.2 %collective-permute-done.15.refs_2_ = f32[128,128]{1,0:T(8,128)S(1)} collective-permute-done((f32[128,128]{1,0:T(8,128)S(1)}, f32[128,128]{1,0:T(8,128)S(1)}, u32[]{:S(2)}, u32[]{:S(2)}) %collective-permute-start.15) | collective-permute-done | bytes 65568 | tf_op jit(solution)/shard_map/ppermute | solution.py:237
  68.5 5.8 %target_second.1 = (f32[64,128]{1,0:T(8,128)S(1)}, f32[128,128]{1,0:T(8,128)S(1)}) custom-call(s32[2113]{0:T(1024)S(1)} %concatenate.14.meta, f32[128,128]{1,0:T(8,128)S(1)} %multiply_add_fusion.refs_0_, f32[128,128]{1,0:T(8,128)S(1)} %collective-permute-done.14.refs_1_, f32[128,128]{1,0:T(8,128)S(1)} %collective-permute-done.15.refs_2_, ...), custom_call_target="tpu_custom_call" | custom-call | tf_op jit(solution)/shard_map/target_second/pallas_call | solution.py:224
  75.1 3.1 %collective-permute-done.17 = f32[64,128]{1,0:T(8,128)S(1)} collective-permute-done((f32[64,128]{1,0:T(8,128)S(1)}, f32[64,128]{1,0:T(8,128)S(1)}, u32[]{:S(2)}, u32[]{:S(2)}) %collective-permute-start.17) | collective-permute-done | bytes 32800 | tf_op jit(solution)/shard_map/ppermute | solution.py:237
  78.3 1.3 %collective-permute-start.19 = (f32[64,128]{1,0:T(8,128)S(1)}, f32[64,128]{1,0:T(8,128)S(1)}, u32[]{:S(2)}, u32[]{:S(2)}) collective-permute-start(f32[64,128]{1,0:T(8,128)S(1)} %multiply_add_fusion.4), channel_id=1, source_target_pairs={{0,4},{4,0},{8,12},{12,8},{16,20},{20,16},{24,28},{28,24},{1,5},{5... | collective-permute-start | bytes 98312 | tf_op jit(solution)/shard_map/ppermute | solution.py:237
  79.6 1.7 %collective-permute-start.20 = (f32[64,128]{1,0:T(8,128)S(1)}, f32[64,128]{1,0:T(8,128)S(1)}, u32[]{:S(2)}, u32[]{:S(2)}) collective-permute-start(f32[64,128]{1,0:T(8,128)S(1)} %multiply_add_fusion.4), channel_id=1, source_target_pairs={{0,20},{4,16},{8,28},{12,24},{16,4},{20,0},{24,12},{28,8},{1,21},{... | collective-permute-start | bytes 98312 | tf_op jit(solution)/shard_map/ppermute | solution.py:237
  81.3 1.5 %collective-permute-start.18 = (f32[64,128]{1,0:T(8,128)S(1)}, f32[64,128]{1,0:T(8,128)S(1)}, u32[]{:S(2)}, u32[]{:S(2)}) collective-permute-start(f32[64,128]{1,0:T(8,128)S(1)} %multiply_add_fusion.4), channel_id=1, source_target_pairs={{0,16},{4,20},{8,24},{12,28},{16,0},{20,4},{24,8},{28,12},{1,17},{... | collective-permute-start | bytes 98312 | tf_op jit(solution)/shard_map/ppermute | solution.py:237
  83.4 1.9 %collective-permute-done.20 = f32[64,128]{1,0:T(8,128)S(1)} collective-permute-done((f32[64,128]{1,0:T(8,128)S(1)}, f32[64,128]{1,0:T(8,128)S(1)}, u32[]{:S(2)}, u32[]{:S(2)}) %collective-permute-start.20) | collective-permute-done | bytes 32800 | tf_op jit(solution)/shard_map/ppermute | solution.py:237
  (53 shorter events, 10.0 us)
Async XLA Ops:
  0.6 9.6 %copy-start = (f32[16384]{0:T(1024)S(1)}, f32[16384]{0:T(1024)}, u32[]{:S(2)}) copy-start(f32[16384]{0:T(1024)} %param.13) | copy-start | bytes 196612
  0.6 25.4 %copy-start.2 = (bf16[2048,64]{0,1:T(8,128)(2,1)S(1)}, bf16[2048,64]{0,1:T(8,128)(2,1)}, u32[]{:S(2)}) copy-start(bf16[2048,64]{0,1:T(8,128)(2,1)} %param.10) | copy-start | bytes 786436
  0.7 25.4 %copy-start.1 = (bf16[8192,64]{0,1:T(8,128)(2,1)S(1)}, bf16[8192,64]{0,1:T(8,128)(2,1)}, u32[]{:S(2)}) copy-start(bf16[8192,64]{0,1:T(8,128)(2,1)} %param.9) | copy-start | bytes 3145732
  0.7 23.7 %collective-permute-start.4 = (bf16[64,2048]{1,0:T(8,128)(2,1)}, bf16[64,2048]{1,0:T(8,128)(2,1)S(1)}, u32[]{:S(2)}, u32[]{:S(2)}) collective-permute-start(bf16[64,2048]{1,0:T(8,128)(2,1)} %bitcast.40), channel_id=1, source_target_pairs={{16,0},{20,4},{0,8},{4,12},{24,16},{28,20},{8,24},{12,28},{17,1},{... | collective-permute-start | bytes 786440 | tf_op jit(solution)/shard_map/ppermute | solution.py:286
  3.7 13.1 %collective-permute-start.1 = (bf16[64,2048]{1,0:T(8,128)(2,1)}, bf16[64,2048]{1,0:T(8,128)(2,1)S(1)}, u32[]{:S(2)}, u32[]{:S(2)}) collective-permute-start(bf16[64,2048]{1,0:T(8,128)(2,1)} %bitcast.41), channel_id=1, source_target_pairs={{0,16},{4,20},{8,0},{12,4},{16,24},{20,28},{24,8},{28,12},{1,17},{... | collective-permute-start | bytes 786440 | tf_op jit(solution)/shard_map/ppermute | solution.py:282
  7.1 9.5 %collective-permute-start = (f32[64,132]{1,0:T(8,128)S(1)}, f32[64,132]{1,0:T(8,128)S(1)}, u32[]{:S(2)}, u32[]{:S(2)}) collective-permute-start(f32[64,132]{1,0:T(8,128)S(1)} %pad_maximum_fusion.1), channel_id=1, source_target_pairs={{0,4},{4,0},{8,12},{12,8},{16,20},{20,16},{24,28},{28,24},{1,5},{5... | collective-permute-start | bytes 101384 | tf_op jit(solution)/shard_map/ppermute | solution.py:237
  10.0 12.9 %collective-permute-start.2 = (bf16[64,4096]{1,0:T(8,128)(2,1)S(1)}, bf16[64,4096]{1,0:T(8,128)(2,1)S(1)}, u32[]{:S(2)}, u32[]{:S(2)}) collective-permute-start(bf16[64,4096]{1,0:T(8,128)(2,1)S(1)} %constant_dynamic-slice_fusion.1), channel_id=1, source_target_pairs={{0,4},{4,0},{8,12},{12,8},{16,20},{20,16},{24,28},{28,24},{1,5},{5... | collective-permute-start | bytes 1572872 | tf_op jit(solution)/shard_map/ppermute | solution.py:237
  17.7 8.3 %collective-permute-start.5 = (bf16[64,2048]{1,0:T(8,128)(2,1)S(1)}, bf16[64,2048]{1,0:T(8,128)(2,1)S(1)}, u32[]{:S(2)}, u32[]{:S(2)}) collective-permute-start(bf16[64,2048]{1,0:T(8,128)(2,1)S(1)} %collective-permute-done.1.refs_4_), channel_id=1, source_target_pairs={{0,16},{4,20},{8,0},{12,4},{16,24},{20,28},{24,8},{28,12},{1,17},{... | collective-permute-start | bytes 786440 | tf_op jit(solution)/shard_map/ppermute | solution.py:282
  22.9 3.2 %collective-permute-start.3 = (bf16[64,4096]{1,0:T(8,128)(2,1)S(1)}, bf16[64,4096]{1,0:T(8,128)(2,1)S(1)}, u32[]{:S(2)}, u32[]{:S(2)}) collective-permute-start(bf16[64,4096]{1,0:T(8,128)(2,1)S(1)} %collective-permute-done.2.refs_1_), channel_id=1, source_target_pairs={{0,1},{1,0},{2,3},{3,2},{4,5},{5,4},{6,7},{7,6},{8,9},{9,8},{10,11... | collective-permute-start | bytes 1572872 | tf_op jit(solution)/shard_map/ppermute | solution.py:239
  32.7 18.7 %copy-start.3 = (f32[16384]{0:T(1024)S(1)}, f32[16384]{0:T(1024)}, u32[]{:S(2)}) copy-start(f32[16384]{0:T(1024)} %param.12) | copy-start | bytes 196612
  32.7 1.3 %collective-permute-start.6 = (f32[128,128]{1,0:T(8,128)S(1)}, f32[128,128]{1,0:T(8,128)S(1)}, u32[]{:S(2)}, u32[]{:S(2)}) collective-permute-start(f32[128,128]{1,0:T(8,128)S(1)} %get-tuple-element.18), channel_id=1, source_target_pairs={{0,1},{1,0},{2,3},{3,2},{4,5},{5,4},{6,7},{7,6},{8,9},{9,8},{10,11... | collective-permute-start | bytes 196616 | tf_op jit(solution)/shard_map/ppermute | solution.py:239
  34.1 5.2 %collective-permute-start.9 = (f32[128,128]{1,0:T(8,128)S(1)}, f32[128,128]{1,0:T(8,128)S(1)}, u32[]{:S(2)}, u32[]{:S(2)}) collective-permute-start(f32[128,128]{1,0:T(8,128)S(1)} %multiply_add_fusion.1.refs_0_), channel_id=1, source_target_pairs={{0,6},{1,7},{2,4},{3,5},{4,2},{5,3},{6,0},{7,1},{8,14},{9,15},{10,... | collective-permute-start | bytes 196616 | tf_op jit(solution)/shard_map/ppermute | solution.py:241
  36.7 4.3 %collective-permute-start.8 = (f32[128,128]{1,0:T(8,128)S(1)}, f32[128,128]{1,0:T(8,128)S(1)}, u32[]{:S(2)}, u32[]{:S(2)}) collective-permute-start(f32[128,128]{1,0:T(8,128)S(1)} %multiply_add_fusion.1.refs_0_), channel_id=1, source_target_pairs={{0,4},{4,0},{8,12},{12,8},{16,20},{20,16},{24,28},{28,24},{1,5},{5... | collective-permute-start | bytes 196616 | tf_op jit(solution)/shard_map/ppermute | solution.py:237
  36.7 4.3 %collective-permute-start.7 = (f32[128,128]{1,0:T(8,128)S(1)}, f32[128,128]{1,0:T(8,128)S(1)}, u32[]{:S(2)}, u32[]{:S(2)}) collective-permute-start(f32[128,128]{1,0:T(8,128)S(1)} %multiply_add_fusion.1.refs_0_), channel_id=1, source_target_pairs={{0,2},{1,3},{2,0},{3,1},{4,6},{5,7},{6,4},{7,5},{8,10},{9,11},{10,... | collective-permute-start | bytes 196616 | tf_op jit(solution)/shard_map/ppermute | solution.py:239
  47.1 5.9 %collective-permute-start.12 = (f32[64,128]{1,0:T(8,128)S(1)}, f32[64,128]{1,0:T(8,128)S(1)}, u32[]{:S(2)}, u32[]{:S(2)}) collective-permute-start(f32[64,128]{1,0:T(8,128)S(1)} %get-tuple-element.21.refs_0_), channel_id=1, source_target_pairs={{0,24},{4,28},{8,16},{12,20},{16,8},{20,12},{24,0},{28,4},{1,25},{... | collective-permute-start | bytes 98312 | tf_op jit(solution)/shard_map/ppermute | solution.py:237
  49.9 4.8 %collective-permute-start.11 = (f32[64,128]{1,0:T(8,128)S(1)}, f32[64,128]{1,0:T(8,128)S(1)}, u32[]{:S(2)}, u32[]{:S(2)}) collective-permute-start(f32[64,128]{1,0:T(8,128)S(1)} %get-tuple-element.21.refs_0_), channel_id=1, source_target_pairs={{0,16},{4,20},{8,24},{12,28},{16,0},{20,4},{24,8},{28,12},{1,17},{... | collective-permute-start | bytes 98312 | tf_op jit(solution)/shard_map/ppermute | solution.py:237
  49.9 4.8 %collective-permute-start.10 = (f32[64,128]{1,0:T(8,128)S(1)}, f32[64,128]{1,0:T(8,128)S(1)}, u32[]{:S(2)}, u32[]{:S(2)}) collective-permute-start(f32[64,128]{1,0:T(8,128)S(1)} %get-tuple-element.21.refs_0_), channel_id=1, source_target_pairs={{0,8},{4,12},{8,0},{12,4},{16,24},{20,28},{24,16},{28,20},{1,9},{5... | collective-permute-start | bytes 98312 | tf_op jit(solution)/shard_map/ppermute | solution.py:237
  60.4 1.3 %collective-permute-start.13 = (f32[128,128]{1,0:T(8,128)S(1)}, f32[128,128]{1,0:T(8,128)S(1)}, u32[]{:S(2)}, u32[]{:S(2)}) collective-permute-start(f32[128,128]{1,0:T(8,128)S(1)} %get-tuple-element.22), channel_id=1, source_target_pairs={{0,1},{1,0},{2,3},{3,2},{4,5},{5,4},{6,7},{7,6},{8,9},{9,8},{10,11... | collective-permute-start | bytes 196616 | tf_op jit(solution)/shard_map/ppermute | solution.py:239
  61.7 5.3 %collective-permute-start.16 = (f32[128,128]{1,0:T(8,128)S(1)}, f32[128,128]{1,0:T(8,128)S(1)}, u32[]{:S(2)}, u32[]{:S(2)}) collective-permute-start(f32[128,128]{1,0:T(8,128)S(1)} %multiply_add_fusion.refs_0_), channel_id=1, source_target_pairs={{0,6},{1,7},{2,4},{3,5},{4,2},{5,3},{6,0},{7,1},{8,14},{9,15},{10,... | collective-permute-start | bytes 196616 | tf_op jit(solution)/shard_map/ppermute | solution.py:241
  63.4 4.8 %collective-permute-start.15 = (f32[128,128]{1,0:T(8,128)S(1)}, f32[128,128]{1,0:T(8,128)S(1)}, u32[]{:S(2)}, u32[]{:S(2)}) collective-permute-start(f32[128,128]{1,0:T(8,128)S(1)} %multiply_add_fusion.refs_0_), channel_id=1, source_target_pairs={{0,4},{4,0},{8,12},{12,8},{16,20},{20,16},{24,28},{28,24},{1,5},{5... | collective-permute-start | bytes 196616 | tf_op jit(solution)/shard_map/ppermute | solution.py:237
  63.6 4.9 %collective-permute-start.14 = (f32[128,128]{1,0:T(8,128)S(1)}, f32[128,128]{1,0:T(8,128)S(1)}, u32[]{:S(2)}, u32[]{:S(2)}) collective-permute-start(f32[128,128]{1,0:T(8,128)S(1)} %multiply_add_fusion.refs_0_), channel_id=1, source_target_pairs={{0,2},{1,3},{2,0},{3,1},{4,6},{5,7},{6,4},{7,5},{8,10},{9,11},{10,... | collective-permute-start | bytes 196616 | tf_op jit(solution)/shard_map/ppermute | solution.py:239
  74.3 4.0 %collective-permute-start.17 = (f32[64,128]{1,0:T(8,128)S(1)}, f32[64,128]{1,0:T(8,128)S(1)}, u32[]{:S(2)}, u32[]{:S(2)}) collective-permute-start(f32[64,128]{1,0:T(8,128)S(1)} %add_subtract_fusion), channel_id=1, source_target_pairs={{0,8},{4,12},{8,0},{12,4},{16,24},{20,28},{24,16},{28,20},{1,9},{5... | collective-permute-start | bytes 98312 | tf_op jit(solution)/shard_map/ppermute | solution.py:237
  78.3 5.1 %collective-permute-start.19 = (f32[64,128]{1,0:T(8,128)S(1)}, f32[64,128]{1,0:T(8,128)S(1)}, u32[]{:S(2)}, u32[]{:S(2)}) collective-permute-start(f32[64,128]{1,0:T(8,128)S(1)} %multiply_add_fusion.4), channel_id=1, source_target_pairs={{0,4},{4,0},{8,12},{12,8},{16,20},{20,16},{24,28},{28,24},{1,5},{5... | collective-permute-start | bytes 98312 | tf_op jit(solution)/shard_map/ppermute | solution.py:237
  79.6 5.7 %collective-permute-start.20 = (f32[64,128]{1,0:T(8,128)S(1)}, f32[64,128]{1,0:T(8,128)S(1)}, u32[]{:S(2)}, u32[]{:S(2)}) collective-permute-start(f32[64,128]{1,0:T(8,128)S(1)} %multiply_add_fusion.4), channel_id=1, source_target_pairs={{0,20},{4,16},{8,28},{12,24},{16,4},{20,0},{24,12},{28,8},{1,21},{... | collective-permute-start | bytes 98312 | tf_op jit(solution)/shard_map/ppermute | solution.py:237
  81.3 4.8 %collective-permute-start.18 = (f32[64,128]{1,0:T(8,128)S(1)}, f32[64,128]{1,0:T(8,128)S(1)}, u32[]{:S(2)}, u32[]{:S(2)}) collective-permute-start(f32[64,128]{1,0:T(8,128)S(1)} %multiply_add_fusion.4), channel_id=1, source_target_pairs={{0,16},{4,20},{8,24},{12,28},{16,0},{20,4},{24,8},{28,12},{1,17},{... | collective-permute-start | bytes 98312 | tf_op jit(solution)/shard_map/ppermute | solution.py:237

commit v5 on v4

--- a/solution.py
+++ b/solution.py
@@ -15,6 +15,8 @@
 turn = 16
 longest = 64
 pad = turn
+place_bits = 12
+place = 1 << place_bits
 
 
 def merge(first, second, third=None, fourth=None):
@@ -32,14 +34,16 @@
     return jnp.sum(wide * wide, axis=0, keepdims=True)
 
 
-def split_rows(pot):
+def rows_of(first, count, stride):
+    return pl.ds(pl.multiple_of(first, 8), count) if stride == 1 else pl.ds(first, count, stride)
+
+
+def store_split(tails, i, pot):
     first = pot.astype(jnp.bfloat16).astype(jnp.float32)
     rest = pot - first
     second = rest.astype(jnp.bfloat16).astype(jnp.float32)
-    third = rest - second
-    rows = lax.broadcasted_iota(jnp.int32, (16, BLOCK), 0)
-    out = jnp.where(rows == 0, first, jnp.where(rows == 1, second, jnp.where(rows == 2, third, 0.0)))
-    return out.astype(jnp.bfloat16)
+    for k, part in enumerate((first, second, rest - second)):
+        tails[pl.ds(i * 64 + k, 8, stride=8), :] = part
 
 
 def one_rows():
@@ -56,68 +60,58 @@
     lax.fori_loop(0, count // 16, body, 0)
 
 
-def tiles_lse(meta, a_at, b_at, lhs, tails, rhs, peaks, sums, top, tot, out):
-    turns = (meta[0] + turn - 1) // turn
+def fetch(tiles_in, listed, arrived):
+    return pltpu.make_async_copy(tiles_in, listed, arrived)
+
+
+def tiles_lse(tiles_in, listed, arrived, lhs, tails, rhs, top, tot, out):
     ones = one_rows()
-    last = rhs.shape[0] - 1
-
-    def tiles(first, count):
+    zeros = jnp.zeros((8, BLOCK), jnp.float32)
+    end = rhs.shape[0] - 1
+    top[...] = jnp.full(top.shape, floor, jnp.float32)
+    tot[...] = jnp.full(tot.shape, 0.125, jnp.float32)
+    fetch(tiles_in, listed, arrived).wait()
+    turns = (listed[0] + turn - 1) // turn
+
+    def tiles(first, count, carry):
+        last, run, total = carry
         for k in range(count):
-            p = first + k
-            a, b = meta[a_at + p], meta[b_at + p]
-            left = jnp.concatenate([lhs[a], tails[a]], axis=0)
-            right = jnp.concatenate([rhs[jnp.minimum(b, last)], ones], axis=0)
+            code = listed[1 + first + k]
+            a, b = code & (place - 1), code >> place_bits
+            tail = jnp.concatenate([tails[rows_of(a * 8, 8, 1), :], zeros]).astype(jnp.bfloat16)
+            left = jnp.concatenate([lhs[a], tail], axis=0)
+            right = jnp.concatenate([rhs[jnp.minimum(b, end)], ones], axis=0)
             z = lax.dot_general(left, right, (((0,), (0,)), ((), ())), preferred_element_type=jnp.float32)
             z = z.reshape(BLOCK // 8, 8, BLOCK)
             peak = jnp.max(z, axis=0)
-            peaks[p] = peak
-            sums[p] = jnp.sum(jnp.exp2((z - peak) * scale), axis=0)
-
-    def loop(first, count, size):
-        def body(i, _):
-            tiles(first + i * size, size)
-            return 0
-
-        lax.fori_loop(0, count, body, 0)
-        return first + count * size
+            part = jnp.sum(jnp.exp2((z - peak) * scale), axis=0)
+            same = b == last
+            joint = jnp.where(same, jnp.maximum(run, peak), peak)
+            part = part * jnp.exp2((peak - joint) * scale)
+            total = jnp.where(same, total * jnp.exp2((run - joint) * scale), 0.0) + part
+            top[rows_of(b * 8, 8, 1), :] = joint
+            tot[rows_of(b * 8, 8, 1), :] = total
+            last, run = b, joint
+        return last, run, total
+
+    def loop(first, count, size, carry):
+        return lax.fori_loop(0, count, lambda i, held: tiles(first + i * size, size, held), carry)
 
     many = turns // (longest // turn)
     left_over = turns - many * (longest // turn)
-    done = loop(0, many, longest)
-    done = loop(done, left_over // 2, 2 * turn)
-    loop(done, lax.rem(left_over, 2), turn)
-    top[...] = jnp.full(top.shape, floor, jnp.float32)
-    tot[...] = jnp.full(tot.shape, 0.125, jnp.float32)
-
-    def peak_step(i, carry):
-        last, run = carry
-        for k in range(turn):
-            p = i * turn + k
-            b = meta[b_at + p]
-            run = jnp.where(b == last, jnp.maximum(run, peaks[p]), peaks[p])
-            top[b] = run
-            last = b
-        return last, run
-
-    zero = jnp.zeros((8, BLOCK), jnp.float32)
-    lax.fori_loop(0, turns, peak_step, (jnp.int32(-1), zero))
-    top[...] = jnp.broadcast_to(jnp.max(top[...], axis=1, keepdims=True), top.shape)
-
-    def sum_step(i, carry):
-        last, run = carry
-        for k in range(turn):
-            p = i * turn + k
-            b = meta[b_at + p]
-            part = sums[p] * jnp.exp2((peaks[p] - top[b]) * scale)
-            run = jnp.where(b == last, run + part, part)
-            tot[b] = run
-            last = b
-        return last, run
-
-    lax.fori_loop(0, turns, sum_step, (jnp.int32(-1), zero))
-    blocks = out.shape[0]
-    lse = top[:, 0, :] + unit * jnp.log2(jnp.sum(tot[...], axis=1))
-    out[...] = lse[:blocks]
+    carry = loop(0, many, longest, (jnp.int32(-1), zeros, zeros))
+    done = many * longest
+    carry = loop(done, left_over // 2, 2 * turn, carry)
+    done += (left_over // 2) * 2 * turn
+    loop(done, lax.rem(left_over, 2), turn, carry)
+
+    for i in range(out.shape[0] // 8):
+        peaks = [top[pl.ds(i * 64 + k, 8, stride=8), :] for k in range(8)]
+        peak = functools.reduce(jnp.maximum, peaks)
+        total = 0.0
+        for k in range(8):
+            total += tot[pl.ds(i * 64 + k, 8, stride=8), :] * jnp.exp2((peaks[k] - peak) * scale)
+        out[i * 8 : i * 8 + 8, :] = peak + unit * jnp.log2(total)
 
 
 def load_parts(parts, places, held, sems):
@@ -133,10 +127,11 @@
     return held[i // per, :, pl.ds(pl.multiple_of(lax.rem(i, per) * BLOCK, BLOCK), BLOCK)]
 
 
-def first_kernel(a_at, b_at, n_src, n_tgt, meta, places, pot_in, *refs):
+def first_kernel(n_src, n_tgt, tiles_in, places, pot_in, *refs):
     srcs, refs = refs[:n_src], refs[n_src:]
     tgts, refs = refs[:n_tgt], refs[n_tgt:]
-    out, ysq, xb, yb, xs, ys, xsem, ysem, tails, peaks, sums, top, tot = refs
+    out, ysq, xb, yb, xs, ys, xsem, ysem, listed, arrived, tails, top, tot = refs
+    fetch(tiles_in, listed, arrived).start()
     half = xs.shape[2]
     pieces = [srcs[0].at[:, :half], srcs[0].at[:, half:]] + list(srcs[1:])
     x_copies = load_parts(pieces, [places[k] for k in range(n_src + 1)], xs, xsem)
@@ -150,7 +145,6 @@
         yb[a] = block
         sq = squares(block)
         ysq[pl.ds(a, 1), :] = sq
-        tails[a] = split_rows(pot_in[pl.ds(a, 1), :] - 0.5 * sq)
 
     for copy in x_copies:
         copy.wait()
@@ -158,21 +152,28 @@
     for copy in y_copies:
         copy.wait()
     fill(yb.shape[0], fill_y)
-    tiles_lse(meta, a_at, b_at, yb, tails, xb, peaks, sums, top, tot, out)
-
-
-def later_kernel(a_at, b_at, n_parts, meta, *refs):
+    tails[...] = jnp.zeros(tails.shape, jnp.float32)
+    for i in range(yb.shape[0] // 8):
+        rows = slice(i * 8, i * 8 + 8)
+        store_split(tails, i, pot_in[rows, :] - 0.5 * ysq[rows, :])
+    tiles_lse(tiles_in, listed, arrived, yb, tails, xb, top, tot, out)
+
+
+def later_kernel(n_parts, keep, tiles_in, *refs):
     parts, refs = refs[:n_parts], refs[n_parts:]
-    mass, lhs, rhs, out, pot_out, tails, peaks, sums, top, tot = refs
-
-    def fill_tails(a):
-        lse = merge(*[part[pl.ds(a, 1), :] for part in parts])
-        pot = unit * jnp.log2(mass[pl.ds(a, 1), :]) - lse
-        pot_out[pl.ds(a, 1), :] = pot
-        tails[a] = split_rows(pot)
-
-    fill(lhs.shape[0], fill_tails)
-    tiles_lse(meta, a_at, b_at, lhs, tails, rhs, peaks, sums, top, tot, out)
+    (mass, lhs, rhs, out), refs = refs[:4], refs[4:]
+    if keep:
+        (pot_out,), refs = refs[:1], refs[1:]
+    listed, arrived, tails, top, tot = refs
+    fetch(tiles_in, listed, arrived).start()
+    tails[...] = jnp.zeros(tails.shape, jnp.float32)
+    for i in range(lhs.shape[0] // 8):
+        rows = slice(i * 8, i * 8 + 8)
+        pot = unit * jnp.log2(mass[rows, :]) - merge(*[part[rows, :] for part in parts])
+        if keep:
+            pot_out[rows, :] = pot
+        store_split(tails, i, pot)
+    tiles_lse(tiles_in, listed, arrived, lhs, tails, rhs, top, tot, out)
 
 
 vmem = pl.BlockSpec(memory_space=pltpu.VMEM)
@@ -180,29 +181,29 @@
 far_off = pl.BlockSpec(memory_space=pltpu.HBM)
 
 
-def tile_scratch(blocks_a, blocks_b, slots):
+def tile_scratch(blocks_a, blocks_b, listed):
     return [
-        pltpu.VMEM((blocks_a, 16, BLOCK), jnp.bfloat16),
-        pltpu.VMEM((slots + pad, 8, BLOCK), jnp.float32),
-        pltpu.VMEM((slots + pad, 8, BLOCK), jnp.float32),
-        pltpu.VMEM((blocks_b + 1, 8, BLOCK), jnp.float32),
-        pltpu.VMEM((blocks_b + 1, 8, BLOCK), jnp.float32),
+        pltpu.SMEM((listed,), jnp.int32),
+        pltpu.SemaphoreType.DMA,
+        pltpu.VMEM((blocks_a * 8, BLOCK), jnp.float32),
+        pltpu.VMEM((blocks_b * 8 + 8, BLOCK), jnp.float32),
+        pltpu.VMEM((blocks_b * 8 + 8, BLOCK), jnp.float32),
     ]
 
 
-def first_pass(meta, places, pot, srcs, tgts, sources, targets, slots, name):
+def first_pass(listed, places, pot, srcs, tgts, sources, targets, name):
     n_src, n_tgt = len(srcs), len(tgts)
     half = srcs[1].shape[1]
     shape = jax.ShapeDtypeStruct
     return pl.pallas_call(
-        functools.partial(first_kernel, 1, 1 + slots + pad, n_src, n_tgt),
+        functools.partial(first_kernel, n_src, n_tgt),
         out_shape=[
             shape((sources, BLOCK), jnp.float32),
             shape((targets, BLOCK), jnp.float32),
             shape((sources, 64, BLOCK), jnp.bfloat16),
             shape((targets, 64, BLOCK), jnp.bfloat16),
         ],
-        in_specs=[smem, smem, vmem] + [far_off] * (n_src + n_tgt),
+        in_specs=[far_off, smem, vmem] + [far_off] * (n_src + n_tgt),
         out_specs=[vmem] * 4,
         scratch_shapes=[
             pltpu.VMEM((n_src + 1, 64, half), jnp.bfloat16),
@@ -210,26 +211,24 @@
             pltpu.SemaphoreType.DMA((n_src + 1,)),
             pltpu.SemaphoreType.DMA((n_tgt,)),
         ]
-        + tile_scratch(targets, sources, slots),
+        + tile_scratch(targets, sources, listed.shape[0]),
         compiler_params=pltpu.CompilerParams(vmem_limit_bytes=32 * 1024 * 1024),
         name=name,
-    )(meta, places, pot, *srcs, *tgts)
-
-
-def later_pass(meta, parts, mass, lhs, rhs, slots, order, name):
+    )(listed, places, pot, *srcs, *tgts)
+
+
+def later_pass(listed, parts, mass, lhs, rhs, keep, name):
     blocks_a, blocks_b = lhs.shape[0], rhs.shape[0]
-    shape = jax.ShapeDtypeStruct
-    width = slots + pad
-    a_at = 1 + 2 * order * width
+    shapes = [(blocks_b, BLOCK)] + [(blocks_a, BLOCK)] * keep
     return pl.pallas_call(
-        functools.partial(later_kernel, a_at, a_at + width, len(parts)),
-        out_shape=[shape((blocks_b, BLOCK), jnp.float32), shape((blocks_a, BLOCK), jnp.float32)],
-        in_specs=[smem] + [vmem] * (len(parts) + 3),
-        out_specs=[vmem, vmem],
-        scratch_shapes=tile_scratch(blocks_a, blocks_b, slots),
+        functools.partial(later_kernel, len(parts), keep),
+        out_shape=[jax.ShapeDtypeStruct(shape, jnp.float32) for shape in shapes],
+        in_specs=[far_off] + [vmem] * (len(parts) + 3),
+        out_specs=[vmem] * len(shapes),
+        scratch_shapes=tile_scratch(blocks_a, blocks_b, listed.shape[0]),
         compiler_params=pltpu.CompilerParams(vmem_limit_bytes=32 * 1024 * 1024),
         name=name,
-    )(meta, *parts, mass, lhs, rhs)
+    )(listed, *parts, mass, lhs, rhs)
 
 
 def swap(value, rows, cols, row_bit, col_bit):
@@ -258,7 +257,7 @@
     places = jnp.arange(slots, dtype=jnp.int32)
     hit = (rank[None, :] == places[:, None]) & alive[None, :]
     ordered = jnp.sum(jnp.where(hit, code[None, :] - after, 0), axis=1) + after
-    return ordered // parts, ordered % parts
+    return place * (ordered // parts) + ordered % parts
 
 
 def shards(rows, cols, emb_source, emb_target, source_mass, target_mass, start_potential, support, count):
@@ -316,10 +315,12 @@
     t_ids = (named // (2 * per)) * per + named % per
     s_ids = jnp.arange(slots, dtype=jnp.int32) // depth
     live = jnp.sum(alive.astype(jnp.int32)).reshape(1)
-    blank = jnp.zeros((pad,), jnp.int32)
-    s_b, s_a = tile_list(s_ids * targets + t_ids, alive, targets, sources * targets)
-    t_b, t_a = tile_list(t_ids * sources + s_ids, alive, sources, sources * targets)
-    meta = jnp.concatenate([live, s_a, blank, s_b, blank + sources, t_a, blank, t_b, blank + targets])
+    last = jnp.full((pad,), place, jnp.int32)
+    by_source = tile_list(s_ids * targets + t_ids, alive, targets, sources * targets)
+    by_source = jnp.concatenate([live, by_source, last * sources])
+    by_target = tile_list(t_ids * sources + s_ids, alive, sources, sources * targets)
+    by_target = jnp.concatenate([live, by_target, last * targets])
+    by_source, by_target = lax.optimization_barrier((by_source, by_target))
     t_mass = of_side(target_mass)
 
     col_bits = [1 << k for k in range((cols - 1).bit_length())]
@@ -328,11 +329,11 @@
     t_hops = [(bit, 0) for bit in row_bits[1:]]
 
     lse, ysq, xb, yb = first_pass(
-        meta, places, of_side(start_potential), srcs, tgts, sources, targets, slots, "source_first"
+        by_source, places, of_side(start_potential), srcs, tgts, sources, targets, "source_first"
     )
-    lse, _ = later_pass(meta, exchange(lse, s_hops, swap_by), s_mass, xb, yb, slots, 1, "target_first")
-    lse, _ = later_pass(meta, exchange(lse, t_hops, swap_by), t_mass, yb, xb, slots, 0, "source_second")
-    lse, pot = later_pass(meta, exchange(lse, s_hops, swap_by), s_mass, xb, yb, slots, 1, "target_second")
+    (lse,) = later_pass(by_target, exchange(lse, s_hops, swap_by), s_mass, xb, yb, False, "target_first")
+    (lse,) = later_pass(by_source, exchange(lse, t_hops, swap_by), t_mass, yb, xb, False, "source_second")
+    lse, pot = later_pass(by_target, exchange(lse, s_hops, swap_by), s_mass, xb, yb, True, "target_second")
 
     lse = lse - (eps * jnp.log(t_mass) + 0.5 * ysq)
     for hop in t_hops[:-1]:

time: 86.6 us -> 84.2 us (0.972)
  Pallas kernels: 24.3 us -> 19.7 us
  between operations: 2.55 us -> 4.13 us
    pallas_call x4, Pallas kernels: 24.3 us -> 19.7 us  [the longest x3 13.5 us: later_pass(): pl.pallas_call(functools.partial(later_kernel, len(parts), keep), out_sha...]
    ppermute x11, waiting for transfers between devices: 14.9 us -> 13.3 us  [swap(): return lax.ppermute(value, 'row', [(i, i ^ row_bit) for i in range(rows)])]
    ppermute x11, starting transfers between devices: 11.7 us -> 13 us  [swap(): return lax.ppermute(value, 'row', [(i, i ^ row_bit) for i in range(rows)])]
    ppermute x2, waiting for transfers between devices: 1.84 us -> 2.93 us  [shards(): ahead = lax.ppermute(ahead, 'row', onward)]
    ppermute x5, starting transfers between devices: 2.79 us -> 1.9 us  [swap(): return lax.ppermute(value, 'col', [(i, i ^ col_bit) for i in range(cols)])]
  transfers between devices with their start and end apart: 21 -> 21, of which waited for: 15 -> 15; matrix products, arithmetic and copies ran while one was open for 13% -> 14% of each run, Pallas kernels for 0% -> 0%
where the time goes in v5:
time: 84.2 us; the launch traced here: 83.8 us
  starting transfers between devices  24.5 us (29%)
  waiting for transfers between devices  23.2 us (28%)
  Pallas kernels  19.7 us (23%)
  local copies, waits for them, and re-layouts  6.61 us (8%)
  other arithmetic  5.72 us (7%)
  between operations  4.13 us (5%)
    pallas_call x3, Pallas kernels, later_pass(): pl.pallas_call(functools.partial(later_kernel, len(parts), keep), out_sha...  13.5 us
    ppermute x11, waiting for transfers between devices, swap(): return lax.ppermute(value, 'row', [(i, i ^ row_bit) for i in range(rows)])  13.3 us
    ppermute x11, starting transfers between devices, swap(): return lax.ppermute(value, 'row', [(i, i ^ row_bit) for i in range(rows)])  13 us
    pallas_call x1, Pallas kernels, first_pass(): pl.pallas_call(functools.partial(first_kernel, n_src, n_tgt), out_shape=[...  6.22 us
    ppermute x2, waiting for transfers between devices, swap(): return lax.ppermute(value, ('row', 'col'), pairs)  3.55 us
    ppermute x5, waiting for transfers between devices, swap(): return lax.ppermute(value, 'col', [(i, i ^ col_bit) for i in range(cols)])  3.39 us
    ppermute x2, starting transfers between devices, swap(): return lax.ppermute(value, ('row', 'col'), pairs)  3.39 us
    ppermute x2, starting transfers between devices, shards(): ahead = lax.ppermute(ahead, 'row', onward)  3.09 us
  transfers between devices with their start and end apart: 21, of which 15 were waited for; matrix products, arithmetic and copies ran while one was open for 14% of the time, Pallas kernels for 0%

profile of v5, /device:TPU:0, one launch (start us, length us, event | category | flops | bytes accessed | tf_op | source)
XLA Modules:
  0.0 83.8 jit_solution(10036215243840371629)
XLA Ops:
  0.7 3.1 %collective-permute-start.4 = (bf16[64,2048]{1,0:T(8,128)(2,1)}, bf16[64,2048]{1,0:T(8,128)(2,1)S(1)}, u32[]{:S(2)}, u32[]{:S(2)}) collective-permute-start(bf16[64,2048]{1,0:T(8,128)(2,1)} %bitcast.42), channel_id=1, source_target_pairs={{16,0},{20,4},{0,8},{4,12},{24,16},{28,20},{8,24},{12,28},{17,1},{... | collective-permute-start | bytes 786440 | tf_op jit(solution)/shard_map/ppermute | solution.py:285
  3.7 1.1 %collective-permute-start.1 = (bf16[64,2048]{1,0:T(8,128)(2,1)}, bf16[64,2048]{1,0:T(8,128)(2,1)S(1)}, u32[]{:S(2)}, u32[]{:S(2)}) collective-permute-start(bf16[64,2048]{1,0:T(8,128)(2,1)} %bitcast.43), channel_id=1, source_target_pairs={{0,16},{4,20},{8,0},{12,4},{16,24},{20,28},{24,8},{28,12},{1,17},{... | collective-permute-start | bytes 786440 | tf_op jit(solution)/shard_map/ppermute | solution.py:281
  7.1 1.8 %collective-permute-start = (f32[64,132]{1,0:T(8,128)S(1)}, f32[64,132]{1,0:T(8,128)S(1)}, u32[]{:S(2)}, u32[]{:S(2)}) collective-permute-start(f32[64,132]{1,0:T(8,128)S(1)} %pad_maximum_fusion.1), channel_id=1, source_target_pairs={{0,4},{4,0},{8,12},{12,8},{16,20},{20,16},{24,28},{28,24},{1,5},{5... | collective-permute-start | bytes 101384 | tf_op jit(solution)/shard_map/ppermute | solution.py:236
  8.9 1.1 %constant_dynamic-slice_fusion.1 = bf16[64,4096]{1,0:T(8,128)(2,1)S(1)} fusion(bf16[64,8192]{1,0:T(8,128)(2,1)} %bitcast.38, s32[]{:T(128)S(6)} %select_n.314), kind=kLoop, calls=%fused_computation.119 | loop fusion | bytes 1048580 | tf_op jit(solution)/shard_map/dynamic_slice | solution.py:299
  10.3 1.2 %dynamic_slice.25 = s32[1]{0:T(128)} dynamic-slice(s32[4]{0:T(128)} %constant.235.clone, s32[]{:T(128)S(6)} %select_n.301), dynamic_slice_sizes={1} | dynamic-slice | bytes 12 | tf_op jit(solution)/shard_map/dynamic_slice | solution.py:276
  14.8 1.4 %fusion.51 = (s32[1]{0:T(128)}, s32[1]{0:T(128)}, s32[1]{0:T(128)}) fusion(s32[4]{0:T(128)} %constant.236.clone, s32[]{:T(128)S(6)} %select_n.312, s32[]{:T(128)S(6)} %select_n.308, s32[]{:T(128)S(6)} %select_n.310), kind=kLoop, calls=%fused_computation.121 | loop fusion | bytes 36 | tf_op jit(solution)/shard_map/dynamic_slice | solution.py:283
  16.2 2.0 %stack.23.places = s32[8]{0:T(128)S(1)} concatenate(s32[1]{0:T(128)} %bitcast.8, s32[1]{0:T(128)} %bitcast.9, s32[1]{0:T(128)} %bitcast.10, s32[1]{0:T(128)} %bitcast.11, s32[1]{0:T(128)} %bitcast.12, s32[1]{0:T(128)} %get-tuple-element.41, s32[1]{0:T(128)} %get-tuple-element.42, s32[1]{0:T(128)} %get-tuple-element.40), dimensions={0} | concatenate | bytes 64 | tf_op jit(solution)/shard_map/stack | solution.py:304
  19.3 2.0 %collective-permute-start.5 = (bf16[64,2048]{1,0:T(8,128)(2,1)S(1)}, bf16[64,2048]{1,0:T(8,128)(2,1)S(1)}, u32[]{:S(2)}, u32[]{:S(2)}) collective-permute-start(bf16[64,2048]{1,0:T(8,128)(2,1)S(1)} %collective-permute-done.1.refs_4_), channel_id=1, source_target_pairs={{0,16},{4,20},{8,0},{12,4},{16,24},{20,28},{24,8},{28,12},{1,17},{... | collective-permute-start | bytes 786440 | tf_op jit(solution)/shard_map/ppermute | solution.py:281
  23.6 2.9 %collective-permute-done.5.refs_6_ = bf16[64,2048]{1,0:T(8,128)(2,1)S(1)} collective-permute-done((bf16[64,2048]{1,0:T(8,128)(2,1)S(1)}, bf16[64,2048]{1,0:T(8,128)(2,1)S(1)}, u32[]{:S(2)}, u32[]{:S(2)}) %collective-permute-start.5) | collective-permute-done | bytes 262176 | tf_op jit(solution)/shard_map/ppermute | solution.py:281
  26.6 6.2 %source_first.1 = (f32[128,128]{1,0:T(8,128)S(1)}, f32[64,128]{1,0:T(8,128)S(1)}, bf16[128,64,128]{2,1,0:T(8,128)(2,1)S(1)}, bf16[64,64,128]{2,1,0:T(8,128)(2,1)S(1)}) custom-call(s32[529]{0:T(1024)S(1)} %get-tuple-element.17.tiles_in, s32[8]{0:T(128)S(1)} %stack.23.places, f32[64,128]{1,0:T(8,128)S(1)} %bitcast.45, bf16[64,8192]{1,0:T(8,128)(2,1)S(1)} %bitcast.39, ...), custom_call_target="tpu_custom_call" | custom-call | tf_op jit(solution)/shard_map/source_first/pallas_call | solution.py:198
  32.9 1.2 %collective-permute-done.6 = f32[128,128]{1,0:T(8,128)S(1)} collective-permute-done((f32[128,128]{1,0:T(8,128)S(1)}, f32[128,128]{1,0:T(8,128)S(1)}, u32[]{:S(2)}, u32[]{:S(2)}) %collective-permute-start.6) | collective-permute-done | bytes 65568 | tf_op jit(solution)/shard_map/ppermute | solution.py:238
  34.2 2.1 %collective-permute-start.9 = (f32[128,128]{1,0:T(8,128)S(1)}, f32[128,128]{1,0:T(8,128)S(1)}, u32[]{:S(2)}, u32[]{:S(2)}) collective-permute-start(f32[128,128]{1,0:T(8,128)S(1)} %multiply_add_fusion.1.refs_0_), channel_id=1, source_target_pairs={{0,6},{1,7},{2,4},{3,5},{4,2},{5,3},{6,0},{7,1},{8,14},{9,15},{10,... | collective-permute-start | bytes 196616 | tf_op jit(solution)/shard_map/ppermute | solution.py:240
  37.8 1.7 %collective-permute-done.9.refs_3_ = f32[128,128]{1,0:T(8,128)S(1)} collective-permute-done((f32[128,128]{1,0:T(8,128)S(1)}, f32[128,128]{1,0:T(8,128)S(1)}, u32[]{:S(2)}, u32[]{:S(2)}) %collective-permute-start.9) | collective-permute-done | bytes 65568 | tf_op jit(solution)/shard_map/ppermute | solution.py:240
  39.5 1.3 %collective-permute-done.8.refs_2_ = f32[128,128]{1,0:T(8,128)S(1)} collective-permute-done((f32[128,128]{1,0:T(8,128)S(1)}, f32[128,128]{1,0:T(8,128)S(1)}, u32[]{:S(2)}, u32[]{:S(2)}) %collective-permute-start.8) | collective-permute-done | bytes 65568 | tf_op jit(solution)/shard_map/ppermute | solution.py:236
  41.5 4.4 %target_first.1.refs_0_ = f32[64,128]{1,0:T(8,128)S(1)} custom-call(s32[529]{0:T(1024)S(1)} %get-tuple-element.16.tiles_in, f32[128,128]{1,0:T(8,128)S(1)} %multiply_add_fusion.1.refs_0_, f32[128,128]{1,0:T(8,128)S(1)} %collective-permute-done.7.refs_1_, f32[128,128]{1,0:T(8,128)S(1)} %collective-permute-done.8.refs_2_, ...), custom_call_target="tpu_custom_call" | custom-call | tf_op jit(solution)/shard_map/target_first/pallas_call | solution.py:223
  45.9 3.2 %collective-permute-start.12 = (f32[64,128]{1,0:T(8,128)S(1)}, f32[64,128]{1,0:T(8,128)S(1)}, u32[]{:S(2)}, u32[]{:S(2)}) collective-permute-start(f32[64,128]{1,0:T(8,128)S(1)} %target_first.1.refs_0_), channel_id=1, source_target_pairs={{0,24},{4,28},{8,16},{12,20},{16,8},{20,12},{24,0},{28,4},{1,25},{... | collective-permute-start | bytes 98312 | tf_op jit(solution)/shard_map/ppermute | solution.py:236
  49.1 1.2 %collective-permute-start.10 = (f32[64,128]{1,0:T(8,128)S(1)}, f32[64,128]{1,0:T(8,128)S(1)}, u32[]{:S(2)}, u32[]{:S(2)}) collective-permute-start(f32[64,128]{1,0:T(8,128)S(1)} %target_first.1.refs_0_), channel_id=1, source_target_pairs={{0,8},{4,12},{8,0},{12,4},{16,24},{20,28},{24,16},{28,20},{1,9},{5... | collective-permute-start | bytes 98312 | tf_op jit(solution)/shard_map/ppermute | solution.py:236
  50.4 1.3 %collective-permute-done.12.refs_3_ = f32[64,128]{1,0:T(8,128)S(1)} collective-permute-done((f32[64,128]{1,0:T(8,128)S(1)}, f32[64,128]{1,0:T(8,128)S(1)}, u32[]{:S(2)}, u32[]{:S(2)}) %collective-permute-start.12) | collective-permute-done | bytes 32800 | tf_op jit(solution)/shard_map/ppermute | solution.py:236
  51.7 2.2 %collective-permute-done.11.refs_2_ = f32[64,128]{1,0:T(8,128)S(1)} collective-permute-done((f32[64,128]{1,0:T(8,128)S(1)}, f32[64,128]{1,0:T(8,128)S(1)}, u32[]{:S(2)}, u32[]{:S(2)}) %collective-permute-start.11) | collective-permute-done | bytes 32800 | tf_op jit(solution)/shard_map/ppermute | solution.py:236
  53.9 4.5 %source_second.1 = f32[128,128]{1,0:T(8,128)S(1)} custom-call(s32[529]{0:T(1024)S(1)} %get-tuple-element.17.tiles_in, f32[64,128]{1,0:T(8,128)S(1)} %target_first.1.refs_0_, f32[64,128]{1,0:T(8,128)S(1)} %collective-permute-done.10.refs_1_, f32[64,128]{1,0:T(8,128)S(1)} %collective-permute-done.11.refs_2_, f32[64,128]{1,0:T(8,128)S(1)} %collective-permute-done.12.refs_3_, ...), custom_call_target="tpu_custom_call" | custom-call | tf_op jit(solution)/shard_map/source_second/pallas_call | solution.py:223
  58.5 1.2 %collective-permute-done.13 = f32[128,128]{1,0:T(8,128)S(1)} collective-permute-done((f32[128,128]{1,0:T(8,128)S(1)}, f32[128,128]{1,0:T(8,128)S(1)}, u32[]{:S(2)}, u32[]{:S(2)}) %collective-permute-start.13) | collective-permute-done | bytes 65568 | tf_op jit(solution)/shard_map/ppermute | solution.py:238
  59.8 1.3 %collective-permute-start.16 = (f32[128,128]{1,0:T(8,128)S(1)}, f32[128,128]{1,0:T(8,128)S(1)}, u32[]{:S(2)}, u32[]{:S(2)}) collective-permute-start(f32[128,128]{1,0:T(8,128)S(1)} %multiply_add_fusion.refs_0_), channel_id=1, source_target_pairs={{0,6},{1,7},{2,4},{3,5},{4,2},{5,3},{6,0},{7,1},{8,14},{9,15},{10,... | collective-permute-start | bytes 196616 | tf_op jit(solution)/shard_map/ppermute | solution.py:240
  61.1 1.0 %collective-permute-start.15 = (f32[128,128]{1,0:T(8,128)S(1)}, f32[128,128]{1,0:T(8,128)S(1)}, u32[]{:S(2)}, u32[]{:S(2)}) collective-permute-start(f32[128,128]{1,0:T(8,128)S(1)} %multiply_add_fusion.refs_0_), channel_id=1, source_target_pairs={{0,4},{4,0},{8,12},{12,8},{16,20},{20,16},{24,28},{28,24},{1,5},{5... | collective-permute-start | bytes 196616 | tf_op jit(solution)/shard_map/ppermute | solution.py:236
  62.1 1.2 %collective-permute-start.14 = (f32[128,128]{1,0:T(8,128)S(1)}, f32[128,128]{1,0:T(8,128)S(1)}, u32[]{:S(2)}, u32[]{:S(2)}) collective-permute-start(f32[128,128]{1,0:T(8,128)S(1)} %multiply_add_fusion.refs_0_), channel_id=1, source_target_pairs={{0,2},{1,3},{2,0},{3,1},{4,6},{5,7},{6,4},{7,5},{8,10},{9,11},{10,... | collective-permute-start | bytes 196616 | tf_op jit(solution)/shard_map/ppermute | solution.py:238
  63.4 1.8 %collective-permute-done.16.refs_3_ = f32[128,128]{1,0:T(8,128)S(1)} collective-permute-done((f32[128,128]{1,0:T(8,128)S(1)}, f32[128,128]{1,0:T(8,128)S(1)}, u32[]{:S(2)}, u32[]{:S(2)}) %collective-permute-start.16) | collective-permute-done | bytes 65568 | tf_op jit(solution)/shard_map/ppermute | solution.py:240
  65.2 1.2 %collective-permute-done.15.refs_2_ = f32[128,128]{1,0:T(8,128)S(1)} collective-permute-done((f32[128,128]{1,0:T(8,128)S(1)}, f32[128,128]{1,0:T(8,128)S(1)}, u32[]{:S(2)}, u32[]{:S(2)}) %collective-permute-start.15) | collective-permute-done | bytes 65568 | tf_op jit(solution)/shard_map/ppermute | solution.py:236
  66.6 4.6 %target_second.1 = (f32[64,128]{1,0:T(8,128)S(1)}, f32[128,128]{1,0:T(8,128)S(1)}) custom-call(s32[529]{0:T(1024)S(1)} %get-tuple-element.16.tiles_in, f32[128,128]{1,0:T(8,128)S(1)} %multiply_add_fusion.refs_0_, f32[128,128]{1,0:T(8,128)S(1)} %collective-permute-done.14.refs_1_, f32[128,128]{1,0:T(8,128)S(1)} %collective-permute-done.15.refs_2_, ...), custom_call_target="tpu_custom_call" | custom-call | tf_op jit(solution)/shard_map/target_second/pallas_call | solution.py:223
  71.6 3.6 %collective-permute-done.17 = f32[64,128]{1,0:T(8,128)S(1)} collective-permute-done((f32[64,128]{1,0:T(8,128)S(1)}, f32[64,128]{1,0:T(8,128)S(1)}, u32[]{:S(2)}, u32[]{:S(2)}) %collective-permute-start.17) | collective-permute-done | bytes 32800 | tf_op jit(solution)/shard_map/ppermute | solution.py:236
  76.1 2.1 %collective-permute-start.20 = (f32[64,128]{1,0:T(8,128)S(1)}, f32[64,128]{1,0:T(8,128)S(1)}, u32[]{:S(2)}, u32[]{:S(2)}) collective-permute-start(f32[64,128]{1,0:T(8,128)S(1)} %multiply_add_fusion.4), channel_id=1, source_target_pairs={{0,20},{4,16},{8,28},{12,24},{16,4},{20,0},{24,12},{28,8},{1,21},{... | collective-permute-start | bytes 98312 | tf_op jit(solution)/shard_map/ppermute | solution.py:236
  78.2 1.5 %collective-permute-start.18 = (f32[64,128]{1,0:T(8,128)S(1)}, f32[64,128]{1,0:T(8,128)S(1)}, u32[]{:S(2)}, u32[]{:S(2)}) collective-permute-start(f32[64,128]{1,0:T(8,128)S(1)} %multiply_add_fusion.4), channel_id=1, source_target_pairs={{0,16},{4,20},{8,24},{12,28},{16,0},{20,4},{24,8},{28,12},{1,17},{... | collective-permute-start | bytes 98312 | tf_op jit(solution)/shard_map/ppermute | solution.py:236
  80.3 1.8 %collective-permute-done.20 = f32[64,128]{1,0:T(8,128)S(1)} collective-permute-done((f32[64,128]{1,0:T(8,128)S(1)}, f32[64,128]{1,0:T(8,128)S(1)}, u32[]{:S(2)}, u32[]{:S(2)}) %collective-permute-start.20) | collective-permute-done | bytes 32800 | tf_op jit(solution)/shard_map/ppermute | solution.py:236
  82.1 1.1 %collective-permute-done.18 = f32[64,128]{1,0:T(8,128)S(1)} collective-permute-done((f32[64,128]{1,0:T(8,128)S(1)}, f32[64,128]{1,0:T(8,128)S(1)}, u32[]{:S(2)}, u32[]{:S(2)}) %collective-permute-start.18) | collective-permute-done | bytes 32800 | tf_op jit(solution)/shard_map/ppermute | solution.py:236
  (53 shorter events, 11.2 us)
Async XLA Ops:
  0.6 9.6 %copy-start = (f32[16384]{0:T(1024)S(1)}, f32[16384]{0:T(1024)}, u32[]{:S(2)}) copy-start(f32[16384]{0:T(1024)} %param.13) | copy-start | bytes 196612
  0.6 25.9 %copy-start.2 = (bf16[2048,64]{0,1:T(8,128)(2,1)S(1)}, bf16[2048,64]{0,1:T(8,128)(2,1)}, u32[]{:S(2)}) copy-start(bf16[2048,64]{0,1:T(8,128)(2,1)} %param.10) | copy-start | bytes 786436
  0.7 25.9 %copy-start.1 = (bf16[8192,64]{0,1:T(8,128)(2,1)S(1)}, bf16[8192,64]{0,1:T(8,128)(2,1)}, u32[]{:S(2)}) copy-start(bf16[8192,64]{0,1:T(8,128)(2,1)} %param.9) | copy-start | bytes 3145732
  0.7 23.0 %collective-permute-start.4 = (bf16[64,2048]{1,0:T(8,128)(2,1)}, bf16[64,2048]{1,0:T(8,128)(2,1)S(1)}, u32[]{:S(2)}, u32[]{:S(2)}) collective-permute-start(bf16[64,2048]{1,0:T(8,128)(2,1)} %bitcast.42), channel_id=1, source_target_pairs={{16,0},{20,4},{0,8},{4,12},{24,16},{28,20},{8,24},{12,28},{17,1},{... | collective-permute-start | bytes 786440 | tf_op jit(solution)/shard_map/ppermute | solution.py:285
  3.7 14.4 %collective-permute-start.1 = (bf16[64,2048]{1,0:T(8,128)(2,1)}, bf16[64,2048]{1,0:T(8,128)(2,1)S(1)}, u32[]{:S(2)}, u32[]{:S(2)}) collective-permute-start(bf16[64,2048]{1,0:T(8,128)(2,1)} %bitcast.43), channel_id=1, source_target_pairs={{0,16},{4,20},{8,0},{12,4},{16,24},{20,28},{24,8},{28,12},{1,17},{... | collective-permute-start | bytes 786440 | tf_op jit(solution)/shard_map/ppermute | solution.py:281
  7.1 11.1 %collective-permute-start = (f32[64,132]{1,0:T(8,128)S(1)}, f32[64,132]{1,0:T(8,128)S(1)}, u32[]{:S(2)}, u32[]{:S(2)}) collective-permute-start(f32[64,132]{1,0:T(8,128)S(1)} %pad_maximum_fusion.1), channel_id=1, source_target_pairs={{0,4},{4,0},{8,12},{12,8},{16,20},{20,16},{24,28},{28,24},{1,5},{5... | collective-permute-start | bytes 101384 | tf_op jit(solution)/shard_map/ppermute | solution.py:236
  10.0 12.9 %collective-permute-start.2 = (bf16[64,4096]{1,0:T(8,128)(2,1)S(1)}, bf16[64,4096]{1,0:T(8,128)(2,1)S(1)}, u32[]{:S(2)}, u32[]{:S(2)}) collective-permute-start(bf16[64,4096]{1,0:T(8,128)(2,1)S(1)} %constant_dynamic-slice_fusion.1), channel_id=1, source_target_pairs={{0,4},{4,0},{8,12},{12,8},{16,20},{20,16},{24,28},{28,24},{1,5},{5... | collective-permute-start | bytes 1572872 | tf_op jit(solution)/shard_map/ppermute | solution.py:236
  19.3 7.3 %collective-permute-start.5 = (bf16[64,2048]{1,0:T(8,128)(2,1)S(1)}, bf16[64,2048]{1,0:T(8,128)(2,1)S(1)}, u32[]{:S(2)}, u32[]{:S(2)}) collective-permute-start(bf16[64,2048]{1,0:T(8,128)(2,1)S(1)} %collective-permute-done.1.refs_4_), channel_id=1, source_target_pairs={{0,16},{4,20},{8,0},{12,4},{16,24},{20,28},{24,8},{28,12},{1,17},{... | collective-permute-start | bytes 786440 | tf_op jit(solution)/shard_map/ppermute | solution.py:281
  22.9 3.7 %collective-permute-start.3 = (bf16[64,4096]{1,0:T(8,128)(2,1)S(1)}, bf16[64,4096]{1,0:T(8,128)(2,1)S(1)}, u32[]{:S(2)}, u32[]{:S(2)}) collective-permute-start(bf16[64,4096]{1,0:T(8,128)(2,1)S(1)} %collective-permute-done.2.refs_1_), channel_id=1, source_target_pairs={{0,1},{1,0},{2,3},{3,2},{4,5},{5,4},{6,7},{7,6},{8,9},{9,8},{10,11... | collective-permute-start | bytes 1572872 | tf_op jit(solution)/shard_map/ppermute | solution.py:238
  32.8 17.6 %copy-start.3 = (f32[16384]{0:T(1024)S(1)}, f32[16384]{0:T(1024)}, u32[]{:S(2)}) copy-start(f32[16384]{0:T(1024)} %param.12) | copy-start | bytes 196612
  32.8 1.3 %collective-permute-start.6 = (f32[128,128]{1,0:T(8,128)S(1)}, f32[128,128]{1,0:T(8,128)S(1)}, u32[]{:S(2)}, u32[]{:S(2)}) collective-permute-start(f32[128,128]{1,0:T(8,128)S(1)} %get-tuple-element.20), channel_id=1, source_target_pairs={{0,1},{1,0},{2,3},{3,2},{4,5},{5,4},{6,7},{7,6},{8,9},{9,8},{10,11... | collective-permute-start | bytes 196616 | tf_op jit(solution)/shard_map/ppermute | solution.py:238
  34.2 5.3 %collective-permute-start.9 = (f32[128,128]{1,0:T(8,128)S(1)}, f32[128,128]{1,0:T(8,128)S(1)}, u32[]{:S(2)}, u32[]{:S(2)}) collective-permute-start(f32[128,128]{1,0:T(8,128)S(1)} %multiply_add_fusion.1.refs_0_), channel_id=1, source_target_pairs={{0,6},{1,7},{2,4},{3,5},{4,2},{5,3},{6,0},{7,1},{8,14},{9,15},{10,... | collective-permute-start | bytes 196616 | tf_op jit(solution)/shard_map/ppermute | solution.py:240
  36.3 4.6 %collective-permute-start.8 = (f32[128,128]{1,0:T(8,128)S(1)}, f32[128,128]{1,0:T(8,128)S(1)}, u32[]{:S(2)}, u32[]{:S(2)}) collective-permute-start(f32[128,128]{1,0:T(8,128)S(1)} %multiply_add_fusion.1.refs_0_), channel_id=1, source_target_pairs={{0,4},{4,0},{8,12},{12,8},{16,20},{20,16},{24,28},{28,24},{1,5},{5... | collective-permute-start | bytes 196616 | tf_op jit(solution)/shard_map/ppermute | solution.py:236
  37.2 4.3 %collective-permute-start.7 = (f32[128,128]{1,0:T(8,128)S(1)}, f32[128,128]{1,0:T(8,128)S(1)}, u32[]{:S(2)}, u32[]{:S(2)}) collective-permute-start(f32[128,128]{1,0:T(8,128)S(1)} %multiply_add_fusion.1.refs_0_), channel_id=1, source_target_pairs={{0,2},{1,3},{2,0},{3,1},{4,6},{5,7},{6,4},{7,5},{8,10},{9,11},{10,... | collective-permute-start | bytes 196616 | tf_op jit(solution)/shard_map/ppermute | solution.py:238
  45.9 5.8 %collective-permute-start.12 = (f32[64,128]{1,0:T(8,128)S(1)}, f32[64,128]{1,0:T(8,128)S(1)}, u32[]{:S(2)}, u32[]{:S(2)}) collective-permute-start(f32[64,128]{1,0:T(8,128)S(1)} %target_first.1.refs_0_), channel_id=1, source_target_pairs={{0,24},{4,28},{8,16},{12,20},{16,8},{20,12},{24,0},{28,4},{1,25},{... | collective-permute-start | bytes 98312 | tf_op jit(solution)/shard_map/ppermute | solution.py:236
  49.1 4.8 %collective-permute-start.11 = (f32[64,128]{1,0:T(8,128)S(1)}, f32[64,128]{1,0:T(8,128)S(1)}, u32[]{:S(2)}, u32[]{:S(2)}) collective-permute-start(f32[64,128]{1,0:T(8,128)S(1)} %target_first.1.refs_0_), channel_id=1, source_target_pairs={{0,16},{4,20},{8,24},{12,28},{16,0},{20,4},{24,8},{28,12},{1,17},{... | collective-permute-start | bytes 98312 | tf_op jit(solution)/shard_map/ppermute | solution.py:236
  49.1 4.8 %collective-permute-start.10 = (f32[64,128]{1,0:T(8,128)S(1)}, f32[64,128]{1,0:T(8,128)S(1)}, u32[]{:S(2)}, u32[]{:S(2)}) collective-permute-start(f32[64,128]{1,0:T(8,128)S(1)} %target_first.1.refs_0_), channel_id=1, source_target_pairs={{0,8},{4,12},{8,0},{12,4},{16,24},{20,28},{24,16},{28,20},{1,9},{5... | collective-permute-start | bytes 98312 | tf_op jit(solution)/shard_map/ppermute | solution.py:236
  58.4 1.3 %collective-permute-start.13 = (f32[128,128]{1,0:T(8,128)S(1)}, f32[128,128]{1,0:T(8,128)S(1)}, u32[]{:S(2)}, u32[]{:S(2)}) collective-permute-start(f32[128,128]{1,0:T(8,128)S(1)} %source_second.1), channel_id=1, source_target_pairs={{0,1},{1,0},{2,3},{3,2},{4,5},{5,4},{6,7},{7,6},{8,9},{9,8},{10,11... | collective-permute-start | bytes 196616 | tf_op jit(solution)/shard_map/ppermute | solution.py:238
  59.8 5.4 %collective-permute-start.16 = (f32[128,128]{1,0:T(8,128)S(1)}, f32[128,128]{1,0:T(8,128)S(1)}, u32[]{:S(2)}, u32[]{:S(2)}) collective-permute-start(f32[128,128]{1,0:T(8,128)S(1)} %multiply_add_fusion.refs_0_), channel_id=1, source_target_pairs={{0,6},{1,7},{2,4},{3,5},{4,2},{5,3},{6,0},{7,1},{8,14},{9,15},{10,... | collective-permute-start | bytes 196616 | tf_op jit(solution)/shard_map/ppermute | solution.py:240
  61.1 5.2 %collective-permute-start.15 = (f32[128,128]{1,0:T(8,128)S(1)}, f32[128,128]{1,0:T(8,128)S(1)}, u32[]{:S(2)}, u32[]{:S(2)}) collective-permute-start(f32[128,128]{1,0:T(8,128)S(1)} %multiply_add_fusion.refs_0_), channel_id=1, source_target_pairs={{0,4},{4,0},{8,12},{12,8},{16,20},{20,16},{24,28},{28,24},{1,5},{5... | collective-permute-start | bytes 196616 | tf_op jit(solution)/shard_map/ppermute | solution.py:236
  62.1 4.4 %collective-permute-start.14 = (f32[128,128]{1,0:T(8,128)S(1)}, f32[128,128]{1,0:T(8,128)S(1)}, u32[]{:S(2)}, u32[]{:S(2)}) collective-permute-start(f32[128,128]{1,0:T(8,128)S(1)} %multiply_add_fusion.refs_0_), channel_id=1, source_target_pairs={{0,2},{1,3},{2,0},{3,1},{4,6},{5,7},{6,4},{7,5},{8,10},{9,11},{10,... | collective-permute-start | bytes 196616 | tf_op jit(solution)/shard_map/ppermute | solution.py:238
  71.2 4.0 %collective-permute-start.17 = (f32[64,128]{1,0:T(8,128)S(1)}, f32[64,128]{1,0:T(8,128)S(1)}, u32[]{:S(2)}, u32[]{:S(2)}) collective-permute-start(f32[64,128]{1,0:T(8,128)S(1)} %add_subtract_fusion), channel_id=1, source_target_pairs={{0,8},{4,12},{8,0},{12,4},{16,24},{20,28},{24,16},{28,20},{1,9},{5... | collective-permute-start | bytes 98312 | tf_op jit(solution)/shard_map/ppermute | solution.py:236
  75.2 5.1 %collective-permute-start.19 = (f32[64,128]{1,0:T(8,128)S(1)}, f32[64,128]{1,0:T(8,128)S(1)}, u32[]{:S(2)}, u32[]{:S(2)}) collective-permute-start(f32[64,128]{1,0:T(8,128)S(1)} %multiply_add_fusion.4), channel_id=1, source_target_pairs={{0,4},{4,0},{8,12},{12,8},{16,20},{20,16},{24,28},{28,24},{1,5},{5... | collective-permute-start | bytes 98312 | tf_op jit(solution)/shard_map/ppermute | solution.py:236
  76.1 5.9 %collective-permute-start.20 = (f32[64,128]{1,0:T(8,128)S(1)}, f32[64,128]{1,0:T(8,128)S(1)}, u32[]{:S(2)}, u32[]{:S(2)}) collective-permute-start(f32[64,128]{1,0:T(8,128)S(1)} %multiply_add_fusion.4), channel_id=1, source_target_pairs={{0,20},{4,16},{8,28},{12,24},{16,4},{20,0},{24,12},{28,8},{1,21},{... | collective-permute-start | bytes 98312 | tf_op jit(solution)/shard_map/ppermute | solution.py:236
  78.2 5.0 %collective-permute-start.18 = (f32[64,128]{1,0:T(8,128)S(1)}, f32[64,128]{1,0:T(8,128)S(1)}, u32[]{:S(2)}, u32[]{:S(2)}) collective-permute-start(f32[64,128]{1,0:T(8,128)S(1)} %multiply_add_fusion.4), channel_id=1, source_target_pairs={{0,16},{4,20},{8,24},{12,28},{16,0},{20,4},{24,8},{28,12},{1,17},{... | collective-permute-start | bytes 98312 | tf_op jit(solution)/shard_map/ppermute | solution.py:236

commit v6 on v5

--- a/solution.py
+++ b/solution.py
@@ -49,15 +49,6 @@
 def one_rows():
     rows = lax.broadcasted_iota(jnp.int32, (16, BLOCK), 0)
     return jnp.where(rows < 3, 1.0, 0.0).astype(jnp.bfloat16)
-
-
-def fill(count, step):
-    def body(i, _):
-        for k in range(16):
-            step(i * 16 + k)
-        return 0
-
-    lax.fori_loop(0, count // 16, body, 0)
 
 
 def fetch(tiles_in, listed, arrived):
@@ -84,10 +75,9 @@
             z = lax.dot_general(left, right, (((0,), (0,)), ((), ())), preferred_element_type=jnp.float32)
             z = z.reshape(BLOCK // 8, 8, BLOCK)
             peak = jnp.max(z, axis=0)
-            part = jnp.sum(jnp.exp2((z - peak) * scale), axis=0)
             same = b == last
             joint = jnp.where(same, jnp.maximum(run, peak), peak)
-            part = part * jnp.exp2((peak - joint) * scale)
+            part = jnp.sum(jnp.exp2((z - joint) * scale), axis=0)
             total = jnp.where(same, total * jnp.exp2((run - joint) * scale), 0.0) + part
             top[rows_of(b * 8, 8, 1), :] = joint
             tot[rows_of(b * 8, 8, 1), :] = total
@@ -114,44 +104,34 @@
         out[i * 8 : i * 8 + 8, :] = peak + unit * jnp.log2(total)
 
 
-def load_parts(parts, places, held, sems):
-    copies = []
-    for k, part in enumerate(parts):
-        copies.append(pltpu.make_async_copy(part, held.at[places[k]], sems.at[k]))
-        copies[-1].start()
-    return copies
-
-
-def block_of(held, i):
-    per = held.shape[2] // BLOCK
-    return held[i // per, :, pl.ds(pl.multiple_of(lax.rem(i, per) * BLOCK, BLOCK), BLOCK)]
-
-
-def first_kernel(n_src, n_tgt, tiles_in, places, pot_in, *refs):
+def ring_place(level, levels):
+    return jnp.where(level % 2 == 0, level // 2, levels - (level + 1) // 2)
+
+
+def ring_level(place, levels):
+    place = lax.rem(place + levels, levels)
+    return jnp.where(place < (levels + 1) // 2, 2 * place, 2 * (levels - place) - 1)
+
+
+def first_kernel(n_src, n_tgt, levels, steps, here, tiles_in, pot_in, *refs):
     srcs, refs = refs[:n_src], refs[n_src:]
     tgts, refs = refs[:n_tgt], refs[n_tgt:]
-    out, ysq, xb, yb, xs, ys, xsem, ysem, listed, arrived, tails, top, tot = refs
+    out, ysq, xb, yb, listed, arrived, tails, top, tot = refs
     fetch(tiles_in, listed, arrived).start()
-    half = xs.shape[2]
-    pieces = [srcs[0].at[:, :half], srcs[0].at[:, half:]] + list(srcs[1:])
-    x_copies = load_parts(pieces, [places[k] for k in range(n_src + 1)], xs, xsem)
-    y_copies = load_parts(tgts, [places[n_src + 1 + k] for k in range(n_tgt)], ys, ysem)
-
-    def fill_x(b):
-        xb[b] = block_of(xs, b)
-
-    def fill_y(a):
-        block = block_of(ys, a)
-        yb[a] = block
-        sq = squares(block)
-        ysq[pl.ds(a, 1), :] = sq
-
-    for copy in x_copies:
-        copy.wait()
-    fill(xb.shape[0], fill_x)
-    for copy in y_copies:
-        copy.wait()
-    fill(yb.shape[0], fill_y)
+    side, level, core = here[0], here[1], here[2]
+    half = srcs[1].shape[1]
+    far = 2 - 2 * side
+    pieces = ((srcs[0], 0, 2 * side), (srcs[0], half, 2 * side + 1), (srcs[1], 0, far + core), (srcs[2], 0, far + 1 - core))
+    for part, first, where in pieces:
+        for j in range(half // BLOCK):
+            xb[where * (half // BLOCK) + j] = part[:, first + j * BLOCK : first + (j + 1) * BLOCK]
+    per = tgts[0].shape[1] // BLOCK
+    for part, step in zip(tgts, steps):
+        where = ring_level(ring_place(level, levels) + step, levels)
+        for j in range(per):
+            block = part[:, j * BLOCK : (j + 1) * BLOCK]
+            yb[where * per + j] = block
+            ysq[pl.ds(where * per + j, 1), :] = squares(block)
     tails[...] = jnp.zeros(tails.shape, jnp.float32)
     for i in range(yb.shape[0] // 8):
         rows = slice(i * 8, i * 8 + 8)
@@ -178,7 +158,6 @@
 
 vmem = pl.BlockSpec(memory_space=pltpu.VMEM)
 smem = pl.BlockSpec(memory_space=pltpu.SMEM)
-far_off = pl.BlockSpec(memory_space=pltpu.HBM)
 
 
 def tile_scratch(blocks_a, blocks_b, listed):
@@ -191,30 +170,23 @@
     ]
 
 
-def first_pass(listed, places, pot, srcs, tgts, sources, targets, name):
+def first_pass(listed, here, pot, srcs, tgts, steps, sources, targets, name):
     n_src, n_tgt = len(srcs), len(tgts)
-    half = srcs[1].shape[1]
     shape = jax.ShapeDtypeStruct
     return pl.pallas_call(
-        functools.partial(first_kernel, n_src, n_tgt),
+        functools.partial(first_kernel, n_src, n_tgt, targets * BLOCK // tgts[0].shape[1], steps),
         out_shape=[
             shape((sources, BLOCK), jnp.float32),
             shape((targets, BLOCK), jnp.float32),
             shape((sources, 64, BLOCK), jnp.bfloat16),
             shape((targets, 64, BLOCK), jnp.bfloat16),
         ],
-        in_specs=[far_off, smem, vmem] + [far_off] * (n_src + n_tgt),
+        in_specs=[smem, vmem, vmem] + [vmem] * (n_src + n_tgt),
         out_specs=[vmem] * 4,
-        scratch_shapes=[
-            pltpu.VMEM((n_src + 1, 64, half), jnp.bfloat16),
-            pltpu.VMEM((n_tgt,) + tgts[0].shape, jnp.bfloat16),
-            pltpu.SemaphoreType.DMA((n_src + 1,)),
-            pltpu.SemaphoreType.DMA((n_tgt,)),
-        ]
-        + tile_scratch(targets, sources, listed.shape[0]),
+        scratch_shapes=tile_scratch(targets, sources, listed.shape[0]),
         compiler_params=pltpu.CompilerParams(vmem_limit_bytes=32 * 1024 * 1024),
         name=name,
-    )(listed, places, pot, *srcs, *tgts)
+    )(here, listed, pot, *srcs, *tgts)
 
 
 def later_pass(listed, parts, mass, lhs, rhs, keep, name):
@@ -223,7 +195,7 @@
     return pl.pallas_call(
         functools.partial(later_kernel, len(parts), keep),
         out_shape=[jax.ShapeDtypeStruct(shape, jnp.float32) for shape in shapes],
-        in_specs=[far_off] + [vmem] * (len(parts) + 3),
+        in_specs=[vmem] + [vmem] * (len(parts) + 3),
         out_specs=[vmem] * len(shapes),
         scratch_shapes=tile_scratch(blocks_a, blocks_b, listed.shape[0]),
         compiler_params=pltpu.CompilerParams(vmem_limit_bytes=32 * 1024 * 1024),
@@ -264,6 +236,7 @@
     row = lax.axis_index("row").astype(jnp.int32)
     side, level = row % 2, row // 2
     core = lax.axis_index("col").astype(jnp.int32) % 2
+    here = jnp.stack([side, level, core])
     levels = rows // 2
     per = emb_target.shape[0] // BLOCK
     own_sources = emb_source.shape[0] // BLOCK
@@ -273,18 +246,16 @@
     after = {order[k]: order[(k + 1) % levels] for k in range(levels)}
     onward = [(2 * z + s, 2 * after[z] + s) for z in range(levels) for s in range(2)]
     back = [(b, a) for a, b in onward]
-    place = jnp.asarray([order.index(z) for z in range(levels)], jnp.int32)[level]
-    ring = jnp.asarray(order, jnp.int32)
-    tgts, tgt_places = [emb_target.T], [level]
+    tgts, steps = [emb_target.T], [0]
     ahead = behind = tgts[0]
     for step in range(1, levels // 2 + 1):
         ahead = lax.ppermute(ahead, "row", onward)
         tgts.append(ahead)
-        tgt_places.append(ring[(place - step) % levels])
+        steps.append(-step)
         if 2 * step < levels:
             behind = lax.ppermute(behind, "row", back)
             tgts.append(behind)
-            tgt_places.append(ring[(place + step) % levels])
+            steps.append(step)
 
     swap_by = lambda value, row_bit, col_bit: swap(value, rows, cols, row_bit, col_bit)
     depth = support.shape[2]
@@ -299,9 +270,6 @@
     part = lax.dynamic_slice(xt, (jnp.int32(0), core * half), (xt.shape[0], half))
     part = swap_by(part, 1, 0)
     srcs = [xt, part, swap_by(part, 0, 1)]
-    far = 2 - 2 * side
-    src_places = [2 * side, 2 * side + 1, far + core, far + 1 - core]
-    places = jnp.stack(src_places + tgt_places)
 
     theirs, tgts[1] = lax.optimization_barrier((theirs, tgts[1]))
     pair = jnp.concatenate([jnp.where(side == 0, mine, theirs), jnp.where(side == 0, theirs, mine)])
@@ -329,7 +297,7 @@
     t_hops = [(bit, 0) for bit in row_bits[1:]]
 
     lse, ysq, xb, yb = first_pass(
-        by_source, places, of_side(start_potential), srcs, tgts, sources, targets, "source_first"
+        by_source, here, of_side(start_potential), srcs, tgts, steps, sources, targets, "source_first"
     )
     (lse,) = later_pass(by_target, exchange(lse, s_hops, swap_by), s_mass, xb, yb, False, "target_first")
     (lse,) = later_pass(by_source, exchange(lse, t_hops, swap_by), t_mass, yb, xb, False, "source_second")

time: 84.2 us -> 81.1 us (0.963)
  waiting for transfers between devices: 23.2 us -> 28.2 us
  local copies, waits for them, and re-layouts: 6.61 us -> 1.99 us
  between operations: 4.13 us -> 0.8 us
  Pallas kernels: 19.7 us -> 18.4 us
    ppermute x2, waiting for transfers between devices: 2.93 us -> 8.17 us  [shards(): ahead = lax.ppermute(ahead, 'row', onward)]
    dynamic_slice x2 -> x0, local copies, waits for them, and re-layouts: 2.66 us -> none  [the longest x1 1.42 us: shards(): tgt_places.append(ring[(place - step) % levels])]
    another operation x1 -> x2, local copies, waits for them, and re-layouts: 1.95 us -> 0.01 us  [shards(): places = jnp.stack(src_places + tgt_places)]
    ppermute x2, starting transfers between devices: 3.39 us -> 4.45 us  [swap(): return lax.ppermute(value, ('row', 'col'), pairs)]
    pallas_call x1, Pallas kernels: 6.22 us -> 5.21 us  [first_pass(): pl.pallas_call(functools.partial(first_kernel, n_src, n_tgt, targets * BL...]
  transfers between devices with their start and end apart: 21 -> 21, of which waited for: 15 -> 18; matrix products, arithmetic and copies ran while one was open for 14% -> 9% of each run, Pallas kernels for 0% -> 0%
where the time goes in v6:
time: 81.1 us; the launch traced here: 80.4 us
  waiting for transfers between devices  28.2 us (35%)
  starting transfers between devices  25.3 us (31%)
  Pallas kernels  18.4 us (23%)
  other arithmetic  5.8 us (7%)
  local copies, waits for them, and re-layouts  1.99 us (2%)
    ppermute x11, waiting for transfers between devices, swap(): return lax.ppermute(value, 'row', [(i, i ^ row_bit) for i in range(rows)])  13.6 us
    ppermute x11, starting transfers between devices, swap(): return lax.ppermute(value, 'row', [(i, i ^ row_bit) for i in range(rows)])  13.2 us
    pallas_call x3, Pallas kernels, later_pass(): pl.pallas_call(functools.partial(later_kernel, len(parts), keep), out_sha...  13.2 us
    ppermute x2, waiting for transfers between devices, shards(): ahead = lax.ppermute(ahead, 'row', onward)  8.17 us
    pallas_call x1, Pallas kernels, first_pass(): pl.pallas_call(functools.partial(first_kernel, n_src, n_tgt, targets * BL...  5.21 us
    ppermute x2, starting transfers between devices, swap(): return lax.ppermute(value, ('row', 'col'), pairs)  4.45 us
    ppermute x2, waiting for transfers between devices, swap(): return lax.ppermute(value, ('row', 'col'), pairs)  3.4 us
    ppermute x1, starting transfers between devices, shards(): behind = lax.ppermute(behind, 'row', back)  3.08 us
  transfers between devices with their start and end apart: 21, of which 18 were waited for; matrix products, arithmetic and copies ran while one was open for 9% of the time, Pallas kernels for 0%

profile of v6, /device:TPU:0, one launch (start us, length us, event | category | flops | bytes accessed | tf_op | source)
XLA Modules:
  0.0 80.4 jit_solution(7513233712039894392)
XLA Ops:
  0.7 3.1 %collective-permute-start.4 = (bf16[64,2048]{1,0:T(8,128)(2,1)}, bf16[64,2048]{1,0:T(8,128)(2,1)S(1)}, u32[]{:S(2)}, u32[]{:S(2)}) collective-permute-start(bf16[64,2048]{1,0:T(8,128)(2,1)} %bitcast.35), channel_id=1, source_target_pairs={{16,0},{20,4},{0,8},{4,12},{24,16},{28,20},{8,24},{12,28},{17,1},{... | collective-permute-start | bytes 786440 | tf_op jit(solution)/shard_map/ppermute | solution.py:256
  3.7 1.1 %collective-permute-start.1 = (bf16[64,2048]{1,0:T(8,128)(2,1)}, bf16[64,2048]{1,0:T(8,128)(2,1)S(1)}, u32[]{:S(2)}, u32[]{:S(2)}) collective-permute-start(bf16[64,2048]{1,0:T(8,128)(2,1)} %bitcast.36), channel_id=1, source_target_pairs={{0,16},{4,20},{8,0},{12,4},{16,24},{20,28},{24,8},{28,12},{1,17},{... | collective-permute-start | bytes 786440 | tf_op jit(solution)/shard_map/ppermute | solution.py:252
  7.1 1.8 %collective-permute-start = (f32[64,132]{1,0:T(8,128)S(1)}, f32[64,132]{1,0:T(8,128)S(1)}, u32[]{:S(2)}, u32[]{:S(2)}) collective-permute-start(f32[64,132]{1,0:T(8,128)S(1)} %pad_maximum_fusion.1), channel_id=1, source_target_pairs={{0,4},{4,0},{8,12},{12,8},{16,20},{20,16},{24,28},{28,24},{1,5},{5... | collective-permute-start | bytes 101384 | tf_op jit(solution)/shard_map/ppermute | solution.py:208
  8.9 1.1 %constant_dynamic-slice_fusion.1 = bf16[64,4096]{1,0:T(8,128)(2,1)S(1)} fusion(bf16[64,8192]{1,0:T(8,128)(2,1)} %bitcast.31, s32[]{:T(128)S(6)} %select_n.283), kind=kLoop, calls=%fused_computation.119 | loop fusion | bytes 1048580 | tf_op jit(solution)/shard_map/dynamic_slice | solution.py:270
  10.3 1.0 %collective-permute-done = f32[64,132]{1,0:T(8,128)S(1)} collective-permute-done((f32[64,132]{1,0:T(8,128)S(1)}, f32[64,132]{1,0:T(8,128)S(1)}, u32[]{:S(2)}, u32[]{:S(2)}) %collective-permute-start) | collective-permute-done | bytes 33824 | tf_op jit(solution)/shard_map/ppermute | solution.py:208
  11.4 5.5 %collective-permute-done.1.refs_4_ = bf16[64,2048]{1,0:T(8,128)(2,1)S(1)} collective-permute-done((bf16[64,2048]{1,0:T(8,128)(2,1)}, bf16[64,2048]{1,0:T(8,128)(2,1)S(1)}, u32[]{:S(2)}, u32[]{:S(2)}) %collective-permute-start.1) | collective-permute-done | bytes 262176 | tf_op jit(solution)/shard_map/ppermute | solution.py:252
  18.0 1.8 %collective-permute-start.5 = (bf16[64,2048]{1,0:T(8,128)(2,1)S(1)}, bf16[64,2048]{1,0:T(8,128)(2,1)S(1)}, u32[]{:S(2)}, u32[]{:S(2)}) collective-permute-start(bf16[64,2048]{1,0:T(8,128)(2,1)S(1)} %collective-permute-done.1.refs_4_), channel_id=1, source_target_pairs={{0,16},{4,20},{8,0},{12,4},{16,24},{20,28},{24,8},{28,12},{1,17},{... | collective-permute-start | bytes 786440 | tf_op jit(solution)/shard_map/ppermute | solution.py:252
  20.6 2.3 %collective-permute-done.2.refs_1_ = bf16[64,4096]{1,0:T(8,128)(2,1)S(1)} collective-permute-done((bf16[64,4096]{1,0:T(8,128)(2,1)S(1)}, bf16[64,4096]{1,0:T(8,128)(2,1)S(1)}, u32[]{:S(2)}, u32[]{:S(2)}) %collective-permute-start.2) | collective-permute-done | bytes 524320 | tf_op jit(solution)/shard_map/ppermute | solution.py:208
  23.6 2.6 %collective-permute-done.5.refs_6_ = bf16[64,2048]{1,0:T(8,128)(2,1)S(1)} collective-permute-done((bf16[64,2048]{1,0:T(8,128)(2,1)S(1)}, bf16[64,2048]{1,0:T(8,128)(2,1)S(1)}, u32[]{:S(2)}, u32[]{:S(2)}) %collective-permute-start.5) | collective-permute-done | bytes 262176 | tf_op jit(solution)/shard_map/ppermute | solution.py:252
  26.3 5.2 %source_first.1 = (f32[128,128]{1,0:T(8,128)S(1)}, f32[64,128]{1,0:T(8,128)S(1)}, bf16[128,64,128]{2,1,0:T(8,128)(2,1)S(1)}, bf16[64,64,128]{2,1,0:T(8,128)(2,1)S(1)}) custom-call(s32[3]{0:T(128)S(1)} %pad_add_fusion.2.here, s32[529]{0:T(1024)S(1)} %get-tuple-element.17.tiles_in, f32[64,128]{1,0:T(8,128)S(1)} %bitcast.38, bf16[64,8192]{1,0:T(8,128)(2,1)S(1)} %bitcast.32, ...), custom_call_target="tpu_custom_call" | custom-call | tf_op jit(solution)/shard_map/source_first/pallas_call | solution.py:176
  31.6 1.2 %collective-permute-done.6 = f32[128,128]{1,0:T(8,128)S(1)} collective-permute-done((f32[128,128]{1,0:T(8,128)S(1)}, f32[128,128]{1,0:T(8,128)S(1)}, u32[]{:S(2)}, u32[]{:S(2)}) %collective-permute-start.6) | collective-permute-done | bytes 65568 | tf_op jit(solution)/shard_map/ppermute | solution.py:210
  32.9 2.7 %collective-permute-start.9 = (f32[128,128]{1,0:T(8,128)S(1)}, f32[128,128]{1,0:T(8,128)S(1)}, u32[]{:S(2)}, u32[]{:S(2)}) collective-permute-start(f32[128,128]{1,0:T(8,128)S(1)} %multiply_add_fusion.1.refs_0_), channel_id=1, source_target_pairs={{0,6},{1,7},{2,4},{3,5},{4,2},{5,3},{6,0},{7,1},{8,14},{9,15},{10,... | collective-permute-start | bytes 196616 | tf_op jit(solution)/shard_map/ppermute | solution.py:212
  36.5 1.7 %collective-permute-done.9.refs_3_ = f32[128,128]{1,0:T(8,128)S(1)} collective-permute-done((f32[128,128]{1,0:T(8,128)S(1)}, f32[128,128]{1,0:T(8,128)S(1)}, u32[]{:S(2)}, u32[]{:S(2)}) %collective-permute-start.9) | collective-permute-done | bytes 65568 | tf_op jit(solution)/shard_map/ppermute | solution.py:212
  38.1 1.8 %collective-permute-done.8.refs_2_ = f32[128,128]{1,0:T(8,128)S(1)} collective-permute-done((f32[128,128]{1,0:T(8,128)S(1)}, f32[128,128]{1,0:T(8,128)S(1)}, u32[]{:S(2)}, u32[]{:S(2)}) %collective-permute-start.8) | collective-permute-done | bytes 65568 | tf_op jit(solution)/shard_map/ppermute | solution.py:208
  40.2 4.3 %target_first.1.refs_0_ = f32[64,128]{1,0:T(8,128)S(1)} custom-call(s32[529]{0:T(1024)S(1)} %get-tuple-element.16.tiles_in, f32[128,128]{1,0:T(8,128)S(1)} %multiply_add_fusion.1.refs_0_, f32[128,128]{1,0:T(8,128)S(1)} %collective-permute-done.7.refs_1_, f32[128,128]{1,0:T(8,128)S(1)} %collective-permute-done.8.refs_2_, ...), custom_call_target="tpu_custom_call" | custom-call | tf_op jit(solution)/shard_map/target_first/pallas_call | solution.py:195
  44.5 1.8 %collective-permute-start.12 = (f32[64,128]{1,0:T(8,128)S(1)}, f32[64,128]{1,0:T(8,128)S(1)}, u32[]{:S(2)}, u32[]{:S(2)}) collective-permute-start(f32[64,128]{1,0:T(8,128)S(1)} %target_first.1.refs_0_), channel_id=1, source_target_pairs={{0,24},{4,28},{8,16},{12,20},{16,8},{20,12},{24,0},{28,4},{1,25},{... | collective-permute-start | bytes 98312 | tf_op jit(solution)/shard_map/ppermute | solution.py:208
  46.4 0.8 %collective-permute-start.11 = (f32[64,128]{1,0:T(8,128)S(1)}, f32[64,128]{1,0:T(8,128)S(1)}, u32[]{:S(2)}, u32[]{:S(2)}) collective-permute-start(f32[64,128]{1,0:T(8,128)S(1)} %target_first.1.refs_0_), channel_id=1, source_target_pairs={{0,16},{4,20},{8,24},{12,28},{16,0},{20,4},{24,8},{28,12},{1,17},{... | collective-permute-start | bytes 98312 | tf_op jit(solution)/shard_map/ppermute | solution.py:208
  47.2 1.8 %collective-permute-start.10 = (f32[64,128]{1,0:T(8,128)S(1)}, f32[64,128]{1,0:T(8,128)S(1)}, u32[]{:S(2)}, u32[]{:S(2)}) collective-permute-start(f32[64,128]{1,0:T(8,128)S(1)} %target_first.1.refs_0_), channel_id=1, source_target_pairs={{0,8},{4,12},{8,0},{12,4},{16,24},{20,28},{24,16},{28,20},{1,9},{5... | collective-permute-start | bytes 98312 | tf_op jit(solution)/shard_map/ppermute | solution.py:208
  49.0 1.5 %collective-permute-done.12.refs_3_ = f32[64,128]{1,0:T(8,128)S(1)} collective-permute-done((f32[64,128]{1,0:T(8,128)S(1)}, f32[64,128]{1,0:T(8,128)S(1)}, u32[]{:S(2)}, u32[]{:S(2)}) %collective-permute-start.12) | collective-permute-done | bytes 32800 | tf_op jit(solution)/shard_map/ppermute | solution.py:208
  51.4 4.4 %source_second.1 = f32[128,128]{1,0:T(8,128)S(1)} custom-call(s32[529]{0:T(1024)S(1)} %get-tuple-element.17.tiles_in, f32[64,128]{1,0:T(8,128)S(1)} %target_first.1.refs_0_, f32[64,128]{1,0:T(8,128)S(1)} %collective-permute-done.10.refs_1_, f32[64,128]{1,0:T(8,128)S(1)} %collective-permute-done.11.refs_2_, f32[64,128]{1,0:T(8,128)S(1)} %collective-permute-done.12.refs_3_, ...), custom_call_target="tpu_custom_call" | custom-call | tf_op jit(solution)/shard_map/source_second/pallas_call | solution.py:195
  55.9 1.2 %collective-permute-done.13 = f32[128,128]{1,0:T(8,128)S(1)} collective-permute-done((f32[128,128]{1,0:T(8,128)S(1)}, f32[128,128]{1,0:T(8,128)S(1)}, u32[]{:S(2)}, u32[]{:S(2)}) %collective-permute-start.13) | collective-permute-done | bytes 65568 | tf_op jit(solution)/shard_map/ppermute | solution.py:210
  57.2 1.7 %collective-permute-start.16 = (f32[128,128]{1,0:T(8,128)S(1)}, f32[128,128]{1,0:T(8,128)S(1)}, u32[]{:S(2)}, u32[]{:S(2)}) collective-permute-start(f32[128,128]{1,0:T(8,128)S(1)} %multiply_add_fusion.refs_0_), channel_id=1, source_target_pairs={{0,6},{1,7},{2,4},{3,5},{4,2},{5,3},{6,0},{7,1},{8,14},{9,15},{10,... | collective-permute-start | bytes 196616 | tf_op jit(solution)/shard_map/ppermute | solution.py:212
  59.7 1.1 %collective-permute-start.14 = (f32[128,128]{1,0:T(8,128)S(1)}, f32[128,128]{1,0:T(8,128)S(1)}, u32[]{:S(2)}, u32[]{:S(2)}) collective-permute-start(f32[128,128]{1,0:T(8,128)S(1)} %multiply_add_fusion.refs_0_), channel_id=1, source_target_pairs={{0,2},{1,3},{2,0},{3,1},{4,6},{5,7},{6,4},{7,5},{8,10},{9,11},{10,... | collective-permute-start | bytes 196616 | tf_op jit(solution)/shard_map/ppermute | solution.py:210
  60.8 1.7 %collective-permute-done.16.refs_3_ = f32[128,128]{1,0:T(8,128)S(1)} collective-permute-done((f32[128,128]{1,0:T(8,128)S(1)}, f32[128,128]{1,0:T(8,128)S(1)}, u32[]{:S(2)}, u32[]{:S(2)}) %collective-permute-start.16) | collective-permute-done | bytes 65568 | tf_op jit(solution)/shard_map/ppermute | solution.py:212
  62.5 1.2 %collective-permute-done.15.refs_2_ = f32[128,128]{1,0:T(8,128)S(1)} collective-permute-done((f32[128,128]{1,0:T(8,128)S(1)}, f32[128,128]{1,0:T(8,128)S(1)}, u32[]{:S(2)}, u32[]{:S(2)}) %collective-permute-start.15) | collective-permute-done | bytes 65568 | tf_op jit(solution)/shard_map/ppermute | solution.py:208
  64.0 4.5 %target_second.1 = (f32[64,128]{1,0:T(8,128)S(1)}, f32[128,128]{1,0:T(8,128)S(1)}) custom-call(s32[529]{0:T(1024)S(1)} %get-tuple-element.16.tiles_in, f32[128,128]{1,0:T(8,128)S(1)} %multiply_add_fusion.refs_0_, f32[128,128]{1,0:T(8,128)S(1)} %collective-permute-done.14.refs_1_, f32[128,128]{1,0:T(8,128)S(1)} %collective-permute-done.15.refs_2_, ...), custom_call_target="tpu_custom_call" | custom-call | tf_op jit(solution)/shard_map/target_second/pallas_call | solution.py:195
  68.5 1.1 %collective-permute-start.17 = (f32[64,128]{1,0:T(8,128)S(1)}, f32[64,128]{1,0:T(8,128)S(1)}, u32[]{:S(2)}, u32[]{:S(2)}) collective-permute-start(f32[64,128]{1,0:T(8,128)S(1)} %add_subtract_fusion), channel_id=1, source_target_pairs={{0,8},{4,12},{8,0},{12,4},{16,24},{20,28},{24,16},{28,20},{1,9},{5... | collective-permute-start | bytes 98312 | tf_op jit(solution)/shard_map/ppermute | solution.py:208
  69.8 2.6 %collective-permute-done.17 = f32[64,128]{1,0:T(8,128)S(1)} collective-permute-done((f32[64,128]{1,0:T(8,128)S(1)}, f32[64,128]{1,0:T(8,128)S(1)}, u32[]{:S(2)}, u32[]{:S(2)}) %collective-permute-start.17) | collective-permute-done | bytes 32800 | tf_op jit(solution)/shard_map/ppermute | solution.py:208
  72.5 0.9 %collective-permute-start.19 = (f32[64,128]{1,0:T(8,128)S(1)}, f32[64,128]{1,0:T(8,128)S(1)}, u32[]{:S(2)}, u32[]{:S(2)}) collective-permute-start(f32[64,128]{1,0:T(8,128)S(1)} %multiply_add_fusion.4), channel_id=1, source_target_pairs={{0,4},{4,0},{8,12},{12,8},{16,20},{20,16},{24,28},{28,24},{1,5},{5... | collective-permute-start | bytes 98312 | tf_op jit(solution)/shard_map/ppermute | solution.py:208
  73.4 1.5 %collective-permute-start.20 = (f32[64,128]{1,0:T(8,128)S(1)}, f32[64,128]{1,0:T(8,128)S(1)}, u32[]{:S(2)}, u32[]{:S(2)}) collective-permute-start(f32[64,128]{1,0:T(8,128)S(1)} %multiply_add_fusion.4), channel_id=1, source_target_pairs={{0,20},{4,16},{8,28},{12,24},{16,4},{20,0},{24,12},{28,8},{1,21},{... | collective-permute-start | bytes 98312 | tf_op jit(solution)/shard_map/ppermute | solution.py:208
  74.9 2.0 %collective-permute-start.18 = (f32[64,128]{1,0:T(8,128)S(1)}, f32[64,128]{1,0:T(8,128)S(1)}, u32[]{:S(2)}, u32[]{:S(2)}) collective-permute-start(f32[64,128]{1,0:T(8,128)S(1)} %multiply_add_fusion.4), channel_id=1, source_target_pairs={{0,16},{4,20},{8,24},{12,28},{16,0},{20,4},{24,8},{28,12},{1,17},{... | collective-permute-start | bytes 98312 | tf_op jit(solution)/shard_map/ppermute | solution.py:208
  77.6 1.5 %collective-permute-done.20 = f32[64,128]{1,0:T(8,128)S(1)} collective-permute-done((f32[64,128]{1,0:T(8,128)S(1)}, f32[64,128]{1,0:T(8,128)S(1)}, u32[]{:S(2)}, u32[]{:S(2)}) %collective-permute-start.20) | collective-permute-done | bytes 32800 | tf_op jit(solution)/shard_map/ppermute | solution.py:208
  (51 shorter events, 11.0 us)
Async XLA Ops:
  0.6 9.6 %copy-start = (f32[16384]{0:T(1024)S(1)}, f32[16384]{0:T(1024)}, u32[]{:S(2)}) copy-start(f32[16384]{0:T(1024)} %param.11) | copy-start | bytes 196612
  0.6 25.6 %copy-start.2 = (bf16[2048,64]{0,1:T(8,128)(2,1)S(1)}, bf16[2048,64]{0,1:T(8,128)(2,1)}, u32[]{:S(2)}) copy-start(bf16[2048,64]{0,1:T(8,128)(2,1)} %param.8) | copy-start | bytes 786436
  0.7 25.6 %copy-start.1 = (bf16[8192,64]{0,1:T(8,128)(2,1)S(1)}, bf16[8192,64]{0,1:T(8,128)(2,1)}, u32[]{:S(2)}) copy-start(bf16[8192,64]{0,1:T(8,128)(2,1)} %param.7) | copy-start | bytes 3145732
  0.7 23.0 %collective-permute-start.4 = (bf16[64,2048]{1,0:T(8,128)(2,1)}, bf16[64,2048]{1,0:T(8,128)(2,1)S(1)}, u32[]{:S(2)}, u32[]{:S(2)}) collective-permute-start(bf16[64,2048]{1,0:T(8,128)(2,1)} %bitcast.35), channel_id=1, source_target_pairs={{16,0},{20,4},{0,8},{4,12},{24,16},{28,20},{8,24},{12,28},{17,1},{... | collective-permute-start | bytes 786440 | tf_op jit(solution)/shard_map/ppermute | solution.py:256
  3.7 13.1 %collective-permute-start.1 = (bf16[64,2048]{1,0:T(8,128)(2,1)}, bf16[64,2048]{1,0:T(8,128)(2,1)S(1)}, u32[]{:S(2)}, u32[]{:S(2)}) collective-permute-start(bf16[64,2048]{1,0:T(8,128)(2,1)} %bitcast.36), channel_id=1, source_target_pairs={{0,16},{4,20},{8,0},{12,4},{16,24},{20,28},{24,8},{28,12},{1,17},{... | collective-permute-start | bytes 786440 | tf_op jit(solution)/shard_map/ppermute | solution.py:252
  7.1 4.3 %collective-permute-start = (f32[64,132]{1,0:T(8,128)S(1)}, f32[64,132]{1,0:T(8,128)S(1)}, u32[]{:S(2)}, u32[]{:S(2)}) collective-permute-start(f32[64,132]{1,0:T(8,128)S(1)} %pad_maximum_fusion.1), channel_id=1, source_target_pairs={{0,4},{4,0},{8,12},{12,8},{16,20},{20,16},{24,28},{28,24},{1,5},{5... | collective-permute-start | bytes 101384 | tf_op jit(solution)/shard_map/ppermute | solution.py:208
  10.0 12.9 %collective-permute-start.2 = (bf16[64,4096]{1,0:T(8,128)(2,1)S(1)}, bf16[64,4096]{1,0:T(8,128)(2,1)S(1)}, u32[]{:S(2)}, u32[]{:S(2)}) collective-permute-start(bf16[64,4096]{1,0:T(8,128)(2,1)S(1)} %constant_dynamic-slice_fusion.1), channel_id=1, source_target_pairs={{0,4},{4,0},{8,12},{12,8},{16,20},{20,16},{24,28},{28,24},{1,5},{5... | collective-permute-start | bytes 1572872 | tf_op jit(solution)/shard_map/ppermute | solution.py:208
  18.0 8.3 %collective-permute-start.5 = (bf16[64,2048]{1,0:T(8,128)(2,1)S(1)}, bf16[64,2048]{1,0:T(8,128)(2,1)S(1)}, u32[]{:S(2)}, u32[]{:S(2)}) collective-permute-start(bf16[64,2048]{1,0:T(8,128)(2,1)S(1)} %collective-permute-done.1.refs_4_), channel_id=1, source_target_pairs={{0,16},{4,20},{8,0},{12,4},{16,24},{20,28},{24,8},{28,12},{1,17},{... | collective-permute-start | bytes 786440 | tf_op jit(solution)/shard_map/ppermute | solution.py:252
  22.9 3.4 %collective-permute-start.3 = (bf16[64,4096]{1,0:T(8,128)(2,1)S(1)}, bf16[64,4096]{1,0:T(8,128)(2,1)S(1)}, u32[]{:S(2)}, u32[]{:S(2)}) collective-permute-start(bf16[64,4096]{1,0:T(8,128)(2,1)S(1)} %collective-permute-done.2.refs_1_), channel_id=1, source_target_pairs={{0,1},{1,0},{2,3},{3,2},{4,5},{5,4},{6,7},{7,6},{8,9},{9,8},{10,11... | collective-permute-start | bytes 1572872 | tf_op jit(solution)/shard_map/ppermute | solution.py:210
  31.5 17.5 %copy-start.3 = (f32[16384]{0:T(1024)S(1)}, f32[16384]{0:T(1024)}, u32[]{:S(2)}) copy-start(f32[16384]{0:T(1024)} %param.10) | copy-start | bytes 196612
  31.5 1.3 %collective-permute-start.6 = (f32[128,128]{1,0:T(8,128)S(1)}, f32[128,128]{1,0:T(8,128)S(1)}, u32[]{:S(2)}, u32[]{:S(2)}) collective-permute-start(f32[128,128]{1,0:T(8,128)S(1)} %get-tuple-element.20), channel_id=1, source_target_pairs={{0,1},{1,0},{2,3},{3,2},{4,5},{5,4},{6,7},{7,6},{8,9},{9,8},{10,11... | collective-permute-start | bytes 196616 | tf_op jit(solution)/shard_map/ppermute | solution.py:210
  32.9 5.2 %collective-permute-start.9 = (f32[128,128]{1,0:T(8,128)S(1)}, f32[128,128]{1,0:T(8,128)S(1)}, u32[]{:S(2)}, u32[]{:S(2)}) collective-permute-start(f32[128,128]{1,0:T(8,128)S(1)} %multiply_add_fusion.1.refs_0_), channel_id=1, source_target_pairs={{0,6},{1,7},{2,4},{3,5},{4,2},{5,3},{6,0},{7,1},{8,14},{9,15},{10,... | collective-permute-start | bytes 196616 | tf_op jit(solution)/shard_map/ppermute | solution.py:212
  35.6 4.3 %collective-permute-start.8 = (f32[128,128]{1,0:T(8,128)S(1)}, f32[128,128]{1,0:T(8,128)S(1)}, u32[]{:S(2)}, u32[]{:S(2)}) collective-permute-start(f32[128,128]{1,0:T(8,128)S(1)} %multiply_add_fusion.1.refs_0_), channel_id=1, source_target_pairs={{0,4},{4,0},{8,12},{12,8},{16,20},{20,16},{24,28},{28,24},{1,5},{5... | collective-permute-start | bytes 196616 | tf_op jit(solution)/shard_map/ppermute | solution.py:208
  36.0 4.3 %collective-permute-start.7 = (f32[128,128]{1,0:T(8,128)S(1)}, f32[128,128]{1,0:T(8,128)S(1)}, u32[]{:S(2)}, u32[]{:S(2)}) collective-permute-start(f32[128,128]{1,0:T(8,128)S(1)} %multiply_add_fusion.1.refs_0_), channel_id=1, source_target_pairs={{0,2},{1,3},{2,0},{3,1},{4,6},{5,7},{6,4},{7,5},{8,10},{9,11},{10,... | collective-permute-start | bytes 196616 | tf_op jit(solution)/shard_map/ppermute | solution.py:210
  44.5 6.0 %collective-permute-start.12 = (f32[64,128]{1,0:T(8,128)S(1)}, f32[64,128]{1,0:T(8,128)S(1)}, u32[]{:S(2)}, u32[]{:S(2)}) collective-permute-start(f32[64,128]{1,0:T(8,128)S(1)} %target_first.1.refs_0_), channel_id=1, source_target_pairs={{0,24},{4,28},{8,16},{12,20},{16,8},{20,12},{24,0},{28,4},{1,25},{... | collective-permute-start | bytes 98312 | tf_op jit(solution)/shard_map/ppermute | solution.py:208
  46.4 4.9 %collective-permute-start.11 = (f32[64,128]{1,0:T(8,128)S(1)}, f32[64,128]{1,0:T(8,128)S(1)}, u32[]{:S(2)}, u32[]{:S(2)}) collective-permute-start(f32[64,128]{1,0:T(8,128)S(1)} %target_first.1.refs_0_), channel_id=1, source_target_pairs={{0,16},{4,20},{8,24},{12,28},{16,0},{20,4},{24,8},{28,12},{1,17},{... | collective-permute-start | bytes 98312 | tf_op jit(solution)/shard_map/ppermute | solution.py:208
  47.2 4.3 %collective-permute-start.10 = (f32[64,128]{1,0:T(8,128)S(1)}, f32[64,128]{1,0:T(8,128)S(1)}, u32[]{:S(2)}, u32[]{:S(2)}) collective-permute-start(f32[64,128]{1,0:T(8,128)S(1)} %target_first.1.refs_0_), channel_id=1, source_target_pairs={{0,8},{4,12},{8,0},{12,4},{16,24},{20,28},{24,16},{28,20},{1,9},{5... | collective-permute-start | bytes 98312 | tf_op jit(solution)/shard_map/ppermute | solution.py:208
  55.9 1.3 %collective-permute-start.13 = (f32[128,128]{1,0:T(8,128)S(1)}, f32[128,128]{1,0:T(8,128)S(1)}, u32[]{:S(2)}, u32[]{:S(2)}) collective-permute-start(f32[128,128]{1,0:T(8,128)S(1)} %source_second.1), channel_id=1, source_target_pairs={{0,1},{1,0},{2,3},{3,2},{4,5},{5,4},{6,7},{7,6},{8,9},{9,8},{10,11... | collective-permute-start | bytes 196616 | tf_op jit(solution)/shard_map/ppermute | solution.py:210
  57.2 5.3 %collective-permute-start.16 = (f32[128,128]{1,0:T(8,128)S(1)}, f32[128,128]{1,0:T(8,128)S(1)}, u32[]{:S(2)}, u32[]{:S(2)}) collective-permute-start(f32[128,128]{1,0:T(8,128)S(1)} %multiply_add_fusion.refs_0_), channel_id=1, source_target_pairs={{0,6},{1,7},{2,4},{3,5},{4,2},{5,3},{6,0},{7,1},{8,14},{9,15},{10,... | collective-permute-start | bytes 196616 | tf_op jit(solution)/shard_map/ppermute | solution.py:212
  58.9 4.8 %collective-permute-start.15 = (f32[128,128]{1,0:T(8,128)S(1)}, f32[128,128]{1,0:T(8,128)S(1)}, u32[]{:S(2)}, u32[]{:S(2)}) collective-permute-start(f32[128,128]{1,0:T(8,128)S(1)} %multiply_add_fusion.refs_0_), channel_id=1, source_target_pairs={{0,4},{4,0},{8,12},{12,8},{16,20},{20,16},{24,28},{28,24},{1,5},{5... | collective-permute-start | bytes 196616 | tf_op jit(solution)/shard_map/ppermute | solution.py:208
  59.7 4.3 %collective-permute-start.14 = (f32[128,128]{1,0:T(8,128)S(1)}, f32[128,128]{1,0:T(8,128)S(1)}, u32[]{:S(2)}, u32[]{:S(2)}) collective-permute-start(f32[128,128]{1,0:T(8,128)S(1)} %multiply_add_fusion.refs_0_), channel_id=1, source_target_pairs={{0,2},{1,3},{2,0},{3,1},{4,6},{5,7},{6,4},{7,5},{8,10},{9,11},{10,... | collective-permute-start | bytes 196616 | tf_op jit(solution)/shard_map/ppermute | solution.py:210
  68.5 4.0 %collective-permute-start.17 = (f32[64,128]{1,0:T(8,128)S(1)}, f32[64,128]{1,0:T(8,128)S(1)}, u32[]{:S(2)}, u32[]{:S(2)}) collective-permute-start(f32[64,128]{1,0:T(8,128)S(1)} %add_subtract_fusion), channel_id=1, source_target_pairs={{0,8},{4,12},{8,0},{12,4},{16,24},{20,28},{24,16},{28,20},{1,9},{5... | collective-permute-start | bytes 98312 | tf_op jit(solution)/shard_map/ppermute | solution.py:208
  72.5 5.1 %collective-permute-start.19 = (f32[64,128]{1,0:T(8,128)S(1)}, f32[64,128]{1,0:T(8,128)S(1)}, u32[]{:S(2)}, u32[]{:S(2)}) collective-permute-start(f32[64,128]{1,0:T(8,128)S(1)} %multiply_add_fusion.4), channel_id=1, source_target_pairs={{0,4},{4,0},{8,12},{12,8},{16,20},{20,16},{24,28},{28,24},{1,5},{5... | collective-permute-start | bytes 98312 | tf_op jit(solution)/shard_map/ppermute | solution.py:208
  73.4 5.7 %collective-permute-start.20 = (f32[64,128]{1,0:T(8,128)S(1)}, f32[64,128]{1,0:T(8,128)S(1)}, u32[]{:S(2)}, u32[]{:S(2)}) collective-permute-start(f32[64,128]{1,0:T(8,128)S(1)} %multiply_add_fusion.4), channel_id=1, source_target_pairs={{0,20},{4,16},{8,28},{12,24},{16,4},{20,0},{24,12},{28,8},{1,21},{... | collective-permute-start | bytes 98312 | tf_op jit(solution)/shard_map/ppermute | solution.py:208
  74.9 4.8 %collective-permute-start.18 = (f32[64,128]{1,0:T(8,128)S(1)}, f32[64,128]{1,0:T(8,128)S(1)}, u32[]{:S(2)}, u32[]{:S(2)}) collective-permute-start(f32[64,128]{1,0:T(8,128)S(1)} %multiply_add_fusion.4), channel_id=1, source_target_pairs={{0,16},{4,20},{8,24},{12,28},{16,0},{20,4},{24,8},{28,12},{1,17},{... | collective-permute-start | bytes 98312 | tf_op jit(solution)/shard_map/ppermute | solution.py:208

commit v7 on v6

--- a/solution.py
+++ b/solution.py
@@ -222,11 +222,13 @@
     return [value, swap_by(value, *first), swap_by(value, *second), swap_by(value, *diagonal)]
 
 
-def tile_list(code, alive, parts, after):
-    slots = code.shape[0]
-    code = jnp.where(alive, code, (1 << 30) + jnp.arange(slots, dtype=jnp.int32))
-    rank = jnp.sum((code[None, :] < code[:, None]).astype(jnp.int32), axis=1)
-    places = jnp.arange(slots, dtype=jnp.int32)
+def ranked(code, alive):
+    code = jnp.where(alive, code, (1 << 30) + jnp.arange(code.shape[0], dtype=jnp.int32))
+    return code, jnp.sum((code[None, :] < code[:, None]).astype(jnp.int32), axis=1)
+
+
+def tile_list(code, rank, alive, parts, after):
+    places = jnp.arange(code.shape[0], dtype=jnp.int32)
     hit = (rank[None, :] == places[:, None]) & alive[None, :]
     ordered = jnp.sum(jnp.where(hit, code[None, :] - after, 0), axis=1) + after
     return place * (ordered // parts) + ordered % parts
@@ -271,7 +273,6 @@
     part = swap_by(part, 1, 0)
     srcs = [xt, part, swap_by(part, 0, 1)]
 
-    theirs, tgts[1] = lax.optimization_barrier((theirs, tgts[1]))
     pair = jnp.concatenate([jnp.where(side == 0, mine, theirs), jnp.where(side == 0, theirs, mine)])
     s_mass = pair[:, :BLOCK]
     named = pair[:, BLOCK:].astype(jnp.int32).reshape(slots)
@@ -284,9 +285,12 @@
     s_ids = jnp.arange(slots, dtype=jnp.int32) // depth
     live = jnp.sum(alive.astype(jnp.int32)).reshape(1)
     last = jnp.full((pad,), place, jnp.int32)
-    by_source = tile_list(s_ids * targets + t_ids, alive, targets, sources * targets)
+    s_code, s_rank = ranked(s_ids * targets + t_ids, alive)
+    t_code, t_rank = ranked(t_ids * sources + s_ids, alive)
+    s_rank, t_rank, tgts[1] = lax.optimization_barrier((s_rank, t_rank, tgts[1]))
+    by_source = tile_list(s_code, s_rank, alive, targets, sources * targets)
     by_source = jnp.concatenate([live, by_source, last * sources])
-    by_target = tile_list(t_ids * sources + s_ids, alive, sources, sources * targets)
+    by_target = tile_list(t_code, t_rank, alive, sources, sources * targets)
     by_target = jnp.concatenate([live, by_target, last * targets])
     by_source, by_target = lax.optimization_barrier((by_source, by_target))
     t_mass = of_side(target_mass)

time: 81.1 us -> 81.3 us (level)
  waiting for transfers between devices: 28.2 us -> 29.6 us
    ppermute x11, waiting for transfers between devices: 13.6 us -> 17.7 us  [swap(): return lax.ppermute(value, 'row', [(i, i ^ row_bit) for i in range(rows)])]
    ppermute x2, waiting for transfers between devices: 8.17 us -> 5.62 us  [shards(): ahead = lax.ppermute(ahead, 'row', onward)]
    ppermute x11, starting transfers between devices: 13.2 us -> 12 us  [swap(): return lax.ppermute(value, 'row', [(i, i ^ row_bit) for i in range(rows)])]
  transfers between devices with their start and end apart: 21 -> 21, of which waited for: 18 -> 16; matrix products, arithmetic and copies ran while one was open for 9% -> 9% of each run, Pallas kernels for 0% -> 0%
where the time goes in v7:
time: 81.3 us; the launch traced here: 81 us
  waiting for transfers between devices  29.6 us (36%)
  starting transfers between devices  24.5 us (30%)
  Pallas kernels  18.4 us (23%)
  other arithmetic  5.79 us (7%)
  local copies, waits for them, and re-layouts  1.99 us (2%)
    ppermute x11, waiting for transfers between devices, swap(): return lax.ppermute(value, 'row', [(i, i ^ row_bit) for i in range(rows)])  17.7 us
    pallas_call x3, Pallas kernels, later_pass(): pl.pallas_call(functools.partial(later_kernel, len(parts), keep), out_sha...  13.2 us
    ppermute x11, starting transfers between devices, swap(): return lax.ppermute(value, 'row', [(i, i ^ row_bit) for i in range(rows)])  12 us
    ppermute x2, waiting for transfers between devices, shards(): ahead = lax.ppermute(ahead, 'row', onward)  5.62 us
    pallas_call x1, Pallas kernels, first_pass(): pl.pallas_call(functools.partial(first_kernel, n_src, n_tgt, targets * BL...  5.21 us
    ppermute x2, starting transfers between devices, swap(): return lax.ppermute(value, ('row', 'col'), pairs)  4.56 us
    ppermute x2, waiting for transfers between devices, swap(): return lax.ppermute(value, ('row', 'col'), pairs)  3.4 us
    ppermute x1, starting transfers between devices, shards(): behind = lax.ppermute(behind, 'row', back)  3.08 us
  transfers between devices with their start and end apart: 21, of which 16 were waited for; matrix products, arithmetic and copies ran while one was open for 9% of the time, Pallas kernels for 0%

profile of v7, /device:TPU:0, one launch (start us, length us, event | category | flops | bytes accessed | tf_op | source)
XLA Modules:
  0.0 81.0 jit_solution(912852049276916268)
XLA Ops:
  0.7 3.1 %collective-permute-start.4 = (bf16[64,2048]{1,0:T(8,128)(2,1)}, bf16[64,2048]{1,0:T(8,128)(2,1)S(1)}, u32[]{:S(2)}, u32[]{:S(2)}) collective-permute-start(bf16[64,2048]{1,0:T(8,128)(2,1)} %bitcast.35), channel_id=1, source_target_pairs={{16,0},{20,4},{0,8},{4,12},{24,16},{28,20},{8,24},{12,28},{17,1},{... | collective-permute-start | bytes 786440 | tf_op jit(solution)/shard_map/ppermute | solution.py:258
  3.7 1.1 %collective-permute-start.1 = (bf16[64,2048]{1,0:T(8,128)(2,1)}, bf16[64,2048]{1,0:T(8,128)(2,1)S(1)}, u32[]{:S(2)}, u32[]{:S(2)}) collective-permute-start(bf16[64,2048]{1,0:T(8,128)(2,1)} %bitcast.36), channel_id=1, source_target_pairs={{0,16},{4,20},{8,0},{12,4},{16,24},{20,28},{24,8},{28,12},{1,17},{... | collective-permute-start | bytes 786440 | tf_op jit(solution)/shard_map/ppermute | solution.py:254
  4.8 0.8 copy.13
  7.1 1.8 %collective-permute-start = (f32[64,132]{1,0:T(8,128)S(1)}, f32[64,132]{1,0:T(8,128)S(1)}, u32[]{:S(2)}, u32[]{:S(2)}) collective-permute-start(f32[64,132]{1,0:T(8,128)S(1)} %pad_maximum_fusion.1), channel_id=1, source_target_pairs={{0,4},{4,0},{8,12},{12,8},{16,20},{20,16},{24,28},{28,24},{1,5},{5... | collective-permute-start | bytes 101384 | tf_op jit(solution)/shard_map/ppermute | solution.py:208
  8.9 1.1 %constant_dynamic-slice_fusion.1 = bf16[64,4096]{1,0:T(8,128)(2,1)S(1)} fusion(bf16[64,8192]{1,0:T(8,128)(2,1)} %bitcast.31, s32[]{:T(128)S(6)} %select_n.283), kind=kLoop, calls=%fused_computation.119 | loop fusion | bytes 1048580 | tf_op jit(solution)/shard_map/dynamic_slice | solution.py:272
  10.3 1.0 %collective-permute-done = f32[64,132]{1,0:T(8,128)S(1)} collective-permute-done((f32[64,132]{1,0:T(8,128)S(1)}, f32[64,132]{1,0:T(8,128)S(1)}, u32[]{:S(2)}, u32[]{:S(2)}) %collective-permute-start) | collective-permute-done | bytes 33824 | tf_op jit(solution)/shard_map/ppermute | solution.py:208
  12.7 4.1 %collective-permute-done.1.refs_4_ = bf16[64,2048]{1,0:T(8,128)(2,1)S(1)} collective-permute-done((bf16[64,2048]{1,0:T(8,128)(2,1)}, bf16[64,2048]{1,0:T(8,128)(2,1)S(1)}, u32[]{:S(2)}, u32[]{:S(2)}) %collective-permute-start.1) | collective-permute-done | bytes 262176 | tf_op jit(solution)/shard_map/ppermute | solution.py:254
  16.9 1.7 %collective-permute-start.5 = (bf16[64,2048]{1,0:T(8,128)(2,1)S(1)}, bf16[64,2048]{1,0:T(8,128)(2,1)S(1)}, u32[]{:S(2)}, u32[]{:S(2)}) collective-permute-start(bf16[64,2048]{1,0:T(8,128)(2,1)S(1)} %collective-permute-done.1.refs_4_), channel_id=1, source_target_pairs={{0,16},{4,20},{8,0},{12,4},{16,24},{20,28},{24,8},{28,12},{1,17},{... | collective-permute-start | bytes 786440 | tf_op jit(solution)/shard_map/ppermute | solution.py:254
  19.1 3.7 %collective-permute-done.2.refs_1_ = bf16[64,4096]{1,0:T(8,128)(2,1)S(1)} collective-permute-done((bf16[64,4096]{1,0:T(8,128)(2,1)S(1)}, bf16[64,4096]{1,0:T(8,128)(2,1)S(1)}, u32[]{:S(2)}, u32[]{:S(2)}) %collective-permute-start.2) | collective-permute-done | bytes 524320 | tf_op jit(solution)/shard_map/ppermute | solution.py:208
  23.6 1.5 %collective-permute-done.5.refs_6_ = bf16[64,2048]{1,0:T(8,128)(2,1)S(1)} collective-permute-done((bf16[64,2048]{1,0:T(8,128)(2,1)S(1)}, bf16[64,2048]{1,0:T(8,128)(2,1)S(1)}, u32[]{:S(2)}, u32[]{:S(2)}) %collective-permute-start.5) | collective-permute-done | bytes 262176 | tf_op jit(solution)/shard_map/ppermute | solution.py:254
  25.1 5.2 %source_first.1 = (f32[128,128]{1,0:T(8,128)S(1)}, f32[64,128]{1,0:T(8,128)S(1)}, bf16[128,64,128]{2,1,0:T(8,128)(2,1)S(1)}, bf16[64,64,128]{2,1,0:T(8,128)(2,1)S(1)}) custom-call(s32[3]{0:T(128)S(1)} %pad_add_fusion.2.here, s32[529]{0:T(1024)S(1)} %get-tuple-element.19.tiles_in, f32[64,128]{1,0:T(8,128)S(1)} %bitcast.38, bf16[64,8192]{1,0:T(8,128)(2,1)S(1)} %bitcast.32, ...), custom_call_target="tpu_custom_call" | custom-call | tf_op jit(solution)/shard_map/source_first/pallas_call | solution.py:176
  30.4 1.2 %collective-permute-done.6 = f32[128,128]{1,0:T(8,128)S(1)} collective-permute-done((f32[128,128]{1,0:T(8,128)S(1)}, f32[128,128]{1,0:T(8,128)S(1)}, u32[]{:S(2)}, u32[]{:S(2)}) %collective-permute-start.6) | collective-permute-done | bytes 65568 | tf_op jit(solution)/shard_map/ppermute | solution.py:210
  31.7 2.7 %collective-permute-start.9 = (f32[128,128]{1,0:T(8,128)S(1)}, f32[128,128]{1,0:T(8,128)S(1)}, u32[]{:S(2)}, u32[]{:S(2)}) collective-permute-start(f32[128,128]{1,0:T(8,128)S(1)} %multiply_add_fusion.1.refs_0_), channel_id=1, source_target_pairs={{0,6},{1,7},{2,4},{3,5},{4,2},{5,3},{6,0},{7,1},{8,14},{9,15},{10,... | collective-permute-start | bytes 196616 | tf_op jit(solution)/shard_map/ppermute | solution.py:212
  35.3 1.7 %collective-permute-done.9.refs_3_ = f32[128,128]{1,0:T(8,128)S(1)} collective-permute-done((f32[128,128]{1,0:T(8,128)S(1)}, f32[128,128]{1,0:T(8,128)S(1)}, u32[]{:S(2)}, u32[]{:S(2)}) %collective-permute-start.9) | collective-permute-done | bytes 65568 | tf_op jit(solution)/shard_map/ppermute | solution.py:212
  37.0 1.8 %collective-permute-done.8.refs_2_ = f32[128,128]{1,0:T(8,128)S(1)} collective-permute-done((f32[128,128]{1,0:T(8,128)S(1)}, f32[128,128]{1,0:T(8,128)S(1)}, u32[]{:S(2)}, u32[]{:S(2)}) %collective-permute-start.8) | collective-permute-done | bytes 65568 | tf_op jit(solution)/shard_map/ppermute | solution.py:208
  39.1 4.3 %target_first.1.refs_0_ = f32[64,128]{1,0:T(8,128)S(1)} custom-call(s32[529]{0:T(1024)S(1)} %get-tuple-element.18.tiles_in, f32[128,128]{1,0:T(8,128)S(1)} %multiply_add_fusion.1.refs_0_, f32[128,128]{1,0:T(8,128)S(1)} %collective-permute-done.7.refs_1_, f32[128,128]{1,0:T(8,128)S(1)} %collective-permute-done.8.refs_2_, ...), custom_call_target="tpu_custom_call" | custom-call | tf_op jit(solution)/shard_map/target_first/pallas_call | solution.py:195
  43.4 2.8 %collective-permute-start.12 = (f32[64,128]{1,0:T(8,128)S(1)}, f32[64,128]{1,0:T(8,128)S(1)}, u32[]{:S(2)}, u32[]{:S(2)}) collective-permute-start(f32[64,128]{1,0:T(8,128)S(1)} %target_first.1.refs_0_), channel_id=1, source_target_pairs={{0,24},{4,28},{8,16},{12,20},{16,8},{20,12},{24,0},{28,4},{1,25},{... | collective-permute-start | bytes 98312 | tf_op jit(solution)/shard_map/ppermute | solution.py:208
  46.2 1.6 %collective-permute-start.10 = (f32[64,128]{1,0:T(8,128)S(1)}, f32[64,128]{1,0:T(8,128)S(1)}, u32[]{:S(2)}, u32[]{:S(2)}) collective-permute-start(f32[64,128]{1,0:T(8,128)S(1)} %target_first.1.refs_0_), channel_id=1, source_target_pairs={{0,8},{4,12},{8,0},{12,4},{16,24},{20,28},{24,16},{28,20},{1,9},{5... | collective-permute-start | bytes 98312 | tf_op jit(solution)/shard_map/ppermute | solution.py:208
  47.8 1.3 %collective-permute-done.12.refs_3_ = f32[64,128]{1,0:T(8,128)S(1)} collective-permute-done((f32[64,128]{1,0:T(8,128)S(1)}, f32[64,128]{1,0:T(8,128)S(1)}, u32[]{:S(2)}, u32[]{:S(2)}) %collective-permute-start.12) | collective-permute-done | bytes 32800 | tf_op jit(solution)/shard_map/ppermute | solution.py:208
  49.2 1.8 %collective-permute-done.11.refs_2_ = f32[64,128]{1,0:T(8,128)S(1)} collective-permute-done((f32[64,128]{1,0:T(8,128)S(1)}, f32[64,128]{1,0:T(8,128)S(1)}, u32[]{:S(2)}, u32[]{:S(2)}) %collective-permute-start.11) | collective-permute-done | bytes 32800 | tf_op jit(solution)/shard_map/ppermute | solution.py:208
  51.0 4.4 %source_second.1 = f32[128,128]{1,0:T(8,128)S(1)} custom-call(s32[529]{0:T(1024)S(1)} %get-tuple-element.19.tiles_in, f32[64,128]{1,0:T(8,128)S(1)} %target_first.1.refs_0_, f32[64,128]{1,0:T(8,128)S(1)} %collective-permute-done.10.refs_1_, f32[64,128]{1,0:T(8,128)S(1)} %collective-permute-done.11.refs_2_, f32[64,128]{1,0:T(8,128)S(1)} %collective-permute-done.12.refs_3_, ...), custom_call_target="tpu_custom_call" | custom-call | tf_op jit(solution)/shard_map/source_second/pallas_call | solution.py:195
  55.5 1.2 %collective-permute-done.13 = f32[128,128]{1,0:T(8,128)S(1)} collective-permute-done((f32[128,128]{1,0:T(8,128)S(1)}, f32[128,128]{1,0:T(8,128)S(1)}, u32[]{:S(2)}, u32[]{:S(2)}) %collective-permute-start.13) | collective-permute-done | bytes 65568 | tf_op jit(solution)/shard_map/ppermute | solution.py:210
  56.8 1.8 %collective-permute-start.16 = (f32[128,128]{1,0:T(8,128)S(1)}, f32[128,128]{1,0:T(8,128)S(1)}, u32[]{:S(2)}, u32[]{:S(2)}) collective-permute-start(f32[128,128]{1,0:T(8,128)S(1)} %multiply_add_fusion.refs_0_), channel_id=1, source_target_pairs={{0,6},{1,7},{2,4},{3,5},{4,2},{5,3},{6,0},{7,1},{8,14},{9,15},{10,... | collective-permute-start | bytes 196616 | tf_op jit(solution)/shard_map/ppermute | solution.py:212
  58.9 1.4 %collective-permute-start.14 = (f32[128,128]{1,0:T(8,128)S(1)}, f32[128,128]{1,0:T(8,128)S(1)}, u32[]{:S(2)}, u32[]{:S(2)}) collective-permute-start(f32[128,128]{1,0:T(8,128)S(1)} %multiply_add_fusion.refs_0_), channel_id=1, source_target_pairs={{0,2},{1,3},{2,0},{3,1},{4,6},{5,7},{6,4},{7,5},{8,10},{9,11},{10,... | collective-permute-start | bytes 196616 | tf_op jit(solution)/shard_map/ppermute | solution.py:210
  60.3 1.7 %collective-permute-done.16.refs_3_ = f32[128,128]{1,0:T(8,128)S(1)} collective-permute-done((f32[128,128]{1,0:T(8,128)S(1)}, f32[128,128]{1,0:T(8,128)S(1)}, u32[]{:S(2)}, u32[]{:S(2)}) %collective-permute-start.16) | collective-permute-done | bytes 65568 | tf_op jit(solution)/shard_map/ppermute | solution.py:212
  62.1 1.2 %collective-permute-done.15.refs_2_ = f32[128,128]{1,0:T(8,128)S(1)} collective-permute-done((f32[128,128]{1,0:T(8,128)S(1)}, f32[128,128]{1,0:T(8,128)S(1)}, u32[]{:S(2)}, u32[]{:S(2)}) %collective-permute-start.15) | collective-permute-done | bytes 65568 | tf_op jit(solution)/shard_map/ppermute | solution.py:208
  63.3 4.5 %target_second.1 = (f32[64,128]{1,0:T(8,128)S(1)}, f32[128,128]{1,0:T(8,128)S(1)}) custom-call(s32[529]{0:T(1024)S(1)} %get-tuple-element.18.tiles_in, f32[128,128]{1,0:T(8,128)S(1)} %multiply_add_fusion.refs_0_, f32[128,128]{1,0:T(8,128)S(1)} %collective-permute-done.14.refs_1_, f32[128,128]{1,0:T(8,128)S(1)} %collective-permute-done.15.refs_2_, ...), custom_call_target="tpu_custom_call" | custom-call | tf_op jit(solution)/shard_map/target_second/pallas_call | solution.py:195
  68.5 3.3 %collective-permute-done.17 = f32[64,128]{1,0:T(8,128)S(1)} collective-permute-done((f32[64,128]{1,0:T(8,128)S(1)}, f32[64,128]{1,0:T(8,128)S(1)}, u32[]{:S(2)}, u32[]{:S(2)}) %collective-permute-start.17) | collective-permute-done | bytes 32800 | tf_op jit(solution)/shard_map/ppermute | solution.py:208
  71.8 1.2 %collective-permute-start.19 = (f32[64,128]{1,0:T(8,128)S(1)}, f32[64,128]{1,0:T(8,128)S(1)}, u32[]{:S(2)}, u32[]{:S(2)}) collective-permute-start(f32[64,128]{1,0:T(8,128)S(1)} %multiply_add_fusion.4), channel_id=1, source_target_pairs={{0,4},{4,0},{8,12},{12,8},{16,20},{20,16},{24,28},{28,24},{1,5},{5... | collective-permute-start | bytes 98312 | tf_op jit(solution)/shard_map/ppermute | solution.py:208
  73.1 2.5 %collective-permute-start.20 = (f32[64,128]{1,0:T(8,128)S(1)}, f32[64,128]{1,0:T(8,128)S(1)}, u32[]{:S(2)}, u32[]{:S(2)}) collective-permute-start(f32[64,128]{1,0:T(8,128)S(1)} %multiply_add_fusion.4), channel_id=1, source_target_pairs={{0,20},{4,16},{8,28},{12,24},{16,4},{20,0},{24,12},{28,8},{1,21},{... | collective-permute-start | bytes 98312 | tf_op jit(solution)/shard_map/ppermute | solution.py:208
  76.9 1.9 %collective-permute-done.20 = f32[64,128]{1,0:T(8,128)S(1)} collective-permute-done((f32[64,128]{1,0:T(8,128)S(1)}, f32[64,128]{1,0:T(8,128)S(1)}, u32[]{:S(2)}, u32[]{:S(2)}) %collective-permute-start.20) | collective-permute-done | bytes 32800 | tf_op jit(solution)/shard_map/ppermute | solution.py:208
  78.8 1.6 %collective-permute-done.18 = f32[64,128]{1,0:T(8,128)S(1)} collective-permute-done((f32[64,128]{1,0:T(8,128)S(1)}, f32[64,128]{1,0:T(8,128)S(1)}, u32[]{:S(2)}, u32[]{:S(2)}) %collective-permute-start.18) | collective-permute-done | bytes 32800 | tf_op jit(solution)/shard_map/ppermute | solution.py:208
  (51 shorter events, 9.0 us)
Async XLA Ops:
  0.6 9.6 %copy-start = (f32[16384]{0:T(1024)S(1)}, f32[16384]{0:T(1024)}, u32[]{:S(2)}) copy-start(f32[16384]{0:T(1024)} %param.11) | copy-start | bytes 196612
  0.6 24.5 %copy-start.2 = (bf16[2048,64]{0,1:T(8,128)(2,1)S(1)}, bf16[2048,64]{0,1:T(8,128)(2,1)}, u32[]{:S(2)}) copy-start(bf16[2048,64]{0,1:T(8,128)(2,1)} %param.8) | copy-start | bytes 786436
  0.7 24.5 %copy-start.1 = (bf16[8192,64]{0,1:T(8,128)(2,1)S(1)}, bf16[8192,64]{0,1:T(8,128)(2,1)}, u32[]{:S(2)}) copy-start(bf16[8192,64]{0,1:T(8,128)(2,1)} %param.7) | copy-start | bytes 3145732
  0.7 23.0 %collective-permute-start.4 = (bf16[64,2048]{1,0:T(8,128)(2,1)}, bf16[64,2048]{1,0:T(8,128)(2,1)S(1)}, u32[]{:S(2)}, u32[]{:S(2)}) collective-permute-start(bf16[64,2048]{1,0:T(8,128)(2,1)} %bitcast.35), channel_id=1, source_target_pairs={{16,0},{20,4},{0,8},{4,12},{24,16},{28,20},{8,24},{12,28},{17,1},{... | collective-permute-start | bytes 786440 | tf_op jit(solution)/shard_map/ppermute | solution.py:258
  3.7 13.1 %collective-permute-start.1 = (bf16[64,2048]{1,0:T(8,128)(2,1)}, bf16[64,2048]{1,0:T(8,128)(2,1)S(1)}, u32[]{:S(2)}, u32[]{:S(2)}) collective-permute-start(bf16[64,2048]{1,0:T(8,128)(2,1)} %bitcast.36), channel_id=1, source_target_pairs={{0,16},{4,20},{8,0},{12,4},{16,24},{20,28},{24,8},{28,12},{1,17},{... | collective-permute-start | bytes 786440 | tf_op jit(solution)/shard_map/ppermute | solution.py:254
  7.1 4.3 %collective-permute-start = (f32[64,132]{1,0:T(8,128)S(1)}, f32[64,132]{1,0:T(8,128)S(1)}, u32[]{:S(2)}, u32[]{:S(2)}) collective-permute-start(f32[64,132]{1,0:T(8,128)S(1)} %pad_maximum_fusion.1), channel_id=1, source_target_pairs={{0,4},{4,0},{8,12},{12,8},{16,20},{20,16},{24,28},{28,24},{1,5},{5... | collective-permute-start | bytes 101384 | tf_op jit(solution)/shard_map/ppermute | solution.py:208
  10.0 12.9 %collective-permute-start.2 = (bf16[64,4096]{1,0:T(8,128)(2,1)S(1)}, bf16[64,4096]{1,0:T(8,128)(2,1)S(1)}, u32[]{:S(2)}, u32[]{:S(2)}) collective-permute-start(bf16[64,4096]{1,0:T(8,128)(2,1)S(1)} %constant_dynamic-slice_fusion.1), channel_id=1, source_target_pairs={{0,4},{4,0},{8,12},{12,8},{16,20},{20,16},{24,28},{28,24},{1,5},{5... | collective-permute-start | bytes 1572872 | tf_op jit(solution)/shard_map/ppermute | solution.py:208
  16.9 8.2 %collective-permute-start.5 = (bf16[64,2048]{1,0:T(8,128)(2,1)S(1)}, bf16[64,2048]{1,0:T(8,128)(2,1)S(1)}, u32[]{:S(2)}, u32[]{:S(2)}) collective-permute-start(bf16[64,2048]{1,0:T(8,128)(2,1)S(1)} %collective-permute-done.1.refs_4_), channel_id=1, source_target_pairs={{0,16},{4,20},{8,0},{12,4},{16,24},{20,28},{24,8},{28,12},{1,17},{... | collective-permute-start | bytes 786440 | tf_op jit(solution)/shard_map/ppermute | solution.py:254
  22.9 2.3 %collective-permute-start.3 = (bf16[64,4096]{1,0:T(8,128)(2,1)S(1)}, bf16[64,4096]{1,0:T(8,128)(2,1)S(1)}, u32[]{:S(2)}, u32[]{:S(2)}) collective-permute-start(bf16[64,4096]{1,0:T(8,128)(2,1)S(1)} %collective-permute-done.2.refs_1_), channel_id=1, source_target_pairs={{0,1},{1,0},{2,3},{3,2},{4,5},{5,4},{6,7},{7,6},{8,9},{9,8},{10,11... | collective-permute-start | bytes 1572872 | tf_op jit(solution)/shard_map/ppermute | solution.py:210
  30.3 17.5 %copy-start.3 = (f32[16384]{0:T(1024)S(1)}, f32[16384]{0:T(1024)}, u32[]{:S(2)}) copy-start(f32[16384]{0:T(1024)} %param.10) | copy-start | bytes 196612
  30.4 1.3 %collective-permute-start.6 = (f32[128,128]{1,0:T(8,128)S(1)}, f32[128,128]{1,0:T(8,128)S(1)}, u32[]{:S(2)}, u32[]{:S(2)}) collective-permute-start(f32[128,128]{1,0:T(8,128)S(1)} %get-tuple-element.22), channel_id=1, source_target_pairs={{0,1},{1,0},{2,3},{3,2},{4,5},{5,4},{6,7},{7,6},{8,9},{9,8},{10,11... | collective-permute-start | bytes 196616 | tf_op jit(solution)/shard_map/ppermute | solution.py:210
  31.7 5.2 %collective-permute-start.9 = (f32[128,128]{1,0:T(8,128)S(1)}, f32[128,128]{1,0:T(8,128)S(1)}, u32[]{:S(2)}, u32[]{:S(2)}) collective-permute-start(f32[128,128]{1,0:T(8,128)S(1)} %multiply_add_fusion.1.refs_0_), channel_id=1, source_target_pairs={{0,6},{1,7},{2,4},{3,5},{4,2},{5,3},{6,0},{7,1},{8,14},{9,15},{10,... | collective-permute-start | bytes 196616 | tf_op jit(solution)/shard_map/ppermute | solution.py:212
  34.4 4.3 %collective-permute-start.8 = (f32[128,128]{1,0:T(8,128)S(1)}, f32[128,128]{1,0:T(8,128)S(1)}, u32[]{:S(2)}, u32[]{:S(2)}) collective-permute-start(f32[128,128]{1,0:T(8,128)S(1)} %multiply_add_fusion.1.refs_0_), channel_id=1, source_target_pairs={{0,4},{4,0},{8,12},{12,8},{16,20},{20,16},{24,28},{28,24},{1,5},{5... | collective-permute-start | bytes 196616 | tf_op jit(solution)/shard_map/ppermute | solution.py:208
  34.8 4.3 %collective-permute-start.7 = (f32[128,128]{1,0:T(8,128)S(1)}, f32[128,128]{1,0:T(8,128)S(1)}, u32[]{:S(2)}, u32[]{:S(2)}) collective-permute-start(f32[128,128]{1,0:T(8,128)S(1)} %multiply_add_fusion.1.refs_0_), channel_id=1, source_target_pairs={{0,2},{1,3},{2,0},{3,1},{4,6},{5,7},{6,4},{7,5},{8,10},{9,11},{10,... | collective-permute-start | bytes 196616 | tf_op jit(solution)/shard_map/ppermute | solution.py:210
  43.4 5.8 %collective-permute-start.12 = (f32[64,128]{1,0:T(8,128)S(1)}, f32[64,128]{1,0:T(8,128)S(1)}, u32[]{:S(2)}, u32[]{:S(2)}) collective-permute-start(f32[64,128]{1,0:T(8,128)S(1)} %target_first.1.refs_0_), channel_id=1, source_target_pairs={{0,24},{4,28},{8,16},{12,20},{16,8},{20,12},{24,0},{28,4},{1,25},{... | collective-permute-start | bytes 98312 | tf_op jit(solution)/shard_map/ppermute | solution.py:208
  46.2 4.8 %collective-permute-start.11 = (f32[64,128]{1,0:T(8,128)S(1)}, f32[64,128]{1,0:T(8,128)S(1)}, u32[]{:S(2)}, u32[]{:S(2)}) collective-permute-start(f32[64,128]{1,0:T(8,128)S(1)} %target_first.1.refs_0_), channel_id=1, source_target_pairs={{0,16},{4,20},{8,24},{12,28},{16,0},{20,4},{24,8},{28,12},{1,17},{... | collective-permute-start | bytes 98312 | tf_op jit(solution)/shard_map/ppermute | solution.py:208
  46.2 4.8 %collective-permute-start.10 = (f32[64,128]{1,0:T(8,128)S(1)}, f32[64,128]{1,0:T(8,128)S(1)}, u32[]{:S(2)}, u32[]{:S(2)}) collective-permute-start(f32[64,128]{1,0:T(8,128)S(1)} %target_first.1.refs_0_), channel_id=1, source_target_pairs={{0,8},{4,12},{8,0},{12,4},{16,24},{20,28},{24,16},{28,20},{1,9},{5... | collective-permute-start | bytes 98312 | tf_op jit(solution)/shard_map/ppermute | solution.py:208
  55.4 1.3 %collective-permute-start.13 = (f32[128,128]{1,0:T(8,128)S(1)}, f32[128,128]{1,0:T(8,128)S(1)}, u32[]{:S(2)}, u32[]{:S(2)}) collective-permute-start(f32[128,128]{1,0:T(8,128)S(1)} %source_second.1), channel_id=1, source_target_pairs={{0,1},{1,0},{2,3},{3,2},{4,5},{5,4},{6,7},{7,6},{8,9},{9,8},{10,11... | collective-permute-start | bytes 196616 | tf_op jit(solution)/shard_map/ppermute | solution.py:210
  56.8 5.3 %collective-permute-start.16 = (f32[128,128]{1,0:T(8,128)S(1)}, f32[128,128]{1,0:T(8,128)S(1)}, u32[]{:S(2)}, u32[]{:S(2)}) collective-permute-start(f32[128,128]{1,0:T(8,128)S(1)} %multiply_add_fusion.refs_0_), channel_id=1, source_target_pairs={{0,6},{1,7},{2,4},{3,5},{4,2},{5,3},{6,0},{7,1},{8,14},{9,15},{10,... | collective-permute-start | bytes 196616 | tf_op jit(solution)/shard_map/ppermute | solution.py:212
  58.6 4.7 %collective-permute-start.15 = (f32[128,128]{1,0:T(8,128)S(1)}, f32[128,128]{1,0:T(8,128)S(1)}, u32[]{:S(2)}, u32[]{:S(2)}) collective-permute-start(f32[128,128]{1,0:T(8,128)S(1)} %multiply_add_fusion.refs_0_), channel_id=1, source_target_pairs={{0,4},{4,0},{8,12},{12,8},{16,20},{20,16},{24,28},{28,24},{1,5},{5... | collective-permute-start | bytes 196616 | tf_op jit(solution)/shard_map/ppermute | solution.py:208
  58.9 4.4 %collective-permute-start.14 = (f32[128,128]{1,0:T(8,128)S(1)}, f32[128,128]{1,0:T(8,128)S(1)}, u32[]{:S(2)}, u32[]{:S(2)}) collective-permute-start(f32[128,128]{1,0:T(8,128)S(1)} %multiply_add_fusion.refs_0_), channel_id=1, source_target_pairs={{0,2},{1,3},{2,0},{3,1},{4,6},{5,7},{6,4},{7,5},{8,10},{9,11},{10,... | collective-permute-start | bytes 196616 | tf_op jit(solution)/shard_map/ppermute | solution.py:210
  67.8 4.0 %collective-permute-start.17 = (f32[64,128]{1,0:T(8,128)S(1)}, f32[64,128]{1,0:T(8,128)S(1)}, u32[]{:S(2)}, u32[]{:S(2)}) collective-permute-start(f32[64,128]{1,0:T(8,128)S(1)} %add_subtract_fusion), channel_id=1, source_target_pairs={{0,8},{4,12},{8,0},{12,4},{16,24},{20,28},{24,16},{28,20},{1,9},{5... | collective-permute-start | bytes 98312 | tf_op jit(solution)/shard_map/ppermute | solution.py:208
  71.8 5.1 %collective-permute-start.19 = (f32[64,128]{1,0:T(8,128)S(1)}, f32[64,128]{1,0:T(8,128)S(1)}, u32[]{:S(2)}, u32[]{:S(2)}) collective-permute-start(f32[64,128]{1,0:T(8,128)S(1)} %multiply_add_fusion.4), channel_id=1, source_target_pairs={{0,4},{4,0},{8,12},{12,8},{16,20},{20,16},{24,28},{28,24},{1,5},{5... | collective-permute-start | bytes 98312 | tf_op jit(solution)/shard_map/ppermute | solution.py:208
  73.1 5.7 %collective-permute-start.20 = (f32[64,128]{1,0:T(8,128)S(1)}, f32[64,128]{1,0:T(8,128)S(1)}, u32[]{:S(2)}, u32[]{:S(2)}) collective-permute-start(f32[64,128]{1,0:T(8,128)S(1)} %multiply_add_fusion.4), channel_id=1, source_target_pairs={{0,20},{4,16},{8,28},{12,24},{16,4},{20,0},{24,12},{28,8},{1,21},{... | collective-permute-start | bytes 98312 | tf_op jit(solution)/shard_map/ppermute | solution.py:208
  75.5 4.8 %collective-permute-start.18 = (f32[64,128]{1,0:T(8,128)S(1)}, f32[64,128]{1,0:T(8,128)S(1)}, u32[]{:S(2)}, u32[]{:S(2)}) collective-permute-start(f32[64,128]{1,0:T(8,128)S(1)} %multiply_add_fusion.4), channel_id=1, source_target_pairs={{0,16},{4,20},{8,24},{12,28},{16,0},{20,4},{24,8},{28,12},{1,17},{... | collective-permute-start | bytes 98312 | tf_op jit(solution)/shard_map/ppermute | solution.py:208

commit v8 on v6

--- a/solution.py
+++ b/solution.py
@@ -304,9 +304,9 @@
     lse, pot = later_pass(by_target, exchange(lse, s_hops, swap_by), s_mass, xb, yb, True, "target_second")
 
     lse = lse - (eps * jnp.log(t_mass) + 0.5 * ysq)
-    for hop in t_hops[:-1]:
+    for hop in t_hops[1:]:
         lse = merge(lse, swap_by(lse, *hop))
-    last = t_hops[-1][0]
+    last = t_hops[0][0]
     own = merge(lse, swap_by(lse, last, 0)).reshape(levels, 1, per, BLOCK)
     other = merge(swap_by(lse, 1, 0), swap_by(lse, last | 1, 0)).reshape(levels, 1, per, BLOCK)
     second_g = -jnp.concatenate([jnp.where(side == 0, own, other), jnp.where(side == 0, other, own)], axis=1)

time: 81.1 us -> 80.4 us (level)
    ppermute x2, starting transfers between devices: 4.45 us -> 3.26 us  [swap(): return lax.ppermute(value, ('row', 'col'), pairs)]
where the time goes in v8:
time: 80.4 us; the launch traced here: 79.8 us
  waiting for transfers between devices  28.1 us (35%)
  starting transfers between devices  24.8 us (31%)
  Pallas kernels  18.4 us (23%)
  other arithmetic  5.8 us (7%)
  local copies, waits for them, and re-layouts  1.99 us (2%)
    ppermute x11, starting transfers between devices, swap(): return lax.ppermute(value, 'row', [(i, i ^ row_bit) for i in range(rows)])  13.3 us
    pallas_call x3, Pallas kernels, later_pass(): pl.pallas_call(functools.partial(later_kernel, len(parts), keep), out_sha...  13.2 us
    ppermute x11, waiting for transfers between devices, swap(): return lax.ppermute(value, 'row', [(i, i ^ row_bit) for i in range(rows)])  13.1 us
    ppermute x2, waiting for transfers between devices, shards(): ahead = lax.ppermute(ahead, 'row', onward)  8.17 us
    pallas_call x1, Pallas kernels, first_pass(): pl.pallas_call(functools.partial(first_kernel, n_src, n_tgt, targets * BL...  5.2 us
    ppermute x2, waiting for transfers between devices, swap(): return lax.ppermute(value, ('row', 'col'), pairs)  3.85 us
    ppermute x2, starting transfers between devices, swap(): return lax.ppermute(value, ('row', 'col'), pairs)  3.26 us
    ppermute x1, starting transfers between devices, shards(): behind = lax.ppermute(behind, 'row', back)  3.08 us
  transfers between devices with their start and end apart: 21, of which 18 were waited for; matrix products, arithmetic and copies ran while one was open for 9% of the time, Pallas kernels for 0%

profile of v8, /device:TPU:0, one launch (start us, length us, event | category | flops | bytes accessed | tf_op | source)
XLA Modules:
  0.0 79.8 jit_solution(16850589028510632728)
XLA Ops:
  0.7 3.1 %collective-permute-start.4 = (bf16[64,2048]{1,0:T(8,128)(2,1)}, bf16[64,2048]{1,0:T(8,128)(2,1)S(1)}, u32[]{:S(2)}, u32[]{:S(2)}) collective-permute-start(bf16[64,2048]{1,0:T(8,128)(2,1)} %bitcast.35), channel_id=1, source_target_pairs={{16,0},{20,4},{0,8},{4,12},{24,16},{28,20},{8,24},{12,28},{17,1},{... | collective-permute-start | bytes 786440 | tf_op jit(solution)/shard_map/ppermute | solution.py:256
  3.7 1.1 %collective-permute-start.1 = (bf16[64,2048]{1,0:T(8,128)(2,1)}, bf16[64,2048]{1,0:T(8,128)(2,1)S(1)}, u32[]{:S(2)}, u32[]{:S(2)}) collective-permute-start(bf16[64,2048]{1,0:T(8,128)(2,1)} %bitcast.36), channel_id=1, source_target_pairs={{0,16},{4,20},{8,0},{12,4},{16,24},{20,28},{24,8},{28,12},{1,17},{... | collective-permute-start | bytes 786440 | tf_op jit(solution)/shard_map/ppermute | solution.py:252
  7.1 1.8 %collective-permute-start = (f32[64,132]{1,0:T(8,128)S(1)}, f32[64,132]{1,0:T(8,128)S(1)}, u32[]{:S(2)}, u32[]{:S(2)}) collective-permute-start(f32[64,132]{1,0:T(8,128)S(1)} %pad_maximum_fusion.1), channel_id=1, source_target_pairs={{0,4},{4,0},{8,12},{12,8},{16,20},{20,16},{24,28},{28,24},{1,5},{5... | collective-permute-start | bytes 101384 | tf_op jit(solution)/shard_map/ppermute | solution.py:208
  8.9 1.1 %constant_dynamic-slice_fusion.1 = bf16[64,4096]{1,0:T(8,128)(2,1)S(1)} fusion(bf16[64,8192]{1,0:T(8,128)(2,1)} %bitcast.31, s32[]{:T(128)S(6)} %select_n.283), kind=kLoop, calls=%fused_computation.119 | loop fusion | bytes 1048580 | tf_op jit(solution)/shard_map/dynamic_slice | solution.py:270
  10.3 1.0 %collective-permute-done = f32[64,132]{1,0:T(8,128)S(1)} collective-permute-done((f32[64,132]{1,0:T(8,128)S(1)}, f32[64,132]{1,0:T(8,128)S(1)}, u32[]{:S(2)}, u32[]{:S(2)}) %collective-permute-start) | collective-permute-done | bytes 33824 | tf_op jit(solution)/shard_map/ppermute | solution.py:208
  11.4 5.5 %collective-permute-done.1.refs_4_ = bf16[64,2048]{1,0:T(8,128)(2,1)S(1)} collective-permute-done((bf16[64,2048]{1,0:T(8,128)(2,1)}, bf16[64,2048]{1,0:T(8,128)(2,1)S(1)}, u32[]{:S(2)}, u32[]{:S(2)}) %collective-permute-start.1) | collective-permute-done | bytes 262176 | tf_op jit(solution)/shard_map/ppermute | solution.py:252
  18.0 1.8 %collective-permute-start.5 = (bf16[64,2048]{1,0:T(8,128)(2,1)S(1)}, bf16[64,2048]{1,0:T(8,128)(2,1)S(1)}, u32[]{:S(2)}, u32[]{:S(2)}) collective-permute-start(bf16[64,2048]{1,0:T(8,128)(2,1)S(1)} %collective-permute-done.1.refs_4_), channel_id=1, source_target_pairs={{0,16},{4,20},{8,0},{12,4},{16,24},{20,28},{24,8},{28,12},{1,17},{... | collective-permute-start | bytes 786440 | tf_op jit(solution)/shard_map/ppermute | solution.py:252
  20.6 2.3 %collective-permute-done.2.refs_1_ = bf16[64,4096]{1,0:T(8,128)(2,1)S(1)} collective-permute-done((bf16[64,4096]{1,0:T(8,128)(2,1)S(1)}, bf16[64,4096]{1,0:T(8,128)(2,1)S(1)}, u32[]{:S(2)}, u32[]{:S(2)}) %collective-permute-start.2) | collective-permute-done | bytes 524320 | tf_op jit(solution)/shard_map/ppermute | solution.py:208
  23.6 2.6 %collective-permute-done.5.refs_6_ = bf16[64,2048]{1,0:T(8,128)(2,1)S(1)} collective-permute-done((bf16[64,2048]{1,0:T(8,128)(2,1)S(1)}, bf16[64,2048]{1,0:T(8,128)(2,1)S(1)}, u32[]{:S(2)}, u32[]{:S(2)}) %collective-permute-start.5) | collective-permute-done | bytes 262176 | tf_op jit(solution)/shard_map/ppermute | solution.py:252
  26.3 5.2 %source_first.1 = (f32[128,128]{1,0:T(8,128)S(1)}, f32[64,128]{1,0:T(8,128)S(1)}, bf16[128,64,128]{2,1,0:T(8,128)(2,1)S(1)}, bf16[64,64,128]{2,1,0:T(8,128)(2,1)S(1)}) custom-call(s32[3]{0:T(128)S(1)} %pad_add_fusion.2.here, s32[529]{0:T(1024)S(1)} %get-tuple-element.17.tiles_in, f32[64,128]{1,0:T(8,128)S(1)} %bitcast.38, bf16[64,8192]{1,0:T(8,128)(2,1)S(1)} %bitcast.32, ...), custom_call_target="tpu_custom_call" | custom-call | tf_op jit(solution)/shard_map/source_first/pallas_call | solution.py:176
  31.6 1.2 %collective-permute-done.6 = f32[128,128]{1,0:T(8,128)S(1)} collective-permute-done((f32[128,128]{1,0:T(8,128)S(1)}, f32[128,128]{1,0:T(8,128)S(1)}, u32[]{:S(2)}, u32[]{:S(2)}) %collective-permute-start.6) | collective-permute-done | bytes 65568 | tf_op jit(solution)/shard_map/ppermute | solution.py:210
  32.9 2.1 %collective-permute-start.9 = (f32[128,128]{1,0:T(8,128)S(1)}, f32[128,128]{1,0:T(8,128)S(1)}, u32[]{:S(2)}, u32[]{:S(2)}) collective-permute-start(f32[128,128]{1,0:T(8,128)S(1)} %multiply_add_fusion.1.refs_0_), channel_id=1, source_target_pairs={{0,6},{1,7},{2,4},{3,5},{4,2},{5,3},{6,0},{7,1},{8,14},{9,15},{10,... | collective-permute-start | bytes 196616 | tf_op jit(solution)/shard_map/ppermute | solution.py:212
  35.5 0.9 %collective-permute-start.7 = (f32[128,128]{1,0:T(8,128)S(1)}, f32[128,128]{1,0:T(8,128)S(1)}, u32[]{:S(2)}, u32[]{:S(2)}) collective-permute-start(f32[128,128]{1,0:T(8,128)S(1)} %multiply_add_fusion.1.refs_0_), channel_id=1, source_target_pairs={{0,2},{1,3},{2,0},{3,1},{4,6},{5,7},{6,4},{7,5},{8,10},{9,11},{10,... | collective-permute-start | bytes 196616 | tf_op jit(solution)/shard_map/ppermute | solution.py:210
  36.4 1.7 %collective-permute-done.9.refs_3_ = f32[128,128]{1,0:T(8,128)S(1)} collective-permute-done((f32[128,128]{1,0:T(8,128)S(1)}, f32[128,128]{1,0:T(8,128)S(1)}, u32[]{:S(2)}, u32[]{:S(2)}) %collective-permute-start.9) | collective-permute-done | bytes 65568 | tf_op jit(solution)/shard_map/ppermute | solution.py:212
  38.2 1.3 %collective-permute-done.8.refs_2_ = f32[128,128]{1,0:T(8,128)S(1)} collective-permute-done((f32[128,128]{1,0:T(8,128)S(1)}, f32[128,128]{1,0:T(8,128)S(1)}, u32[]{:S(2)}, u32[]{:S(2)}) %collective-permute-start.8) | collective-permute-done | bytes 65568 | tf_op jit(solution)/shard_map/ppermute | solution.py:208
  39.8 4.3 %target_first.1.refs_0_ = f32[64,128]{1,0:T(8,128)S(1)} custom-call(s32[529]{0:T(1024)S(1)} %get-tuple-element.16.tiles_in, f32[128,128]{1,0:T(8,128)S(1)} %multiply_add_fusion.1.refs_0_, f32[128,128]{1,0:T(8,128)S(1)} %collective-permute-done.7.refs_1_, f32[128,128]{1,0:T(8,128)S(1)} %collective-permute-done.8.refs_2_, ...), custom_call_target="tpu_custom_call" | custom-call | tf_op jit(solution)/shard_map/target_first/pallas_call | solution.py:195
  44.1 1.9 %collective-permute-start.12 = (f32[64,128]{1,0:T(8,128)S(1)}, f32[64,128]{1,0:T(8,128)S(1)}, u32[]{:S(2)}, u32[]{:S(2)}) collective-permute-start(f32[64,128]{1,0:T(8,128)S(1)} %target_first.1.refs_0_), channel_id=1, source_target_pairs={{0,24},{4,28},{8,16},{12,20},{16,8},{20,12},{24,0},{28,4},{1,25},{... | collective-permute-start | bytes 98312 | tf_op jit(solution)/shard_map/ppermute | solution.py:208
  46.0 1.2 %collective-permute-start.11 = (f32[64,128]{1,0:T(8,128)S(1)}, f32[64,128]{1,0:T(8,128)S(1)}, u32[]{:S(2)}, u32[]{:S(2)}) collective-permute-start(f32[64,128]{1,0:T(8,128)S(1)} %target_first.1.refs_0_), channel_id=1, source_target_pairs={{0,16},{4,20},{8,24},{12,28},{16,0},{20,4},{24,8},{28,12},{1,17},{... | collective-permute-start | bytes 98312 | tf_op jit(solution)/shard_map/ppermute | solution.py:208
  47.2 1.4 %collective-permute-start.10 = (f32[64,128]{1,0:T(8,128)S(1)}, f32[64,128]{1,0:T(8,128)S(1)}, u32[]{:S(2)}, u32[]{:S(2)}) collective-permute-start(f32[64,128]{1,0:T(8,128)S(1)} %target_first.1.refs_0_), channel_id=1, source_target_pairs={{0,8},{4,12},{8,0},{12,4},{16,24},{20,28},{24,16},{28,20},{1,9},{5... | collective-permute-start | bytes 98312 | tf_op jit(solution)/shard_map/ppermute | solution.py:208
  48.6 1.5 %collective-permute-done.12.refs_3_ = f32[64,128]{1,0:T(8,128)S(1)} collective-permute-done((f32[64,128]{1,0:T(8,128)S(1)}, f32[64,128]{1,0:T(8,128)S(1)}, u32[]{:S(2)}, u32[]{:S(2)}) %collective-permute-start.12) | collective-permute-done | bytes 32800 | tf_op jit(solution)/shard_map/ppermute | solution.py:208
  51.2 4.4 %source_second.1 = f32[128,128]{1,0:T(8,128)S(1)} custom-call(s32[529]{0:T(1024)S(1)} %get-tuple-element.17.tiles_in, f32[64,128]{1,0:T(8,128)S(1)} %target_first.1.refs_0_, f32[64,128]{1,0:T(8,128)S(1)} %collective-permute-done.10.refs_1_, f32[64,128]{1,0:T(8,128)S(1)} %collective-permute-done.11.refs_2_, f32[64,128]{1,0:T(8,128)S(1)} %collective-permute-done.12.refs_3_, ...), custom_call_target="tpu_custom_call" | custom-call | tf_op jit(solution)/shard_map/source_second/pallas_call | solution.py:195
  55.6 1.2 %collective-permute-done.13 = f32[128,128]{1,0:T(8,128)S(1)} collective-permute-done((f32[128,128]{1,0:T(8,128)S(1)}, f32[128,128]{1,0:T(8,128)S(1)}, u32[]{:S(2)}, u32[]{:S(2)}) %collective-permute-start.13) | collective-permute-done | bytes 65568 | tf_op jit(solution)/shard_map/ppermute | solution.py:210
  56.9 1.1 %collective-permute-start.16 = (f32[128,128]{1,0:T(8,128)S(1)}, f32[128,128]{1,0:T(8,128)S(1)}, u32[]{:S(2)}, u32[]{:S(2)}) collective-permute-start(f32[128,128]{1,0:T(8,128)S(1)} %multiply_add_fusion.refs_0_), channel_id=1, source_target_pairs={{0,6},{1,7},{2,4},{3,5},{4,2},{5,3},{6,0},{7,1},{8,14},{9,15},{10,... | collective-permute-start | bytes 196616 | tf_op jit(solution)/shard_map/ppermute | solution.py:212
  58.0 1.2 %collective-permute-start.15 = (f32[128,128]{1,0:T(8,128)S(1)}, f32[128,128]{1,0:T(8,128)S(1)}, u32[]{:S(2)}, u32[]{:S(2)}) collective-permute-start(f32[128,128]{1,0:T(8,128)S(1)} %multiply_add_fusion.refs_0_), channel_id=1, source_target_pairs={{0,4},{4,0},{8,12},{12,8},{16,20},{20,16},{24,28},{28,24},{1,5},{5... | collective-permute-start | bytes 196616 | tf_op jit(solution)/shard_map/ppermute | solution.py:208
  59.3 1.2 %collective-permute-start.14 = (f32[128,128]{1,0:T(8,128)S(1)}, f32[128,128]{1,0:T(8,128)S(1)}, u32[]{:S(2)}, u32[]{:S(2)}) collective-permute-start(f32[128,128]{1,0:T(8,128)S(1)} %multiply_add_fusion.refs_0_), channel_id=1, source_target_pairs={{0,2},{1,3},{2,0},{3,1},{4,6},{5,7},{6,4},{7,5},{8,10},{9,11},{10,... | collective-permute-start | bytes 196616 | tf_op jit(solution)/shard_map/ppermute | solution.py:210
  60.5 2.1 %collective-permute-done.16.refs_3_ = f32[128,128]{1,0:T(8,128)S(1)} collective-permute-done((f32[128,128]{1,0:T(8,128)S(1)}, f32[128,128]{1,0:T(8,128)S(1)}, u32[]{:S(2)}, u32[]{:S(2)}) %collective-permute-start.16) | collective-permute-done | bytes 65568 | tf_op jit(solution)/shard_map/ppermute | solution.py:212
  63.5 4.5 %target_second.1 = (f32[64,128]{1,0:T(8,128)S(1)}, f32[128,128]{1,0:T(8,128)S(1)}) custom-call(s32[529]{0:T(1024)S(1)} %get-tuple-element.16.tiles_in, f32[128,128]{1,0:T(8,128)S(1)} %multiply_add_fusion.refs_0_, f32[128,128]{1,0:T(8,128)S(1)} %collective-permute-done.14.refs_1_, f32[128,128]{1,0:T(8,128)S(1)} %collective-permute-done.15.refs_2_, ...), custom_call_target="tpu_custom_call" | custom-call | tf_op jit(solution)/shard_map/target_second/pallas_call | solution.py:195
  68.0 1.5 %collective-permute-start.17 = (f32[64,128]{1,0:T(8,128)S(1)}, f32[64,128]{1,0:T(8,128)S(1)}, u32[]{:S(2)}, u32[]{:S(2)}) collective-permute-start(f32[64,128]{1,0:T(8,128)S(1)} %add_subtract_fusion), channel_id=1, source_target_pairs={{0,16},{4,20},{8,24},{12,28},{16,0},{20,4},{24,8},{28,12},{1,17},{... | collective-permute-start | bytes 98312 | tf_op jit(solution)/shard_map/ppermute | solution.py:208
  69.8 3.5 %collective-permute-done.17 = f32[64,128]{1,0:T(8,128)S(1)} collective-permute-done((f32[64,128]{1,0:T(8,128)S(1)}, f32[64,128]{1,0:T(8,128)S(1)}, u32[]{:S(2)}, u32[]{:S(2)}) %collective-permute-start.17) | collective-permute-done | bytes 32800 | tf_op jit(solution)/shard_map/ppermute | solution.py:208
  73.6 1.5 %collective-permute-start.20 = (f32[64,128]{1,0:T(8,128)S(1)}, f32[64,128]{1,0:T(8,128)S(1)}, u32[]{:S(2)}, u32[]{:S(2)}) collective-permute-start(f32[64,128]{1,0:T(8,128)S(1)} %multiply_add_fusion.4), channel_id=1, source_target_pairs={{0,12},{4,8},{8,4},{12,0},{16,28},{20,24},{24,20},{28,16},{1,13},{... | collective-permute-start | bytes 98312 | tf_op jit(solution)/shard_map/ppermute | solution.py:208
  75.1 1.7 %collective-permute-start.18 = (f32[64,128]{1,0:T(8,128)S(1)}, f32[64,128]{1,0:T(8,128)S(1)}, u32[]{:S(2)}, u32[]{:S(2)}) collective-permute-start(f32[64,128]{1,0:T(8,128)S(1)} %multiply_add_fusion.4), channel_id=1, source_target_pairs={{0,8},{4,12},{8,0},{12,4},{16,24},{20,28},{24,16},{28,20},{1,9},{5... | collective-permute-start | bytes 98312 | tf_op jit(solution)/shard_map/ppermute | solution.py:208
  77.5 0.9 %collective-permute-done.20 = f32[64,128]{1,0:T(8,128)S(1)} collective-permute-done((f32[64,128]{1,0:T(8,128)S(1)}, f32[64,128]{1,0:T(8,128)S(1)}, u32[]{:S(2)}, u32[]{:S(2)}) %collective-permute-start.20) | collective-permute-done | bytes 32800 | tf_op jit(solution)/shard_map/ppermute | solution.py:208
  (51 shorter events, 11.0 us)
Async XLA Ops:
  0.6 9.6 %copy-start = (f32[16384]{0:T(1024)S(1)}, f32[16384]{0:T(1024)}, u32[]{:S(2)}) copy-start(f32[16384]{0:T(1024)} %param.11) | copy-start | bytes 196612
  0.6 25.6 %copy-start.2 = (bf16[2048,64]{0,1:T(8,128)(2,1)S(1)}, bf16[2048,64]{0,1:T(8,128)(2,1)}, u32[]{:S(2)}) copy-start(bf16[2048,64]{0,1:T(8,128)(2,1)} %param.8) | copy-start | bytes 786436
  0.7 25.6 %copy-start.1 = (bf16[8192,64]{0,1:T(8,128)(2,1)S(1)}, bf16[8192,64]{0,1:T(8,128)(2,1)}, u32[]{:S(2)}) copy-start(bf16[8192,64]{0,1:T(8,128)(2,1)} %param.7) | copy-start | bytes 3145732
  0.7 23.0 %collective-permute-start.4 = (bf16[64,2048]{1,0:T(8,128)(2,1)}, bf16[64,2048]{1,0:T(8,128)(2,1)S(1)}, u32[]{:S(2)}, u32[]{:S(2)}) collective-permute-start(bf16[64,2048]{1,0:T(8,128)(2,1)} %bitcast.35), channel_id=1, source_target_pairs={{16,0},{20,4},{0,8},{4,12},{24,16},{28,20},{8,24},{12,28},{17,1},{... | collective-permute-start | bytes 786440 | tf_op jit(solution)/shard_map/ppermute | solution.py:256
  3.7 13.1 %collective-permute-start.1 = (bf16[64,2048]{1,0:T(8,128)(2,1)}, bf16[64,2048]{1,0:T(8,128)(2,1)S(1)}, u32[]{:S(2)}, u32[]{:S(2)}) collective-permute-start(bf16[64,2048]{1,0:T(8,128)(2,1)} %bitcast.36), channel_id=1, source_target_pairs={{0,16},{4,20},{8,0},{12,4},{16,24},{20,28},{24,8},{28,12},{1,17},{... | collective-permute-start | bytes 786440 | tf_op jit(solution)/shard_map/ppermute | solution.py:252
  7.1 4.3 %collective-permute-start = (f32[64,132]{1,0:T(8,128)S(1)}, f32[64,132]{1,0:T(8,128)S(1)}, u32[]{:S(2)}, u32[]{:S(2)}) collective-permute-start(f32[64,132]{1,0:T(8,128)S(1)} %pad_maximum_fusion.1), channel_id=1, source_target_pairs={{0,4},{4,0},{8,12},{12,8},{16,20},{20,16},{24,28},{28,24},{1,5},{5... | collective-permute-start | bytes 101384 | tf_op jit(solution)/shard_map/ppermute | solution.py:208
  10.0 12.9 %collective-permute-start.2 = (bf16[64,4096]{1,0:T(8,128)(2,1)S(1)}, bf16[64,4096]{1,0:T(8,128)(2,1)S(1)}, u32[]{:S(2)}, u32[]{:S(2)}) collective-permute-start(bf16[64,4096]{1,0:T(8,128)(2,1)S(1)} %constant_dynamic-slice_fusion.1), channel_id=1, source_target_pairs={{0,4},{4,0},{8,12},{12,8},{16,20},{20,16},{24,28},{28,24},{1,5},{5... | collective-permute-start | bytes 1572872 | tf_op jit(solution)/shard_map/ppermute | solution.py:208
  18.0 8.3 %collective-permute-start.5 = (bf16[64,2048]{1,0:T(8,128)(2,1)S(1)}, bf16[64,2048]{1,0:T(8,128)(2,1)S(1)}, u32[]{:S(2)}, u32[]{:S(2)}) collective-permute-start(bf16[64,2048]{1,0:T(8,128)(2,1)S(1)} %collective-permute-done.1.refs_4_), channel_id=1, source_target_pairs={{0,16},{4,20},{8,0},{12,4},{16,24},{20,28},{24,8},{28,12},{1,17},{... | collective-permute-start | bytes 786440 | tf_op jit(solution)/shard_map/ppermute | solution.py:252
  22.9 3.4 %collective-permute-start.3 = (bf16[64,4096]{1,0:T(8,128)(2,1)S(1)}, bf16[64,4096]{1,0:T(8,128)(2,1)S(1)}, u32[]{:S(2)}, u32[]{:S(2)}) collective-permute-start(bf16[64,4096]{1,0:T(8,128)(2,1)S(1)} %collective-permute-done.2.refs_1_), channel_id=1, source_target_pairs={{0,1},{1,0},{2,3},{3,2},{4,5},{5,4},{6,7},{7,6},{8,9},{9,8},{10,11... | collective-permute-start | bytes 1572872 | tf_op jit(solution)/shard_map/ppermute | solution.py:210
  31.5 17.1 %copy-start.3 = (f32[16384]{0:T(1024)S(1)}, f32[16384]{0:T(1024)}, u32[]{:S(2)}) copy-start(f32[16384]{0:T(1024)} %param.10) | copy-start | bytes 196612
  31.5 1.3 %collective-permute-start.6 = (f32[128,128]{1,0:T(8,128)S(1)}, f32[128,128]{1,0:T(8,128)S(1)}, u32[]{:S(2)}, u32[]{:S(2)}) collective-permute-start(f32[128,128]{1,0:T(8,128)S(1)} %get-tuple-element.20), channel_id=1, source_target_pairs={{0,1},{1,0},{2,3},{3,2},{4,5},{5,4},{6,7},{7,6},{8,9},{9,8},{10,11... | collective-permute-start | bytes 196616 | tf_op jit(solution)/shard_map/ppermute | solution.py:210
  32.9 5.3 %collective-permute-start.9 = (f32[128,128]{1,0:T(8,128)S(1)}, f32[128,128]{1,0:T(8,128)S(1)}, u32[]{:S(2)}, u32[]{:S(2)}) collective-permute-start(f32[128,128]{1,0:T(8,128)S(1)} %multiply_add_fusion.1.refs_0_), channel_id=1, source_target_pairs={{0,6},{1,7},{2,4},{3,5},{4,2},{5,3},{6,0},{7,1},{8,14},{9,15},{10,... | collective-permute-start | bytes 196616 | tf_op jit(solution)/shard_map/ppermute | solution.py:212
  35.0 4.5 %collective-permute-start.8 = (f32[128,128]{1,0:T(8,128)S(1)}, f32[128,128]{1,0:T(8,128)S(1)}, u32[]{:S(2)}, u32[]{:S(2)}) collective-permute-start(f32[128,128]{1,0:T(8,128)S(1)} %multiply_add_fusion.1.refs_0_), channel_id=1, source_target_pairs={{0,4},{4,0},{8,12},{12,8},{16,20},{20,16},{24,28},{28,24},{1,5},{5... | collective-permute-start | bytes 196616 | tf_op jit(solution)/shard_map/ppermute | solution.py:208
  35.5 4.3 %collective-permute-start.7 = (f32[128,128]{1,0:T(8,128)S(1)}, f32[128,128]{1,0:T(8,128)S(1)}, u32[]{:S(2)}, u32[]{:S(2)}) collective-permute-start(f32[128,128]{1,0:T(8,128)S(1)} %multiply_add_fusion.1.refs_0_), channel_id=1, source_target_pairs={{0,2},{1,3},{2,0},{3,1},{4,6},{5,7},{6,4},{7,5},{8,10},{9,11},{10,... | collective-permute-start | bytes 196616 | tf_op jit(solution)/shard_map/ppermute | solution.py:210
  44.1 5.9 %collective-permute-start.12 = (f32[64,128]{1,0:T(8,128)S(1)}, f32[64,128]{1,0:T(8,128)S(1)}, u32[]{:S(2)}, u32[]{:S(2)}) collective-permute-start(f32[64,128]{1,0:T(8,128)S(1)} %target_first.1.refs_0_), channel_id=1, source_target_pairs={{0,24},{4,28},{8,16},{12,20},{16,8},{20,12},{24,0},{28,4},{1,25},{... | collective-permute-start | bytes 98312 | tf_op jit(solution)/shard_map/ppermute | solution.py:208
  46.0 4.8 %collective-permute-start.11 = (f32[64,128]{1,0:T(8,128)S(1)}, f32[64,128]{1,0:T(8,128)S(1)}, u32[]{:S(2)}, u32[]{:S(2)}) collective-permute-start(f32[64,128]{1,0:T(8,128)S(1)} %target_first.1.refs_0_), channel_id=1, source_target_pairs={{0,16},{4,20},{8,24},{12,28},{16,0},{20,4},{24,8},{28,12},{1,17},{... | collective-permute-start | bytes 98312 | tf_op jit(solution)/shard_map/ppermute | solution.py:208
  47.2 4.0 %collective-permute-start.10 = (f32[64,128]{1,0:T(8,128)S(1)}, f32[64,128]{1,0:T(8,128)S(1)}, u32[]{:S(2)}, u32[]{:S(2)}) collective-permute-start(f32[64,128]{1,0:T(8,128)S(1)} %target_first.1.refs_0_), channel_id=1, source_target_pairs={{0,8},{4,12},{8,0},{12,4},{16,24},{20,28},{24,16},{28,20},{1,9},{5... | collective-permute-start | bytes 98312 | tf_op jit(solution)/shard_map/ppermute | solution.py:208
  55.6 1.3 %collective-permute-start.13 = (f32[128,128]{1,0:T(8,128)S(1)}, f32[128,128]{1,0:T(8,128)S(1)}, u32[]{:S(2)}, u32[]{:S(2)}) collective-permute-start(f32[128,128]{1,0:T(8,128)S(1)} %source_second.1), channel_id=1, source_target_pairs={{0,1},{1,0},{2,3},{3,2},{4,5},{5,4},{6,7},{7,6},{8,9},{9,8},{10,11... | collective-permute-start | bytes 196616 | tf_op jit(solution)/shard_map/ppermute | solution.py:210
  56.9 5.7 %collective-permute-start.16 = (f32[128,128]{1,0:T(8,128)S(1)}, f32[128,128]{1,0:T(8,128)S(1)}, u32[]{:S(2)}, u32[]{:S(2)}) collective-permute-start(f32[128,128]{1,0:T(8,128)S(1)} %multiply_add_fusion.refs_0_), channel_id=1, source_target_pairs={{0,6},{1,7},{2,4},{3,5},{4,2},{5,3},{6,0},{7,1},{8,14},{9,15},{10,... | collective-permute-start | bytes 196616 | tf_op jit(solution)/shard_map/ppermute | solution.py:212
  58.0 5.3 %collective-permute-start.15 = (f32[128,128]{1,0:T(8,128)S(1)}, f32[128,128]{1,0:T(8,128)S(1)}, u32[]{:S(2)}, u32[]{:S(2)}) collective-permute-start(f32[128,128]{1,0:T(8,128)S(1)} %multiply_add_fusion.refs_0_), channel_id=1, source_target_pairs={{0,4},{4,0},{8,12},{12,8},{16,20},{20,16},{24,28},{28,24},{1,5},{5... | collective-permute-start | bytes 196616 | tf_op jit(solution)/shard_map/ppermute | solution.py:208
  59.3 4.3 %collective-permute-start.14 = (f32[128,128]{1,0:T(8,128)S(1)}, f32[128,128]{1,0:T(8,128)S(1)}, u32[]{:S(2)}, u32[]{:S(2)}) collective-permute-start(f32[128,128]{1,0:T(8,128)S(1)} %multiply_add_fusion.refs_0_), channel_id=1, source_target_pairs={{0,2},{1,3},{2,0},{3,1},{4,6},{5,7},{6,4},{7,5},{8,10},{9,11},{10,... | collective-permute-start | bytes 196616 | tf_op jit(solution)/shard_map/ppermute | solution.py:210
  68.0 5.2 %collective-permute-start.17 = (f32[64,128]{1,0:T(8,128)S(1)}, f32[64,128]{1,0:T(8,128)S(1)}, u32[]{:S(2)}, u32[]{:S(2)}) collective-permute-start(f32[64,128]{1,0:T(8,128)S(1)} %add_subtract_fusion), channel_id=1, source_target_pairs={{0,16},{4,20},{8,24},{12,28},{16,0},{20,4},{24,8},{28,12},{1,17},{... | collective-permute-start | bytes 98312 | tf_op jit(solution)/shard_map/ppermute | solution.py:208
  73.3 4.2 %collective-permute-start.19 = (f32[64,128]{1,0:T(8,128)S(1)}, f32[64,128]{1,0:T(8,128)S(1)}, u32[]{:S(2)}, u32[]{:S(2)}) collective-permute-start(f32[64,128]{1,0:T(8,128)S(1)} %multiply_add_fusion.4), channel_id=1, source_target_pairs={{0,4},{4,0},{8,12},{12,8},{16,20},{20,16},{24,28},{28,24},{1,5},{5... | collective-permute-start | bytes 98312 | tf_op jit(solution)/shard_map/ppermute | solution.py:208
  73.6 4.8 %collective-permute-start.20 = (f32[64,128]{1,0:T(8,128)S(1)}, f32[64,128]{1,0:T(8,128)S(1)}, u32[]{:S(2)}, u32[]{:S(2)}) collective-permute-start(f32[64,128]{1,0:T(8,128)S(1)} %multiply_add_fusion.4), channel_id=1, source_target_pairs={{0,12},{4,8},{8,4},{12,0},{16,28},{20,24},{24,20},{28,16},{1,13},{... | collective-permute-start | bytes 98312 | tf_op jit(solution)/shard_map/ppermute | solution.py:208
  75.1 3.9 %collective-permute-start.18 = (f32[64,128]{1,0:T(8,128)S(1)}, f32[64,128]{1,0:T(8,128)S(1)}, u32[]{:S(2)}, u32[]{:S(2)}) collective-permute-start(f32[64,128]{1,0:T(8,128)S(1)} %multiply_add_fusion.4), channel_id=1, source_target_pairs={{0,8},{4,12},{8,0},{12,4},{16,24},{20,28},{24,16},{28,20},{1,9},{5... | collective-permute-start | bytes 98312 | tf_op jit(solution)/shard_map/ppermute | solution.py:208
